TPU v7x, 512 devices: a whole 4x4x16 slice. The times are simulated.
512 devices in a mesh: front: 8 (over x, core), row: 16 (over z), col: 4 (over y).
Axes of the slice: x: 4, y: 4, z: 16, core: 2. Of those that a mesh axis runs over, the one named last changes fastest.
Arguments:
- child_rhs: float32 [8, 4096, 512], P('front', ('row', 'col')), may hold values from -6 to 6
- pivot_inverse: float32 [8, 4096, 4096], P('front', 'col', 'row')
- border_factor: float32 [8, 4096, 4096], P('front', 'row', 'col'), may hold values from -0.09375 to 0.09375
- front_sizes: int32 [8, 2], P('front'), may hold values from 1024 to 4096, as said below
- border_index: int32 [8, 4096], P('front'), may hold values from 0 to 8191, as said below
- root_rhs: float32 [8192, 512], P('row'), may hold values from -6 to 6
- root_inverse: float32 [8192, 8192], P(('front', 'col'), 'row')
Outputs:
- child_solution: float32 [8, 4096, 512], P('front', 'col', 'row')
- root_solution: float32 [8192, 512], P(('front', 'col'), 'row')
Inputs may be any that keep to these rules, and one draw needn't show every extreme that they name: `front_sizes`: row c holds child c's pivot count, from 1024 to 4096, and its border count, from 1024 to 4096; some child has both at 4096 and 4096. `border_index`: for each child, 4096 distinct root rows in no particular order; border row i takes part only if i is below the child's border count.
All inputs are finite; a program needn't handle non-finite values.
Results may differ from a plain program's by a relative error of at most 0.0003.
Values sent between devices are 32-bit elements; how exact they have to be, the bound alone decides.
No kernel may reach another device: no remote copies, remote signals or barrier semaphores. Data moves between devices by JAX's collectives and lax.ppermute only.
A program may use at most 64 MiB of HBM per device.

v0:
```python
import jax
import jax.numpy as jnp
from jax import lax
from jax.sharding import PartitionSpec as P


def product(left, right):
    return jnp.dot(left, right, preferred_element_type=jnp.float32, precision=lax.Precision.HIGHEST)


def pick_block(source, which_block, block_count, groups):
    row_count = source.shape[0]
    block_width = source.shape[1] // (groups * block_count)
    shaped = source.reshape(row_count, groups, block_count, block_width)
    return shaped[:, :, which_block, :].reshape(row_count, groups * block_width)


def local(
    child_rhs, pivot_inverse, border_factor, front_sizes, border_index, root_rhs, root_inverse
):
    groups = lax.axis_size("row")
    col_count = lax.axis_size("col")
    col_id = lax.axis_index("col")
    row_id = lax.axis_index("row")
    pivots = front_sizes[0, 0]
    borders = front_sizes[0, 1]
    local_inv = pivot_inverse[0]
    local_border = border_factor[0]
    index_all = border_index[0]
    pivot_rows = local_inv.shape[0]
    root_rows = root_rhs.shape[0]
    block_count = 1
    pivot_live = col_id * pivot_rows + jnp.arange(pivot_rows, dtype=jnp.int32) < pivots
    rhs_block = pick_block(child_rhs[0], 0, block_count, groups)
    partial_value = product(local_inv, lax.all_gather(rhs_block, "col", axis=0, tiled=True))
    own_part = lax.psum_scatter(partial_value, "row", scatter_dimension=1, tiled=True)
    own_part = jnp.where(pivot_live[:, None], own_part, 0.0)
    solved = lax.all_gather(own_part, "row", axis=1, tiled=True)
    update = lax.psum_scatter(product(local_border, solved), "col", scatter_dimension=0, tiled=True)
    shard_rows = update.shape[0]
    portion = lax.all_gather(update, "row", axis=0, tiled=True)
    amount = portion.shape[0]
    gathered = jnp.arange(amount, dtype=jnp.int32)
    border_pos = (
        gathered // shard_rows * (shard_rows * col_count)
        + col_id * shard_rows
        + gathered % shard_rows
    )
    target = jnp.take(index_all, border_pos) - row_id * root_rows
    usable = border_pos < borders
    select = (
        (target[None, :] == jnp.arange(root_rows, dtype=jnp.int32)[:, None]) & usable[None, :]
    ).astype(jnp.float32)
    landed = product(select, portion)
    assembled = lax.psum(landed, ("front", "col"))
    residual_root = pick_block(root_rhs, 0, block_count, groups) - assembled
    root_partial = product(root_inverse, residual_root)
    root_parts = lax.psum_scatter(root_partial, "row", scatter_dimension=1, tiled=True)
    child_solution = own_part[None]
    return (child_solution, root_parts)


def solution(mesh):
    in_specs = (
        P("front", ("row", "col"), None),
        P("front", "col", "row"),
        P("front", "row", "col"),
        P("front", None),
        P("front", None),
        P("row", None),
        P(("front", "col"), "row"),
    )
    out_specs = (P("front", "col", "row"), P(("front", "col"), "row"))
    return jax.shard_map(local, mesh=mesh, in_specs=in_specs, out_specs=out_specs, check_vma=False)
```

profile of v0, /device:TPU:2, one launch (start us, length us, event | category | flops | bytes accessed | tf_op | source)
XLA Modules:
  0.0 498.6 jit_solution(8312727389216858346)
XLA Ops:
  7.2 0.0 copy-start
  7.2 0.0 reduce-scatter.6.cloned.1.call-start
  7.2 13.6 %all-gather = f32[1,256,512]{2,1,0:T(8,128)S(1)} all-gather(f32[1,64,512]{2,1,0:T(8,128)} %param.7), channel_id=2, replica_groups=mesh['front'=8,'row'=16,'col'=4] {'col'}, dimensions={1}, use_global_device_ids=true | all-gather | bytes 655360 | tf_op jit(solution)/shard_map/all_gather | solution.py:35
  20.9 0.0 copy-done
  20.9 0.0 copy-start.6
  20.9 3.3 fusion.4
  24.2 0.0 copy-start.2
  24.2 0.0 reduce-scatter.6.cloned.1.call-update
  24.2 0.0 all-gather.4.cloned.1.call-start
  24.2 0.0 copy-done.6
  24.2 0.6 fusion.23
  24.8 0.7 add_compare_fusion
  25.5 76.6 %reduce-scatter.6.cloned.1.call-done = f32[1024,32]{0,1:T(8,128)} async-done(((f32[1024,512]{0,1:T(8,128)}), f32[1024,32]{0,1:T(8,128)}) %reduce-scatter.6.cloned.1.call-update) | async-done | bytes 131088 | tf_op jit(solution)/shard_map/reduce_scatter | solution.py:36
  102.1 1.6 broadcast_select_fusion
  103.6 0.0 all-gather.4.cloned.1.call-update
  103.6 0.0 copy-start.1
  103.7 0.0 reduce-scatter.10.cloned.1.call-start
  103.7 72.0 %all-gather.4.cloned.1.call-done = f32[1024,512]{0,1:T(8,128)} async-done(((f32[1024,32]{0,1:T(8,128)}), f32[1024,512]{0,1:T(8,128)}) %all-gather.4.cloned.1.call-update) | async-done | bytes 2097168 | tf_op jit(solution)/shard_map/all_gather | solution.py:38
  175.7 0.0 copy-done.2
  175.7 3.4 convolution_bitcast_fusion.1
  179.1 1.0 copy.10
  180.1 0.0 reduce-scatter.10.cloned.1.call-update
  180.1 0.0 all-gather.6.cloned.1.call-start
  180.2 26.3 %reduce-scatter.10.cloned.1.call-done = f32[64,512]{1,0:T(8,128)} async-done(((f32[256,512]{1,0:T(8,128)}), f32[64,512]{1,0:T(8,128)}) %reduce-scatter.10.cloned.1.call-update) | async-done | bytes 131088 | tf_op jit(solution)/shard_map/reduce_scatter | solution.py:39
  206.5 0.0 all-gather.6.cloned.1.call-update
  206.5 0.0 all-reduce.2.cloned.1.call-start
  206.6 0.0 copy-done.1
  206.6 6.2 %gather_fusion = s32[1024]{0:T(1024)S(1)} fusion(s32[4096]{0:T(1024)S(1)} %bitcast.23, s32[1024]{0:T(1024)S(1)} %broadcast_clamp_fusion), kind=kCustom, calls=%fused_computation | custom fusion | bytes 12288 | tf_op jit(solution)/shard_map/jit(_take)/gather | solution.py:49
  212.8 0.7 broadcast_compare_fusion
  213.5 0.0 copy-start.3
  213.5 0.0 copy-start.5
  213.5 67.8 %all-gather.6.cloned.1.call-done = f32[1024,512]{1,0:T(8,128)} async-done(((f32[64,512]{1,0:T(8,128)}), f32[1024,512]{1,0:T(8,128)}) %all-gather.6.cloned.1.call-update) | async-done | bytes 2097168 | tf_op jit(solution)/shard_map/all_gather | solution.py:41
  281.3 4.6 fusion.1
  286.0 0.0 all-reduce.2.cloned.1.call-update
  286.0 0.0 copy-start.4
  286.0 0.0 reduce-scatter.8.cloned.1.call-start
  286.0 132.0 %all-reduce.2.cloned.1.call-done = f32[512,512]{1,0:T(8,128)} async-done(((f32[512,512]{1,0:T(8,128)}), f32[512,512]{1,0:T(8,128)}) %all-reduce.2.cloned.1.call-update) | async-done | bytes 1048592 | tf_op jit(solution)/shard_map/psum | solution.py:55
  418.1 0.0 copy-done.3
  418.1 0.0 copy-done.5
  418.1 3.9 convolution_bitcast_fusion
  422.0 0.0 reduce-scatter.8.cloned.1.call-update
  422.0 0.0 copy-done.4
  422.0 0.7 fusion.27
  422.7 69.0 %reduce-scatter.8.cloned.1.call-done = f32[256,32]{0,1:T(8,128)} async-done(((f32[256,512]{0,1:T(8,128)}), f32[256,32]{0,1:T(8,128)}) %reduce-scatter.8.cloned.1.call-update) | async-done | bytes 32784 | tf_op jit(solution)/shard_map/reduce_scatter | solution.py:58
  (3 shorter events, 0.0 us)
Async XLA Ops:
  7.2 13.7 %copy-start = (f32[1,1024,256]{2,1,0:T(8,128)S(1)}, f32[1,1024,256]{2,1,0:T(8,128)}, u32[]{:S(2)}) copy-start(f32[1,1024,256]{2,1,0:T(8,128)} %param.8) | copy-start | bytes 3145732
  7.2 94.9 %reduce-scatter.6.cloned.1.call-start = ((), (), s32[]{:S(2)}) async-start(), calls=%async_computation.3 | async-start | bytes 2228224 | tf_op jit(solution)/shard_map/reduce_scatter | solution.py:36
  20.9 3.4 copy-start.6
  24.2 151.5 %copy-start.2 = (f32[1,256,1024]{2,1,0:T(8,128)S(1)}, f32[1,256,1024]{2,1,0:T(8,128)}, u32[]{:S(2)}) copy-start(f32[1,256,1024]{2,1,0:T(8,128)} %param.9) | copy-start | bytes 3145732
  24.2 151.5 %all-gather.4.cloned.1.call-start = ((), (), s32[]{:S(2)}) async-start(), calls=%async_computation.4 | async-start | bytes 2228224 | tf_op jit(solution)/shard_map/all_gather | solution.py:38
  103.6 103.0 %copy-start.1 = (s32[1,4096]{1,0:T(1,128)S(1)}, s32[1,4096]{1,0:T(1,128)}, u32[]{:S(2)}) copy-start(s32[1,4096]{1,0:T(1,128)} %param.11) | copy-start | bytes 49156
  103.7 102.8 %reduce-scatter.10.cloned.1.call-start = ((), (), s32[]{:S(2)}) async-start(), calls=%async_computation.8 | async-start | bytes 655360 | tf_op jit(solution)/shard_map/reduce_scatter | solution.py:39
  180.1 101.2 %all-gather.6.cloned.1.call-start = ((), (), s32[]{:S(2)}) async-start(), calls=%async_computation.5 | async-start | bytes 2228224 | tf_op jit(solution)/shard_map/all_gather | solution.py:41
  206.5 211.6 %all-reduce.2.cloned.1.call-start = ((), (), s32[]{:S(2)}) async-start(), calls=%async_computation.6 | async-start | bytes 2097152 | tf_op jit(solution)/shard_map/psum | solution.py:55
  213.5 204.6 %copy-start.3 = (f32[512,512]{1,0:T(8,128)S(1)}, f32[512,512]{1,0:T(8,128)}, u32[]{:S(2)}) copy-start(f32[512,512]{1,0:T(8,128)} %param.12) | copy-start | bytes 3145732
  213.5 204.6 %copy-start.5 = (f32[256,512]{1,0:T(8,128)S(1)}, f32[256,512]{1,0:T(8,128)}, u32[]{:S(2)}) copy-start(f32[256,512]{1,0:T(8,128)} %param.13) | copy-start | bytes 1572868
  286.0 136.1 %copy-start.4 = (f32[1024,32]{0,1:T(8,128)S(1)}, f32[1024,32]{0,1:T(8,128)}, u32[]{:S(2)}) copy-start(f32[1024,32]{0,1:T(8,128)} %reduce-scatter.6.cloned.1.call-done) | copy-start | bytes 393220
  286.0 205.8 %reduce-scatter.8.cloned.1.call-start = ((), (), s32[]{:S(2)}) async-start(), calls=%async_computation.7 | async-start | bytes 557056 | tf_op jit(solution)/shard_map/reduce_scatter | solution.py:58
Sparse Core Ops, SparseCore 0:
  24.3 77.7 reduce-scatter.5
  104.7 70.9 all-gather.3
  180.3 26.2 reduce-scatter.9
  208.4 72.8 all-gather.5
  286.1 131.9 all-reduce.1
  422.2 69.5 reduce-scatter.7
where the time goes:
time: 499 us
  waiting for transfers between devices  444 us (89%)
  matrix products  15.2 us (3%)
  between operations  14.2 us (3%)
  blocking collectives  13.6 us (3%)
  local copies, waits for them, and re-layouts  7.77 us (2%)
    psum x1, waiting for transfers between devices, local(): assembled = lax.psum(landed, ('front', 'col'))  132 us
    reduce_scatter x1, waiting for transfers between devices, local(): lax.psum_scatter(partial_value, 'row', scatter_dimension=1, tiled=True)  76.6 us
    all_gather x1, waiting for transfers between devices, local(): solved = lax.all_gather(own_part, 'row', axis=1, tiled=True)  72 us
    reduce_scatter x1, waiting for transfers between devices, local(): lax.psum_scatter(root_partial, 'row', scatter_dimension=1, tiled=True)  69 us
    all_gather x1, waiting for transfers between devices, local(): portion = lax.all_gather(update, 'row', axis=0, tiled=True)  67.8 us
    reduce_scatter x1, waiting for transfers between devices, local(): lax.psum_scatter(product(local_border, solved), 'col', scatter_dimension=...  26.3 us
    dot_general x4, matrix products, product(): jnp.dot(left, right, preferred_element_type=jnp.float32, precision=lax.Pr...  15.2 us
    all_gather x1, blocking collectives, local(): lax.all_gather(rhs_block, 'col', axis=0, tiled=True)  13.6 us
  transfers between devices with their start and end apart: 6, of which 6 were waited for; matrix products, arithmetic and copies ran while one was open for 2% of the time, Pallas kernels for 0%

commit v1 on v0

v1 whole, which is shorter than its diff:
```python
import jax
import jax.numpy as jnp
from jax import lax
from jax.sharding import PartitionSpec as P

HIGH = lax.Precision.HIGH


def contract(left, right, left_dims, right_dims):
    return lax.dot_general(
        left,
        right,
        ((left_dims, right_dims), ((), ())),
        precision=HIGH,
        preferred_element_type=jnp.float32,
    )


def exchange(blocks, axes):
    return lax.all_to_all(blocks, axes, split_axis=0, concat_axis=0, tiled=True)


def local(
    child_rhs, pivot_inverse, border_factor, front_sizes, border_index, root_rhs, root_inverse
):
    rows = lax.axis_size("row")
    cols = lax.axis_size("col")
    fronts = lax.axis_size("front")
    layer = fronts * cols
    col_id = lax.axis_index("col")
    row_id = lax.axis_index("row")
    front_id = lax.axis_index("front")
    inverse = pivot_inverse[0]
    border = border_factor[0]
    pivot_rows = inverse.shape[0]
    border_rows = border.shape[0]
    root_rows, sources = root_rhs.shape
    part = sources // layer
    halves = 2
    low_count = rows * halves
    high_count = root_rows // halves

    start = row_id * border_rows
    index = lax.dynamic_slice_in_dim(border_index[0], start, border_rows)
    live = start + jnp.arange(border_rows, dtype=jnp.int32) < front_sizes[0, 1]
    index = lax.all_gather(jnp.where(live, index, -1), "front", axis=0)

    rhs = lax.all_gather(child_rhs[0], "col", axis=0, tiled=True)
    partial = contract(inverse, rhs, (1,), (0,))
    own = lax.psum_scatter(partial, "row", scatter_dimension=1, tiled=True)
    pivot_live = col_id * pivot_rows + jnp.arange(pivot_rows, dtype=jnp.int32) < front_sizes[0, 0]
    own = jnp.where(pivot_live[:, None], own, 0.0)
    solved = lax.all_gather(own, "row", axis=1, tiled=True)

    update = contract(solved, border, (0,), (1,))
    update = exchange(update, ("front", "col"))
    update = update.reshape(fronts, cols, part, border_rows).sum(1)

    low = jnp.where(index < 0, -1, index // high_count)
    high = index % high_count
    at_low = low[None, :, :] == jnp.arange(low_count, dtype=jnp.int32)[:, None, None]
    at_high = high[:, :, None] == jnp.arange(high_count, dtype=jnp.int32)
    spread = jnp.where(at_low[:, None], update.transpose(1, 0, 2)[None], 0.0)
    landed = contract(
        spread.reshape(low_count * part, fronts * border_rows),
        at_high.astype(jnp.float32).reshape(fronts * border_rows, high_count),
        (1,),
        (0,),
    )
    landed = exchange(landed, "row").reshape(rows, halves, part, high_count).sum(0)

    share = front_id * cols + col_id
    rhs_share = lax.dynamic_slice_in_dim(root_rhs, share * part, part, 1)
    rhs_share = rhs_share.reshape(halves, high_count, part).transpose(0, 2, 1)
    residual = rhs_share - landed
    residual = exchange(
        jnp.broadcast_to(residual[None], (layer, halves, part, high_count)), ("front", "col")
    )
    residual = residual.transpose(0, 2, 1, 3).reshape(sources, root_rows)

    root = contract(residual, root_inverse, (1,), (1,))
    root = exchange(root, "row").reshape(rows, sources // rows, root_inverse.shape[0]).sum(0)
    return own[None], root.T


def solution(mesh):
    in_specs = (
        P("front", ("row", "col"), None),
        P("front", "col", "row"),
        P("front", "row", "col"),
        P("front", None),
        P("front", None),
        P("row", None),
        P(("front", "col"), "row"),
    )
    out_specs = (P("front", "col", "row"), P(("front", "col"), "row"))
    return jax.shard_map(local, mesh=mesh, in_specs=in_specs, out_specs=out_specs, check_vma=False)
```

time: 499 us -> 317 us (0.64)
  waiting for transfers between devices: 444 us -> 205 us
  blocking collectives: 13.6 us -> 46.1 us
  starting transfers between devices: 0.24 us -> 22.1 us
    psum x1 -> x0, waiting for transfers between devices: 132 us -> none  [local(): assembled = lax.psum(landed, ('front', 'col'))]
    reduce_scatter x3 -> x1, waiting for transfers between devices: 172 us -> 76.6 us  [local(): own = lax.psum_scatter(partial, 'row', scatter_dimension=1, tiled=True)]
    all_gather x2 -> x1, waiting for transfers between devices: 140 us -> 72 us  [local(): solved = lax.all_gather(own, 'row', axis=1, tiled=True)]
    all_to_all x0 -> x3, waiting for transfers between devices: none -> 56.6 us  [exchange(): return lax.all_to_all(blocks, axes, split_axis=0, concat_axis=0, tiled=True)]
    all_to_all x0 -> x3, starting transfers between devices: none -> 22 us  [exchange(): return lax.all_to_all(blocks, axes, split_axis=0, concat_axis=0, tiled=True)]
    all_to_all x0 -> x1, blocking collectives: none -> 21.9 us  [exchange(): return lax.all_to_all(blocks, axes, split_axis=0, concat_axis=0, tiled=True)]
    all_gather x1 -> x2, blocking collectives: 13.6 us -> 24.3 us  [the longest x1 13.6 us: local(): rhs = lax.all_gather(child_rhs[0], 'col', axis=0, tiled=True)]
    gather x1 -> x0, local copies, waits for them, and re-layouts: 6.15 us -> none  [local(): target = jnp.take(index_all, border_pos) - row_id * root_rows]
  transfers between devices with their start and end apart: 6 -> 5, of which waited for: 6 -> 4; matrix products, arithmetic and copies ran while one was open for 2% -> 1% of each run, Pallas kernels for 0% -> 0%
where the time goes in v1:
time: 317 us; the launch traced here: 316 us
  waiting for transfers between devices  205 us (65%)
  blocking collectives  46.1 us (15%)
  starting transfers between devices  22.1 us (7%)
  between operations  14.2 us (4%)
  matrix products  12.6 us (4%)
  local copies, waits for them, and re-layouts  8.06 us (3%)
  other arithmetic  7.48 us (2%)
    reduce_scatter x1, waiting for transfers between devices, local(): own = lax.psum_scatter(partial, 'row', scatter_dimension=1, tiled=True)  76.6 us
    all_gather x1, waiting for transfers between devices, local(): solved = lax.all_gather(own, 'row', axis=1, tiled=True)  72 us
    all_to_all x3, waiting for transfers between devices, exchange(): return lax.all_to_all(blocks, axes, split_axis=0, concat_axis=0, tiled=True)  56.6 us
    all_to_all x3, starting transfers between devices, exchange(): return lax.all_to_all(blocks, axes, split_axis=0, concat_axis=0, tiled=True)  22 us
    all_to_all x1, blocking collectives, exchange(): return lax.all_to_all(blocks, axes, split_axis=0, concat_axis=0, tiled=True)  21.9 us
    all_gather x1, blocking collectives, local(): rhs = lax.all_gather(child_rhs[0], 'col', axis=0, tiled=True)  13.6 us
    dot_general x4, matrix products, contract(): lax.dot_general(left, right, ((left_dims, right_dims), ((), ())), precisi...  12.6 us
    all_gather x1, blocking collectives, local(): index = lax.all_gather(jnp.where(live, index, -1), 'front', axis=0)  10.6 us
  transfers between devices with their start and end apart: 5, of which 4 were waited for; matrix products, arithmetic and copies ran while one was open for 1% of the time, Pallas kernels for 0%

profile of v1, /device:TPU:2, one launch (start us, length us, event | category | flops | bytes accessed | tf_op | source)
XLA Modules:
  0.0 315.8 jit_solution(7400299095870156874)
XLA Ops:
  7.2 0.0 copy-start
  7.2 0.0 copy-start.3
  7.2 0.0 copy-start.1
  7.2 0.0 reduce-scatter.2.cloned.1.call-start
  7.2 13.6 %all-gather = f32[1,256,512]{2,1,0:T(8,128)S(1)} all-gather(f32[1,64,512]{2,1,0:T(8,128)} %param.7), channel_id=2, replica_groups=mesh['front'=8,'row'=16,'col'=4] {'col'}, dimensions={1}, use_global_device_ids=true | all-gather | bytes 655360 | tf_op jit(solution)/shard_map/all_gather | solution.py:48
  20.9 0.0 copy-done
  20.9 2.4 fusion.5
  23.3 0.0 reduce-scatter.2.cloned.1.call-update
  23.3 0.0 all-gather.4.cloned.1.call-start
  23.4 0.0 copy-done.3
  23.4 0.6 fusion.17
  23.9 0.7 add_compare_fusion
  24.6 76.6 %reduce-scatter.2.cloned.1.call-done = f32[1024,32]{0,1:T(8,128)} async-done(((f32[1024,512]{0,1:T(8,128)}), f32[1024,32]{0,1:T(8,128)}) %reduce-scatter.2.cloned.1.call-update) | async-done | bytes 131088 | tf_op jit(solution)/shard_map/reduce_scatter | solution.py:50
  101.2 1.6 broadcast_select_fusion.1
  102.8 0.0 all-gather.4.cloned.1.call-update
  102.8 72.0 %all-gather.4.cloned.1.call-done = f32[1024,512]{0,1:T(8,128)} async-done(((f32[1024,32]{0,1:T(8,128)}), f32[1024,512]{0,1:T(8,128)}) %all-gather.4.cloned.1.call-update) | async-done | bytes 2097168 | tf_op jit(solution)/shard_map/all_gather | solution.py:53
  174.8 0.0 copy-done.1
  174.8 3.4 %fusion.3 = f32[32,16,256]{2,1,0:T(8,128)} fusion(f32[32,16,1024]{2,1,0:T(8,128)} %bitcast.69, f32[1,256,1024]{2,1,0:T(8,128)S(1)} %copy-done.1), kind=kOutput, calls=%fused_computation.4 | convolution fusion | flops 805306368 | bytes 3670016 | tf_op jit(solution)/shard_map/dot_general | solution.py:10
  178.3 7.4 %all-to-all-start = ((f32[32,16,256]{2,1,0:T(8,128)}), f32[32,16,256]{2,1,0:T(8,128)S(1)}, u32[]{:S(2)}, u32[]{:S(2)}) async-start(f32[32,16,256]{2,1,0:T(8,128)} %fusion.3), calls=%async_computation.1 | async-start | bytes 1048576 | tf_op jit(solution)/shard_map/all_to_all | solution.py:20
  185.7 1.3 fusion.16
  187.0 10.6 %all-gather.1 = s32[8,1,256]{2,1,0:T(1,128)S(1)} all-gather(s32[1,1,256]{2,1,0:T(1,128)S(1)} %fusion.16), channel_id=1, replica_groups=mesh['front'=8,'row'=16,'col'=4] {'front'}, dimensions={0}, use_global_device_ids=true | all-gather | bytes 9216 | tf_op jit(solution)/shard_map/all_gather | solution.py:46
  197.7 0.0 all-to-all-done
  197.8 0.1 copy.12
  197.9 2.4 broadcast_select_fusion
  200.3 4.9 %select_n.47 = f32[16,32,2048]{2,1,0:T(8,128)} reshape(f32[32,16,8,256]{3,2,1,0:T(8,128)} %broadcast_select_fusion) | data formatting | bytes 8388608 | tf_op jit(solution)/shard_map/jit(_where)/select_n | solution.py:63
  205.2 4.3 %fusion.1 = f32[16,32,256]{2,1,0:T(8,128)} fusion(f32[16,32,2048]{2,1,0:T(8,128)} %select_n.47, s32[2048]{0:T(1024)S(1)} %bitcast.73), kind=kOutput, calls=%fused_computation.3 | convolution fusion | flops 1611137024 | bytes 4726784 | tf_op jit(solution)/shard_map/dot_general | solution.py:10
  209.5 8.0 %all-to-all-start.1 = ((f32[16,32,256]{2,1,0:T(8,128)}), f32[16,32,256]{2,1,0:T(8,128)S(1)}, u32[]{:S(2)}, u32[]{:S(2)}) async-start(f32[16,32,256]{2,1,0:T(8,128)} %fusion.1), calls=%async_computation.2 | async-start | bytes 1048576 | tf_op jit(solution)/shard_map/all_to_all | solution.py:20
  217.6 1.1 constant_dynamic-slice_fusion
  218.7 0.1 copy.14
  218.8 28.1 %all-to-all-done.1 = f32[16,32,256]{2,1,0:T(8,128)S(1)} async-done(((f32[16,32,256]{2,1,0:T(8,128)}), f32[16,32,256]{2,1,0:T(8,128)S(1)}, u32[]{:S(2)}, u32[]{:S(2)}) %all-to-all-start.1) | async-done | bytes 524320 | tf_op jit(solution)/shard_map/all_to_all | solution.py:20
  247.0 0.0 copy-start.2
  247.0 0.5 broadcast_in_dim.64
  247.4 21.9 %all_to_all.23 = f32[32,2,16,256]{3,1,2,0:T(2,128)S(1)} all-to-all(f32[32,2,16,256]{3,1,2,0:T(2,128)S(1)} %broadcast_in_dim.64), channel_id=1, replica_groups=mesh['front'=8,'row'=16,'col'=4] {'front','col'}, dimensions={0} | all-to-all | bytes 2097152 | tf_op jit(solution)/shard_map/all_to_all | solution.py:20
  269.3 0.8 dot_general.23
  270.1 2.5 fusion.8
  272.6 6.5 %all-to-all-start.3 = ((f32[16,32,256]{2,1,0:T(8,128)}), f32[16,32,256]{2,1,0:T(8,128)S(1)}, u32[]{:S(2)}, u32[]{:S(2)}) async-start(f32[16,32,256]{2,1,0:T(8,128)} %fusion.8), calls=%async_computation.4 | async-start | bytes 1048576 | tf_op jit(solution)/shard_map/all_to_all | solution.py:20
  279.2 0.0 copy-done.2
  279.2 0.7 fusion.21
  279.8 28.4 %all-to-all-done.3 = f32[16,32,256]{2,1,0:T(8,128)S(1)} async-done(((f32[16,32,256]{2,1,0:T(8,128)}), f32[16,32,256]{2,1,0:T(8,128)S(1)}, u32[]{:S(2)}, u32[]{:S(2)}) %all-to-all-start.3) | async-done | bytes 524320 | tf_op jit(solution)/shard_map/all_to_all | solution.py:20
  308.3 0.6 reduce_sum.32
  (6 shorter events, 0.2 us)
Async XLA Ops:
  7.2 13.7 %copy-start = (f32[1,1024,256]{2,1,0:T(8,128)S(1)}, f32[1,1024,256]{2,1,0:T(8,128)}, u32[]{:S(2)}) copy-start(f32[1,1024,256]{2,1,0:T(8,128)} %param.8) | copy-start | bytes 3145732
  7.2 16.2 %copy-start.3 = (s32[1,2]{1,0:T(1,128)S(1)}, s32[1,2]{1,0:T(1,128)}, u32[]{:S(2)}) copy-start(s32[1,2]{1,0:T(1,128)} %param.10) | copy-start | bytes 28
  7.2 167.7 %copy-start.1 = (f32[1,256,1024]{2,1,0:T(8,128)S(1)}, f32[1,256,1024]{2,1,0:T(8,128)}, u32[]{:S(2)}) copy-start(f32[1,256,1024]{2,1,0:T(8,128)} %param.9) | copy-start | bytes 3145732
  7.2 94.0 %reduce-scatter.2.cloned.1.call-start = ((), (), s32[]{:S(2)}) async-start(), calls=%async_computation.5 | async-start | bytes 2228224 | tf_op jit(solution)/shard_map/reduce_scatter | solution.py:50
  23.3 151.5 %all-gather.4.cloned.1.call-start = ((), (), s32[]{:S(2)}) async-start(), calls=%async_computation.6 | async-start | bytes 2228224 | tf_op jit(solution)/shard_map/all_gather | solution.py:53
  178.3 19.5 %all-to-all-start = ((f32[32,16,256]{2,1,0:T(8,128)}), f32[32,16,256]{2,1,0:T(8,128)S(1)}, u32[]{:S(2)}, u32[]{:S(2)}) async-start(f32[32,16,256]{2,1,0:T(8,128)} %fusion.3), calls=%async_computation.1 | async-start | bytes 1048576 | tf_op jit(solution)/shard_map/all_to_all | solution.py:20
  209.5 37.4 %all-to-all-start.1 = ((f32[16,32,256]{2,1,0:T(8,128)}), f32[16,32,256]{2,1,0:T(8,128)S(1)}, u32[]{:S(2)}, u32[]{:S(2)}) async-start(f32[16,32,256]{2,1,0:T(8,128)} %fusion.1), calls=%async_computation.2 | async-start | bytes 1048576 | tf_op jit(solution)/shard_map/all_to_all | solution.py:20
  247.0 32.2 %copy-start.2 = (f32[1024,32]{0,1:T(8,128)S(1)}, f32[1024,32]{0,1:T(8,128)}, u32[]{:S(2)}) copy-start(f32[1024,32]{0,1:T(8,128)} %reduce-scatter.2.cloned.1.call-done) | copy-start | bytes 393220
  272.6 35.7 %all-to-all-start.3 = ((f32[16,32,256]{2,1,0:T(8,128)}), f32[16,32,256]{2,1,0:T(8,128)S(1)}, u32[]{:S(2)}, u32[]{:S(2)}) async-start(f32[16,32,256]{2,1,0:T(8,128)} %fusion.8), calls=%async_computation.4 | async-start | bytes 1048576 | tf_op jit(solution)/shard_map/all_to_all | solution.py:20
Sparse Core Ops, SparseCore 0:
  23.4 77.7 reduce-scatter.1
  103.9 70.9 all-gather.3

commit v2 on v1

--- a/solution.py
+++ b/solution.py
@@ -43,16 +43,67 @@
     start = row_id * border_rows
     index = lax.dynamic_slice_in_dim(border_index[0], start, border_rows)
     live = start + jnp.arange(border_rows, dtype=jnp.int32) < front_sizes[0, 1]
-    index = lax.all_gather(jnp.where(live, index, -1), "front", axis=0)
+    index = jnp.where(live, index, -1)
 
-    rhs = lax.all_gather(child_rhs[0], "col", axis=0, tiled=True)
-    partial = contract(inverse, rhs, (1,), (0,))
-    own = lax.psum_scatter(partial, "row", scatter_dimension=1, tiled=True)
+    near = 4
+    far = rows // near
+    block = sources // rows
+    step = 1 - 2 * lax.rem(front_id, 2)
+
+    def shift(value, distance, mirrored=True):
+        pairs = []
+        for front in range(fronts):
+            by = -distance if mirrored and front % 2 else distance
+            pairs += [(front * rows + z, front * rows + (z + by) % rows) for z in range(rows)]
+        return lax.ppermute(value, ("front", "row"), pairs)
+
+    def group_at(offset):
+        return lax.rem(row_id + offset + near, near)
+
+    rhs = child_rhs[0].reshape(-1, far, near, block).transpose(2, 0, 1, 3)
+    rhs = rhs.reshape(near, -1, far * block)
+    rhs = jnp.stack(
+        [
+            lax.dynamic_index_in_dim(rhs, group_at(offset), 0, keepdims=False)
+            for offset in (2, step, -step, 0)
+        ]
+    )
+    rhs = lax.all_gather(rhs, "col", axis=1, tiled=True)
+
+    def pivot_product(which):
+        return contract(rhs[which], inverse, (0,), (1,))
+
+    from_two = shift(pivot_product(0), -1)
+    below, index = lax.optimization_barrier((pivot_product(1), index))
+    from_below = shift(below, 1)
+    index = lax.all_gather(index, "front", axis=0)
+    from_two, index = lax.optimization_barrier((from_two, index))
+    from_above = shift(pivot_product(2) + from_two, -1)
+    near_sum = pivot_product(3) + from_below + from_above
+    near_sum = near_sum.reshape(far, block, pivot_rows)
+    far_id = lax.div(row_id, near)
+
+    def far_block(offset):
+        return lax.dynamic_index_in_dim(near_sum, lax.rem(far_id + offset, far), 0, keepdims=False)
+
+    own = far_block(0)
+    for offset in range(1, far):
+        own = own + shift(far_block(offset), offset * near, False)
     pivot_live = col_id * pivot_rows + jnp.arange(pivot_rows, dtype=jnp.int32) < front_sizes[0, 0]
-    own = jnp.where(pivot_live[:, None], own, 0.0)
-    solved = lax.all_gather(own, "row", axis=1, tiled=True)
+    own = jnp.where(pivot_live[None, :], own, 0.0)
 
-    update = contract(solved, border, (0,), (1,))
+    apart = [[g + near * i for i in range(far)] for g in range(near)]
+    solved = lax.all_gather(own, "row", axis_index_groups=apart, axis=0, tiled=True)
+    solved_above = shift(solved, -1)
+    solved_below = shift(solved, 1)
+    solved_two = shift(solved_above, -1)
+    update = jnp.zeros((near, far * block, border_rows), jnp.float32)
+    for value, offset in (
+        (solved, 0), (solved_above, step), (solved_below, -step), (solved_two, 2)
+    ):
+        piece = contract(value, border, (1,), (1,))
+        update = lax.dynamic_update_slice_in_dim(update, piece[None], group_at(offset), 0)
+    update = update.reshape(sources, border_rows)
     update = exchange(update, ("front", "col"))
     update = update.reshape(fronts, cols, part, border_rows).sum(1)
 
@@ -70,17 +121,23 @@
     landed = exchange(landed, "row").reshape(rows, halves, part, high_count).sum(0)
 
     share = front_id * cols + col_id
-    rhs_share = lax.dynamic_slice_in_dim(root_rhs, share * part, part, 1)
+    per_block = block // part
+    in_block = lax.rem(share, per_block)
+    far_share = lax.rem(lax.div(share, per_block), far)
+    near_share = lax.div(share, per_block * far)
+    first = (far_share * near + near_share) * block + in_block * part
+    rhs_share = lax.dynamic_slice_in_dim(root_rhs, first, part, 1)
     rhs_share = rhs_share.reshape(halves, high_count, part).transpose(0, 2, 1)
     residual = rhs_share - landed
     residual = exchange(
         jnp.broadcast_to(residual[None], (layer, halves, part, high_count)), ("front", "col")
     )
-    residual = residual.transpose(0, 2, 1, 3).reshape(sources, root_rows)
+    residual = residual.reshape(near, far, per_block, halves, part, high_count)
+    residual = residual.transpose(1, 0, 2, 4, 3, 5).reshape(sources, root_rows)
 
     root = contract(residual, root_inverse, (1,), (1,))
     root = exchange(root, "row").reshape(rows, sources // rows, root_inverse.shape[0]).sum(0)
-    return own[None], root.T
+    return own.T[None], root.T
 
 
 def solution(mesh):

time: 317 us -> 273 us (0.86)
  waiting for transfers between devices: 205 us -> 69.1 us
  blocking collectives: 46.1 us -> 104 us
  starting transfers between devices: 22.1 us -> 65.1 us
  between operations: 14.2 us -> 1.1 us
  local copies, waits for them, and re-layouts: 8.06 us -> 11.8 us
  matrix products: 12.6 us -> 15.8 us
    reduce_scatter x1 -> x0, waiting for transfers between devices: 76.6 us -> none  [local(): own = lax.psum_scatter(partial, 'row', scatter_dimension=1, tiled=True)]
    all_gather x1 -> x0, waiting for transfers between devices: 72 us -> none  [local(): solved = lax.all_gather(own, 'row', axis=1, tiled=True)]
    ppermute x0 -> x9, starting transfers between devices: none -> 49.9 us  [shift(): return lax.ppermute(value, ('front', 'row'), pairs)]
    all_to_all x1 -> x2, blocking collectives: 21.9 us -> 55.6 us  [exchange(): return lax.all_to_all(blocks, axes, split_axis=0, concat_axis=0, tiled=True)]
    ppermute x0 -> x9, waiting for transfers between devices: none -> 30.8 us  [shift(): return lax.ppermute(value, ('front', 'row'), pairs)]
    all_gather x2 -> x3, blocking collectives: 24.3 us -> 48.6 us  [the longest x1 26.6 us: local(): lax.all_gather(own, 'row', axis_index_groups=apart, axis=0, tiled=True)]
    all_to_all x3 -> x2, waiting for transfers between devices: 56.6 us -> 38.3 us  [exchange(): return lax.all_to_all(blocks, axes, split_axis=0, concat_axis=0, tiled=True)]
    all_to_all x3 -> x2, starting transfers between devices: 22 us -> 15.1 us  [exchange(): return lax.all_to_all(blocks, axes, split_axis=0, concat_axis=0, tiled=True)]
  transfers between devices with their start and end apart: 5 -> 11, of which waited for: 4 -> 8; matrix products, arithmetic and copies ran while one was open for 1% -> 4% of each run, Pallas kernels for 0% -> 0%
where the time goes in v2:
time: 273 us; the launch traced here: 272 us
  blocking collectives  104 us (38%)
  waiting for transfers between devices  69.1 us (25%)
  starting transfers between devices  65.1 us (24%)
  matrix products  15.8 us (6%)
  local copies, waits for them, and re-layouts  11.8 us (4%)
  other arithmetic  4.66 us (2%)
    all_to_all x2, blocking collectives, exchange(): return lax.all_to_all(blocks, axes, split_axis=0, concat_axis=0, tiled=True)  55.6 us
    ppermute x9, starting transfers between devices, shift(): return lax.ppermute(value, ('front', 'row'), pairs)  49.9 us
    all_to_all x2, waiting for transfers between devices, exchange(): return lax.all_to_all(blocks, axes, split_axis=0, concat_axis=0, tiled=True)  38.3 us
    ppermute x9, waiting for transfers between devices, shift(): return lax.ppermute(value, ('front', 'row'), pairs)  30.8 us
    all_gather x1, blocking collectives, local(): lax.all_gather(own, 'row', axis_index_groups=apart, axis=0, tiled=True)  26.6 us
    dot_general x10, matrix products, contract(): lax.dot_general(left, right, ((left_dims, right_dims), ((), ())), precisi...  15.8 us
    all_to_all x2, starting transfers between devices, exchange(): return lax.all_to_all(blocks, axes, split_axis=0, concat_axis=0, tiled=True)  15.1 us
    all_gather x1, blocking collectives, local(): rhs = lax.all_gather(rhs, 'col', axis=1, tiled=True)  13.3 us
  transfers between devices with their start and end apart: 11, of which 8 were waited for; matrix products, arithmetic and copies ran while one was open for 4% of the time, Pallas kernels for 0%

profile of v2, /device:TPU:2, one launch (start us, length us, event | category | flops | bytes accessed | tf_op | source)
XLA Modules:
  0.0 271.7 jit_solution(1847714504849137342)
XLA Ops:
  0.7 1.1 copy.28
  1.9 0.1 copy.30
  2.0 13.3 %all_gather.12 = f32[4,256,128]{2,0,1:T(4,128)S(1)} all-gather(f32[4,64,128]{2,0,1:T(4,128)S(1)} %copy.30), channel_id=1, replica_groups=mesh['front'=8,'row'=16,'col'=4] {'col'}, dimensions={1}, use_global_device_ids=true | all-gather | bytes 655360 | tf_op jit(solution)/shard_map/all_gather | solution.py:71
  15.4 0.4 fusion.29
  15.7 0.7 fusion.12
  16.4 11.3 %collective-permute-start.1 = (f32[128,1024]{1,0:T(8,128)S(1)}, f32[128,1024]{1,0:T(8,128)S(1)}, u32[]{:S(2)}, u32[]{:S(2)}) collective-permute-start(f32[128,1024]{1,0:T(8,128)S(1)} %fusion.12), channel_id=1, source_target_pairs={{0,60},{4,0},{8,4},{12,8},{16,12},{20,16},{24,20},{28,24},{32,28},... | collective-permute-start | bytes 1572872 | tf_op jit(solution)/shard_map/ppermute | solution.py:58
  27.8 0.6 fusion.30
  28.4 0.7 constant_dynamic-slice_fusion.1
  29.1 0.6 compare_select_fusion
  29.7 1.5 fusion.16
  31.2 1.9 collective-permute-start
  33.1 8.7 %all-gather.1 = s32[8,1,256]{2,1,0:T(1,128)S(1)} all-gather(s32[1,1,256]{2,1,0:T(1,128)S(1)} %bitcast.116), channel_id=2, replica_groups=mesh['front'=8,'row'=16,'col'=4] {'front'}, dimensions={0}, use_global_device_ids=true | all-gather | bytes 9216 | tf_op jit(solution)/shard_map/all_gather | solution.py:79
  41.8 0.7 fusion.14
  42.6 5.1 %collective-permute-start.2 = (f32[128,1024]{1,0:T(8,128)S(1)}, f32[128,1024]{1,0:T(8,128)S(1)}, u32[]{:S(2)}, u32[]{:S(2)}) collective-permute-start(f32[128,1024]{1,0:T(8,128)S(1)} %add.139), channel_id=1, source_target_pairs={{0,60},{4,0},{8,4},{12,8},{16,12},{20,16},{24,20},{28,24},{32,28},... | collective-permute-start | bytes 1572872 | tf_op jit(solution)/shard_map/ppermute | solution.py:58
  47.8 6.6 %collective-permute-done.2 = f32[128,1024]{1,0:T(8,128)S(1)} collective-permute-done((f32[128,1024]{1,0:T(8,128)S(1)}, f32[128,1024]{1,0:T(8,128)S(1)}, u32[]{:S(2)}, u32[]{:S(2)}) %collective-permute-start.2) | collective-permute-done | bytes 524320 | tf_op jit(solution)/shard_map/ppermute | solution.py:58
  54.4 1.7 fusion.3
  56.2 1.9 collective-permute-start.3
  58.1 10.9 %collective-permute-start.4 = (f32[32,1024]{1,0:T(8,128)S(1)}, f32[32,1024]{1,0:T(8,128)S(1)}, u32[]{:S(2)}, u32[]{:S(2)}) collective-permute-start(f32[32,1024]{1,0:T(8,128)S(1)} %get-tuple-element.12), channel_id=1, source_target_pairs={{0,32},{4,36},{8,40},{12,44},{16,48},{20,52},{24,56},{28,60},{32,0... | collective-permute-start | bytes 393224 | tf_op jit(solution)/shard_map/ppermute | solution.py:58
  69.1 4.5 %collective-permute-start.5 = (f32[32,1024]{1,0:T(8,128)S(1)}, f32[32,1024]{1,0:T(8,128)S(1)}, u32[]{:S(2)}, u32[]{:S(2)}) collective-permute-start(f32[32,1024]{1,0:T(8,128)S(1)} %get-tuple-element.11), channel_id=1, source_target_pairs={{0,48},{4,52},{8,56},{12,60},{16,0},{20,4},{24,8},{28,12},{32,16},... | collective-permute-start | bytes 393224 | tf_op jit(solution)/shard_map/ppermute | solution.py:58
  73.6 0.7 add_compare_fusion
  74.3 6.0 %collective-permute-done.3 = f32[32,1024]{1,0:T(8,128)S(1)} collective-permute-done((f32[32,1024]{1,0:T(8,128)S(1)}, f32[32,1024]{1,0:T(8,128)S(1)}, u32[]{:S(2)}, u32[]{:S(2)}) %collective-permute-start.3) | collective-permute-done | bytes 131104 | tf_op jit(solution)/shard_map/ppermute | solution.py:58
  80.3 7.0 %collective-permute-done.4 = f32[32,1024]{1,0:T(8,128)S(1)} collective-permute-done((f32[32,1024]{1,0:T(8,128)S(1)}, f32[32,1024]{1,0:T(8,128)S(1)}, u32[]{:S(2)}, u32[]{:S(2)}) %collective-permute-start.4) | collective-permute-done | bytes 131104 | tf_op jit(solution)/shard_map/ppermute | solution.py:58
  87.2 1.6 collective-permute-done.5
  88.9 26.6 %all_gather.15 = f32[128,1024]{1,0:T(8,128)S(1)} all-gather(f32[32,1024]{1,0:T(8,128)S(1)} %fusion.24), channel_id=1, replica_groups={{0,16,32,48},{4,20,36,52},{8,24,40,56},{12,28,44,60},{1,17,33,49},{5,21..., dimensions={0}, use_global_device_ids=true | all-gather | bytes 655360 | tf_op jit(solution)/shard_map/all_gather | solution.py:96
  115.5 4.8 %collective-permute-start.6 = (f32[128,1024]{1,0:T(8,128)S(1)}, f32[128,1024]{1,0:T(8,128)S(1)}, u32[]{:S(2)}, u32[]{:S(2)}) collective-permute-start(f32[128,1024]{1,0:T(8,128)S(1)} %all_gather.15), channel_id=1, source_target_pairs={{0,60},{4,0},{8,4},{12,8},{16,12},{20,16},{24,20},{28,24},{32,28},... | collective-permute-start | bytes 1572872 | tf_op jit(solution)/shard_map/ppermute | solution.py:58
  120.3 1.9 collective-permute-start.7
  122.2 0.8 broadcast_in_dim.77
  123.1 1.3 fusion.7
  124.4 5.5 %collective-permute-done.6 = f32[128,1024]{1,0:T(8,128)S(1)} collective-permute-done((f32[128,1024]{1,0:T(8,128)S(1)}, f32[128,1024]{1,0:T(8,128)S(1)}, u32[]{:S(2)}, u32[]{:S(2)}) %collective-permute-start.6) | collective-permute-done | bytes 524320 | tf_op jit(solution)/shard_map/ppermute | solution.py:58
  129.9 7.5 %collective-permute-start.8 = (f32[128,1024]{1,0:T(8,128)S(1)}, f32[128,1024]{1,0:T(8,128)S(1)}, u32[]{:S(2)}, u32[]{:S(2)}) collective-permute-start(f32[128,1024]{1,0:T(8,128)S(1)} %collective-permute-done.6), channel_id=1, source_target_pairs={{0,60},{4,0},{8,4},{12,8},{16,12},{20,16},{24,20},{28,24},{32,28},... | collective-permute-start | bytes 1572872 | tf_op jit(solution)/shard_map/ppermute | solution.py:58
  137.4 1.3 fusion.6
  138.7 1.3 fusion.5
  140.1 4.1 %collective-permute-done.8 = f32[128,1024]{1,0:T(8,128)S(1)} collective-permute-done((f32[128,1024]{1,0:T(8,128)S(1)}, f32[128,1024]{1,0:T(8,128)S(1)}, u32[]{:S(2)}, u32[]{:S(2)}) %collective-permute-start.8) | collective-permute-done | bytes 524320 | tf_op jit(solution)/shard_map/ppermute | solution.py:58
  144.1 1.3 fusion.4
  145.4 7.3 %all-to-all-start = ((f32[32,16,256]{2,1,0:T(8,128)}), f32[32,16,256]{2,1,0:T(8,128)S(1)}, u32[]{:S(2)}, u32[]{:S(2)}) async-start(f32[32,16,256]{2,1,0:T(8,128)} %bitcast.26), calls=%async_computation | async-start | bytes 1048576 | tf_op jit(solution)/shard_map/all_to_all | solution.py:20
  152.8 10.3 %all-to-all-done = f32[32,16,256]{2,1,0:T(8,128)S(1)} async-done(((f32[32,16,256]{2,1,0:T(8,128)}), f32[32,16,256]{2,1,0:T(8,128)S(1)}, u32[]{:S(2)}, u32[]{:S(2)}) %all-to-all-start) | async-done | bytes 524320 | tf_op jit(solution)/shard_map/all_to_all | solution.py:20
  163.2 2.5 broadcast_select_fusion
  165.7 4.9 %select_n.84 = f32[16,32,2048]{2,1,0:T(8,128)} reshape(f32[32,16,8,256]{3,2,1,0:T(8,128)} %broadcast_select_fusion) | data formatting | bytes 8388608 | tf_op jit(solution)/shard_map/jit(_where)/select_n | solution.py:114
  170.5 4.3 %fusion.1 = f32[16,32,256]{2,1,0:T(8,128)} fusion(f32[16,32,2048]{2,1,0:T(8,128)} %select_n.84, s32[2048]{0:T(1024)S(1)} %bitcast.113), kind=kOutput, calls=%fused_computation.3 | convolution fusion | flops 1611137024 | bytes 4726784 | tf_op jit(solution)/shard_map/dot_general | solution.py:10
  174.9 7.9 %all-to-all-start.1 = ((f32[16,32,256]{2,1,0:T(8,128)}), f32[16,32,256]{2,1,0:T(8,128)S(1)}, u32[]{:S(2)}, u32[]{:S(2)}) async-start(f32[16,32,256]{2,1,0:T(8,128)} %fusion.1), calls=%async_computation.1 | async-start | bytes 1048576 | tf_op jit(solution)/shard_map/all_to_all | solution.py:20
  182.8 1.1 constant_dynamic-slice_fusion
  183.9 28.0 %all-to-all-done.1 = f32[16,32,256]{2,1,0:T(8,128)S(1)} async-done(((f32[16,32,256]{2,1,0:T(8,128)}), f32[16,32,256]{2,1,0:T(8,128)S(1)}, u32[]{:S(2)}, u32[]{:S(2)}) %all-to-all-start.1) | async-done | bytes 524320 | tf_op jit(solution)/shard_map/all_to_all | solution.py:20
  212.2 20.4 %all_to_all.26 = f32[32,2,16,256]{3,2,1,0:T(8,128)S(1)} all-to-all(f32[32,2,16,256]{3,2,1,0:T(8,128)S(1)} %broadcast_in_dim.84), channel_id=1, replica_groups=mesh['front'=8,'row'=16,'col'=4] {'front','col'}, dimensions={0} | all-to-all | bytes 2097152 | tf_op jit(solution)/shard_map/all_to_all | solution.py:20
  232.5 0.8 copy.34
  233.3 0.8 dot_general.41
  234.2 1.7 fusion.20
  235.9 35.2 %all_to_all.27 = f32[16,32,256]{2,1,0:T(8,128)S(1)} all-to-all(f32[16,32,256]{2,1,0:T(8,128)S(1)} %fusion.20), channel_id=1, replica_groups=mesh['front'=8,'row'=16,'col'=4] {'row'}, dimensions={0} | all-to-all | bytes 1048576 | tf_op jit(solution)/shard_map/all_to_all | solution.py:20
  271.1 0.6 reduce_sum.32
  (27 shorter events, 0.7 us)
Async XLA Ops:
  0.6 15.1 %copy-start = (f32[1,1024,256]{2,1,0:T(8,128)S(1)}, f32[1,1024,256]{2,1,0:T(8,128)}, u32[]{:S(2)}) copy-start(f32[1,1024,256]{2,1,0:T(8,128)} %param.8) | copy-start | bytes 3145732
  0.6 27.1 %copy-start.3 = (s32[1,2]{1,0:T(1,128)S(1)}, s32[1,2]{1,0:T(1,128)}, u32[]{:S(2)}) copy-start(s32[1,2]{1,0:T(1,128)} %param.10) | copy-start | bytes 28
  16.4 26.1 %collective-permute-start.1 = (f32[128,1024]{1,0:T(8,128)S(1)}, f32[128,1024]{1,0:T(8,128)S(1)}, u32[]{:S(2)}, u32[]{:S(2)}) collective-permute-start(f32[128,1024]{1,0:T(8,128)S(1)} %fusion.12), channel_id=1, source_target_pairs={{0,60},{4,0},{8,4},{12,8},{16,12},{20,16},{24,20},{28,24},{32,28},... | collective-permute-start | bytes 1572872 | tf_op jit(solution)/shard_map/ppermute | solution.py:58
  31.2 16.6 %collective-permute-start = (f32[128,1024]{1,0:T(8,128)}, f32[128,1024]{1,0:T(8,128)}, u32[]{:S(2)}, u32[]{:S(2)}) collective-permute-start(f32[128,1024]{1,0:T(8,128)} %fusion.16), channel_id=1, source_target_pairs={{0,4},{4,8},{8,12},{12,16},{16,20},{20,24},{24,28},{28,32},{32,36}... | collective-permute-start | bytes 1572872 | tf_op jit(solution)/shard_map/ppermute | solution.py:58
  41.8 81.3 %copy-start.1 = (f32[1,256,1024]{2,1,0:T(8,128)S(1)}, f32[1,256,1024]{2,1,0:T(8,128)}, u32[]{:S(2)}) copy-start(f32[1,256,1024]{2,1,0:T(8,128)} %param.9) | copy-start | bytes 3145732
  42.6 11.8 %collective-permute-start.2 = (f32[128,1024]{1,0:T(8,128)S(1)}, f32[128,1024]{1,0:T(8,128)S(1)}, u32[]{:S(2)}, u32[]{:S(2)}) collective-permute-start(f32[128,1024]{1,0:T(8,128)S(1)} %add.139), channel_id=1, source_target_pairs={{0,60},{4,0},{8,4},{12,8},{16,12},{20,16},{24,20},{28,24},{32,28},... | collective-permute-start | bytes 1572872 | tf_op jit(solution)/shard_map/ppermute | solution.py:58
  56.2 24.0 %collective-permute-start.3 = (f32[32,1024]{1,0:T(8,128)S(1)}, f32[32,1024]{1,0:T(8,128)S(1)}, u32[]{:S(2)}, u32[]{:S(2)}) collective-permute-start(f32[32,1024]{1,0:T(8,128)S(1)} %get-tuple-element.10), channel_id=1, source_target_pairs={{0,16},{4,20},{8,24},{12,28},{16,32},{20,36},{24,40},{28,44},{32,4... | collective-permute-start | bytes 393224 | tf_op jit(solution)/shard_map/ppermute | solution.py:58
  58.1 29.1 %collective-permute-start.4 = (f32[32,1024]{1,0:T(8,128)S(1)}, f32[32,1024]{1,0:T(8,128)S(1)}, u32[]{:S(2)}, u32[]{:S(2)}) collective-permute-start(f32[32,1024]{1,0:T(8,128)S(1)} %get-tuple-element.12), channel_id=1, source_target_pairs={{0,32},{4,36},{8,40},{12,44},{16,48},{20,52},{24,56},{28,60},{32,0... | collective-permute-start | bytes 393224 | tf_op jit(solution)/shard_map/ppermute | solution.py:58
  69.1 19.8 %collective-permute-start.5 = (f32[32,1024]{1,0:T(8,128)S(1)}, f32[32,1024]{1,0:T(8,128)S(1)}, u32[]{:S(2)}, u32[]{:S(2)}) collective-permute-start(f32[32,1024]{1,0:T(8,128)S(1)} %get-tuple-element.11), channel_id=1, source_target_pairs={{0,48},{4,52},{8,56},{12,60},{16,0},{20,4},{24,8},{28,12},{32,16},... | collective-permute-start | bytes 393224 | tf_op jit(solution)/shard_map/ppermute | solution.py:58
  88.9 56.6 %copy-start.2 = (f32[32,1024]{1,0:T(8,128)}, f32[32,1024]{1,0:T(8,128)S(1)}, u32[]{:S(2)}) copy-start(f32[32,1024]{1,0:T(8,128)S(1)} %fusion.24) | copy-start | bytes 393220
  115.5 14.4 %collective-permute-start.6 = (f32[128,1024]{1,0:T(8,128)S(1)}, f32[128,1024]{1,0:T(8,128)S(1)}, u32[]{:S(2)}, u32[]{:S(2)}) collective-permute-start(f32[128,1024]{1,0:T(8,128)S(1)} %all_gather.15), channel_id=1, source_target_pairs={{0,60},{4,0},{8,4},{12,8},{16,12},{20,16},{24,20},{28,24},{32,28},... | collective-permute-start | bytes 1572872 | tf_op jit(solution)/shard_map/ppermute | solution.py:58
  120.3 18.5 %collective-permute-start.7 = (f32[128,1024]{1,0:T(8,128)S(1)}, f32[128,1024]{1,0:T(8,128)S(1)}, u32[]{:S(2)}, u32[]{:S(2)}) collective-permute-start(f32[128,1024]{1,0:T(8,128)S(1)} %all_gather.15), channel_id=1, source_target_pairs={{0,4},{4,8},{8,12},{12,16},{16,20},{20,24},{24,28},{28,32},{32,36}... | collective-permute-start | bytes 1572872 | tf_op jit(solution)/shard_map/ppermute | solution.py:58
  129.9 14.2 %collective-permute-start.8 = (f32[128,1024]{1,0:T(8,128)S(1)}, f32[128,1024]{1,0:T(8,128)S(1)}, u32[]{:S(2)}, u32[]{:S(2)}) collective-permute-start(f32[128,1024]{1,0:T(8,128)S(1)} %collective-permute-done.6), channel_id=1, source_target_pairs={{0,60},{4,0},{8,4},{12,8},{16,12},{20,16},{24,20},{28,24},{32,28},... | collective-permute-start | bytes 1572872 | tf_op jit(solution)/shard_map/ppermute | solution.py:58
  145.4 17.6 %all-to-all-start = ((f32[32,16,256]{2,1,0:T(8,128)}), f32[32,16,256]{2,1,0:T(8,128)S(1)}, u32[]{:S(2)}, u32[]{:S(2)}) async-start(f32[32,16,256]{2,1,0:T(8,128)} %bitcast.26), calls=%async_computation | async-start | bytes 1048576 | tf_op jit(solution)/shard_map/all_to_all | solution.py:20
  174.9 37.1 %all-to-all-start.1 = ((f32[16,32,256]{2,1,0:T(8,128)}), f32[16,32,256]{2,1,0:T(8,128)S(1)}, u32[]{:S(2)}, u32[]{:S(2)}) async-start(f32[16,32,256]{2,1,0:T(8,128)} %fusion.1), calls=%async_computation.1 | async-start | bytes 1048576 | tf_op jit(solution)/shard_map/all_to_all | solution.py:20

commit v3 on v2

--- a/solution.py
+++ b/solution.py
@@ -1,6 +1,10 @@
+import functools
+
 import jax
 import jax.numpy as jnp
 from jax import lax
+from jax.experimental import pallas as pl
+from jax.experimental.pallas import tpu as pltpu
 from jax.sharding import PartitionSpec as P
 
 HIGH = lax.Precision.HIGH
@@ -18,6 +22,55 @@
 
 def exchange(blocks, axes):
     return lax.all_to_all(blocks, axes, split_axis=0, concat_axis=0, tiled=True)
+
+
+def land_kernel(fronts, cols, update_ref, place_ref, high_ref, out_ref):
+    part, border_rows = update_ref.shape[1:]
+    places = out_ref.shape[0] // part
+    high_count = out_ref.shape[1]
+    place_iota = lax.broadcasted_iota(jnp.int32, (places, 1, border_rows), 0)
+    high_iota = lax.broadcasted_iota(jnp.int32, (high_count, border_rows), 0)
+    fronts_a_step = 2
+    for base in range(0, fronts, fronts_a_step):
+        left, right = [], []
+        for front in range(base, base + fronts_a_step):
+            value = update_ref[front * cols]
+            for col in range(1, cols):
+                value = value + update_ref[front * cols + col]
+            coarse = value.astype(jnp.bfloat16).astype(jnp.float32)
+            at_high = jnp.where(high_iota == high_ref[front], 1.0, 0.0).astype(jnp.bfloat16)
+            at_place = place_iota == place_ref[front][None]
+            for piece in (coarse, value - coarse):
+                spread = jnp.where(at_place, piece[None], 0.0)
+                left.append(spread.reshape(places * part, border_rows).astype(jnp.bfloat16))
+                right.append(at_high)
+        landed = lax.dot_general(
+            jnp.concatenate(left, 1),
+            jnp.concatenate(right, 1),
+            (((1,), (1,)), ((), ())),
+            preferred_element_type=jnp.float32,
+        )
+        if base == 0:
+            out_ref[...] = landed
+        else:
+            out_ref[...] += landed
+
+
+def land(update, place, high, fronts, cols, places, high_count):
+    part, border_rows = update.shape[1:]
+    out = jax.ShapeDtypeStruct((places * part, high_count), jnp.float32)
+    return pl.pallas_call(
+        functools.partial(land_kernel, fronts, cols),
+        out_shape=out,
+        in_specs=[pl.BlockSpec(memory_space=pltpu.VMEM)] * 3,
+        out_specs=pl.BlockSpec(memory_space=pltpu.VMEM),
+        compiler_params=pltpu.CompilerParams(vmem_limit_bytes=32 * 1024 * 1024),
+        cost_estimate=pl.CostEstimate(
+            flops=4 * places * part * high_count * fronts * border_rows,
+            bytes_accessed=4 * (update.size + places * part * high_count),
+            transcendentals=0,
+        ),
+    )(update, place[:, None], high[:, None])
 
 
 def local(
@@ -57,6 +110,21 @@
             pairs += [(front * rows + z, front * rows + (z + by) % rows) for z in range(rows)]
         return lax.ppermute(value, ("front", "row"), pairs)
 
+    def row_sum(blocks):
+        parity = lax.rem(row_id, 2)
+        pairs = []
+        for front in range(fronts):
+            by = front % 2
+            pairs += [
+                (front * rows + z, front * rows + (((z + by) ^ 1) - by) % rows) for z in range(rows)
+            ]
+        theirs = lax.dynamic_index_in_dim(blocks, 1 - parity, 0, keepdims=False)
+        mine = lax.dynamic_index_in_dim(blocks, parity, 0, keepdims=False)
+        mine = mine + lax.ppermute(theirs, ("front", "row"), pairs)
+        same = [list(range(first, rows, 2)) for first in (0, 1)]
+        mine = lax.all_to_all(mine, "row", 0, 0, axis_index_groups=same, tiled=True)
+        return mine.sum(0)
+
     def group_at(offset):
         return lax.rem(row_id + offset + near, near)
 
@@ -104,21 +172,15 @@
         piece = contract(value, border, (1,), (1,))
         update = lax.dynamic_update_slice_in_dim(update, piece[None], group_at(offset), 0)
     update = update.reshape(sources, border_rows)
-    update = exchange(update, ("front", "col"))
-    update = update.reshape(fronts, cols, part, border_rows).sum(1)
-
-    low = jnp.where(index < 0, -1, index // high_count)
-    high = index % high_count
-    at_low = low[None, :, :] == jnp.arange(low_count, dtype=jnp.int32)[:, None, None]
-    at_high = high[:, :, None] == jnp.arange(high_count, dtype=jnp.int32)
-    spread = jnp.where(at_low[:, None], update.transpose(1, 0, 2)[None], 0.0)
-    landed = contract(
-        spread.reshape(low_count * part, fronts * border_rows),
-        at_high.astype(jnp.float32).reshape(fronts * border_rows, high_count),
-        (1,),
-        (0,),
-    )
-    landed = exchange(landed, "row").reshape(rows, halves, part, high_count).sum(0)
+    update = exchange(update.reshape(layer, part, border_rows), ("front", "col"))
+
+    low = jnp.where(index < 0, -1, lax.div(index, high_count))
+    owner = lax.div(low, halves)
+    place = lax.rem(owner, 2) * (low_count // 2) + lax.div(owner, 2) * halves + lax.rem(low, halves)
+    place = jnp.where(index < 0, -1, place)
+    high = lax.rem(index, high_count)
+    landed = land(update, place, high, fronts, cols, low_count, high_count)
+    landed = row_sum(landed.reshape(2, rows // 2, halves, part, high_count))
 
     share = front_id * cols + col_id
     per_block = block // part
@@ -132,11 +194,11 @@
     residual = exchange(
         jnp.broadcast_to(residual[None], (layer, halves, part, high_count)), ("front", "col")
     )
-    residual = residual.reshape(near, far, per_block, halves, part, high_count)
-    residual = residual.transpose(1, 0, 2, 4, 3, 5).reshape(sources, root_rows)
+    residual = residual.reshape(near // 2, 2, far, per_block, halves, part, high_count)
+    residual = residual.transpose(1, 2, 0, 3, 5, 4, 6).reshape(sources, root_rows)
 
     root = contract(residual, root_inverse, (1,), (1,))
-    root = exchange(root, "row").reshape(rows, sources // rows, root_inverse.shape[0]).sum(0)
+    root = row_sum(root.reshape(2, rows // 2, block, root_inverse.shape[0]))
     return own.T[None], root.T
 
 

time: 273 us -> 259 us (0.949)
  blocking collectives: 104 us -> 92.2 us
  starting transfers between devices: 65.1 us -> 71.8 us
  matrix products: 15.8 us -> 9.7 us
  local copies, waits for them, and re-layouts: 11.8 us -> 7.51 us
    all_to_all x2 -> x1, blocking collectives: 55.6 us -> 20.3 us  [exchange(): return lax.all_to_all(blocks, axes, split_axis=0, concat_axis=0, tiled=True)]
    all_to_all x2 -> x1, waiting for transfers between devices: 38.3 us -> 10.3 us  [exchange(): return lax.all_to_all(blocks, axes, split_axis=0, concat_axis=0, tiled=True)]
    all_to_all x0 -> x1, blocking collectives: none -> 24 us  [row_sum(): mine = lax.all_to_all(mine, 'row', 0, 0, axis_index_groups=same, tiled=True)]
    all_to_all x0 -> x1, waiting for transfers between devices: none -> 20.2 us  [row_sum(): mine = lax.all_to_all(mine, 'row', 0, 0, axis_index_groups=same, tiled=True)]
    ppermute x0 -> x2, waiting for transfers between devices: none -> 11 us  [row_sum(): mine = mine + lax.ppermute(theirs, ('front', 'row'), pairs)]
    all_to_all x2 -> x1, starting transfers between devices: 15.1 us -> 7.23 us  [exchange(): return lax.all_to_all(blocks, axes, split_axis=0, concat_axis=0, tiled=True)]
    all_to_all x0 -> x1, starting transfers between devices: none -> 7.53 us  [row_sum(): mine = lax.all_to_all(mine, 'row', 0, 0, axis_index_groups=same, tiled=True)]
    dot_general x10 -> x9, matrix products: 15.8 us -> 9.7 us  [contract(): lax.dot_general(left, right, ((left_dims, right_dims), ((), ())), precisi...]
  transfers between devices with their start and end apart: 11 -> 13, of which waited for: 8 -> 10; matrix products, arithmetic and copies ran while one was open for 4% -> 4% of each run, Pallas kernels for 0% -> 0%
where the time goes in v3:
time: 259 us; the launch traced here: 258 us
  blocking collectives  92.2 us (36%)
  starting transfers between devices  71.8 us (28%)
  waiting for transfers between devices  71.3 us (28%)
  matrix products  9.7 us (4%)
  local copies, waits for them, and re-layouts  7.51 us (3%)
  other arithmetic  2.89 us (1%)
    ppermute x9, starting transfers between devices, shift(): return lax.ppermute(value, ('front', 'row'), pairs)  51.5 us
    ppermute x9, waiting for transfers between devices, shift(): return lax.ppermute(value, ('front', 'row'), pairs)  29.8 us
    all_gather x1, blocking collectives, local(): lax.all_gather(own, 'row', axis_index_groups=apart, axis=0, tiled=True)  26 us
    all_to_all x1, blocking collectives, row_sum(): mine = lax.all_to_all(mine, 'row', 0, 0, axis_index_groups=same, tiled=True)  24 us
    all_to_all x1, blocking collectives, exchange(): return lax.all_to_all(blocks, axes, split_axis=0, concat_axis=0, tiled=True)  20.3 us
    all_to_all x1, waiting for transfers between devices, row_sum(): mine = lax.all_to_all(mine, 'row', 0, 0, axis_index_groups=same, tiled=True)  20.2 us
    all_gather x1, blocking collectives, local(): rhs = lax.all_gather(rhs, 'col', axis=1, tiled=True)  13.3 us
    ppermute x2, waiting for transfers between devices, row_sum(): mine = mine + lax.ppermute(theirs, ('front', 'row'), pairs)  11 us
  transfers between devices with their start and end apart: 13, of which 10 were waited for; matrix products, arithmetic and copies ran while one was open for 4% of the time, Pallas kernels for 0%

profile of v3, /device:TPU:2, one launch (start us, length us, event | category | flops | bytes accessed | tf_op | source)
XLA Modules:
  0.0 257.9 jit_solution(46741195485622037)
XLA Ops:
  0.7 1.1 copy.16
  2.0 13.3 %all_gather.12 = f32[4,256,128]{2,0,1:T(4,128)S(1)} all-gather(f32[4,64,128]{2,0,1:T(4,128)S(1)} %copy.18), channel_id=1, replica_groups=mesh['front'=8,'row'=16,'col'=4] {'col'}, dimensions={1}, use_global_device_ids=true | all-gather | bytes 655360 | tf_op jit(solution)/shard_map/all_gather | solution.py:139
  15.7 0.7 fusion.9
  16.4 11.3 %collective-permute-start.1 = (f32[128,1024]{1,0:T(8,128)S(1)}, f32[128,1024]{1,0:T(8,128)S(1)}, u32[]{:S(2)}, u32[]{:S(2)}) collective-permute-start(f32[128,1024]{1,0:T(8,128)S(1)} %fusion.9), channel_id=1, source_target_pairs={{0,60},{4,0},{8,4},{12,8},{16,12},{20,16},{24,20},{28,24},{32,28},... | collective-permute-start | bytes 1572872 | tf_op jit(solution)/shard_map/ppermute | solution.py:111
  27.8 0.6 copy-done.3
  29.0 0.7 constant_dynamic-slice_fusion.1
  29.7 0.6 compare_select_fusion
  30.3 0.7 fusion.13
  31.1 1.9 collective-permute-start
  33.0 8.7 %all-gather.1 = s32[8,1,256]{2,1,0:T(1,128)S(1)} all-gather(s32[1,1,256]{2,1,0:T(1,128)S(1)} %bitcast.115), channel_id=2, replica_groups=mesh['front'=8,'row'=16,'col'=4] {'front'}, dimensions={0}, use_global_device_ids=true | all-gather | bytes 9216 | tf_op jit(solution)/shard_map/all_gather | solution.py:147
  41.7 0.7 fusion.11
  42.5 5.1 %collective-permute-start.2 = (f32[128,1024]{1,0:T(8,128)S(1)}, f32[128,1024]{1,0:T(8,128)S(1)}, u32[]{:S(2)}, u32[]{:S(2)}) collective-permute-start(f32[128,1024]{1,0:T(8,128)S(1)} %add.155), channel_id=1, source_target_pairs={{0,60},{4,0},{8,4},{12,8},{16,12},{20,16},{24,20},{28,24},{32,28},... | collective-permute-start | bytes 1572872 | tf_op jit(solution)/shard_map/ppermute | solution.py:111
  47.7 6.6 %collective-permute-done.2 = f32[128,1024]{1,0:T(8,128)S(1)} collective-permute-done((f32[128,1024]{1,0:T(8,128)S(1)}, f32[128,1024]{1,0:T(8,128)S(1)}, u32[]{:S(2)}, u32[]{:S(2)}) %collective-permute-start.2) | collective-permute-done | bytes 524320 | tf_op jit(solution)/shard_map/ppermute | solution.py:111
  54.3 0.7 fusion
  55.0 2.1 collective-permute-start.3
  57.1 10.9 %collective-permute-start.4 = (f32[32,1024]{1,0:T(8,128)S(1)}, f32[32,1024]{1,0:T(8,128)S(1)}, u32[]{:S(2)}, u32[]{:S(2)}) collective-permute-start(f32[32,1024]{1,0:T(8,128)S(1)} %get-tuple-element.12), channel_id=1, source_target_pairs={{0,32},{4,36},{8,40},{12,44},{16,48},{20,52},{24,56},{28,60},{32,0... | collective-permute-start | bytes 393224 | tf_op jit(solution)/shard_map/ppermute | solution.py:111
  68.0 4.5 %collective-permute-start.5 = (f32[32,1024]{1,0:T(8,128)S(1)}, f32[32,1024]{1,0:T(8,128)S(1)}, u32[]{:S(2)}, u32[]{:S(2)}) collective-permute-start(f32[32,1024]{1,0:T(8,128)S(1)} %get-tuple-element.11), channel_id=1, source_target_pairs={{0,48},{4,52},{8,56},{12,60},{16,0},{20,4},{24,8},{28,12},{32,16},... | collective-permute-start | bytes 393224 | tf_op jit(solution)/shard_map/ppermute | solution.py:111
  72.6 0.7 add_compare_fusion
  73.2 6.0 %collective-permute-done.3 = f32[32,1024]{1,0:T(8,128)S(1)} collective-permute-done((f32[32,1024]{1,0:T(8,128)S(1)}, f32[32,1024]{1,0:T(8,128)S(1)}, u32[]{:S(2)}, u32[]{:S(2)}) %collective-permute-start.3) | collective-permute-done | bytes 131104 | tf_op jit(solution)/shard_map/ppermute | solution.py:111
  79.2 7.0 %collective-permute-done.4 = f32[32,1024]{1,0:T(8,128)S(1)} collective-permute-done((f32[32,1024]{1,0:T(8,128)S(1)}, f32[32,1024]{1,0:T(8,128)S(1)}, u32[]{:S(2)}, u32[]{:S(2)}) %collective-permute-start.4) | collective-permute-done | bytes 131104 | tf_op jit(solution)/shard_map/ppermute | solution.py:111
  86.2 1.6 collective-permute-done.5
  87.8 26.0 %all_gather.15 = f32[128,1024]{1,0:T(8,128)S(1)} all-gather(f32[32,1024]{1,0:T(8,128)S(1)} %fusion.20), channel_id=1, replica_groups={{0,16,32,48},{4,20,36,52},{8,24,40,56},{12,28,44,60},{1,17,33,49},{5,21..., dimensions={0}, use_global_device_ids=true | all-gather | bytes 655360 | tf_op jit(solution)/shard_map/all_gather | solution.py:164
  113.8 5.2 %collective-permute-start.6 = (f32[128,1024]{1,0:T(8,128)S(1)}, f32[128,1024]{1,0:T(8,128)S(1)}, u32[]{:S(2)}, u32[]{:S(2)}) collective-permute-start(f32[128,1024]{1,0:T(8,128)S(1)} %all_gather.15), channel_id=1, source_target_pairs={{0,60},{4,0},{8,4},{12,8},{16,12},{20,16},{24,20},{28,24},{32,28},... | collective-permute-start | bytes 1572872 | tf_op jit(solution)/shard_map/ppermute | solution.py:111
  119.0 1.9 collective-permute-start.7
  121.0 0.9 broadcast_in_dim.56
  121.8 1.3 fusion.4
  123.1 4.6 %collective-permute-done.6 = f32[128,1024]{1,0:T(8,128)S(1)} collective-permute-done((f32[128,1024]{1,0:T(8,128)S(1)}, f32[128,1024]{1,0:T(8,128)S(1)}, u32[]{:S(2)}, u32[]{:S(2)}) %collective-permute-start.6) | collective-permute-done | bytes 524320 | tf_op jit(solution)/shard_map/ppermute | solution.py:111
  127.7 8.5 %collective-permute-start.8 = (f32[128,1024]{1,0:T(8,128)S(1)}, f32[128,1024]{1,0:T(8,128)S(1)}, u32[]{:S(2)}, u32[]{:S(2)}) collective-permute-start(f32[128,1024]{1,0:T(8,128)S(1)} %collective-permute-done.6), channel_id=1, source_target_pairs={{0,60},{4,0},{8,4},{12,8},{16,12},{20,16},{24,20},{28,24},{32,28},... | collective-permute-start | bytes 1572872 | tf_op jit(solution)/shard_map/ppermute | solution.py:111
  136.2 1.3 fusion.3
  137.5 1.3 fusion.2
  138.8 4.1 %collective-permute-done.8 = f32[128,1024]{1,0:T(8,128)S(1)} collective-permute-done((f32[128,1024]{1,0:T(8,128)S(1)}, f32[128,1024]{1,0:T(8,128)S(1)}, u32[]{:S(2)}, u32[]{:S(2)}) %collective-permute-start.8) | collective-permute-done | bytes 524320 | tf_op jit(solution)/shard_map/ppermute | solution.py:111
  142.9 1.3 fusion.1
  144.2 7.2 %all-to-all-start = ((f32[32,16,256]{2,1,0:T(8,128)}), f32[32,16,256]{2,1,0:T(8,128)S(1)}, u32[]{:S(2)}, u32[]{:S(2)}) async-start(f32[32,16,256]{2,1,0:T(8,128)} %bitcast.26), calls=%async_computation | async-start | bytes 1048576 | tf_op jit(solution)/shard_map/all_to_all | solution.py:24
  151.5 10.3 %all-to-all-done.update_ref = f32[32,16,256]{2,1,0:T(8,128)S(1)} async-done(((f32[32,16,256]{2,1,0:T(8,128)}), f32[32,16,256]{2,1,0:T(8,128)S(1)}, u32[]{:S(2)}, u32[]{:S(2)}) %all-to-all-start) | async-done | bytes 524320 | tf_op jit(solution)/shard_map/all_to_all | solution.py:24
  161.8 1.3 shard_map.86
  163.2 3.4 %collective-permute-start.9 = (f32[8,2,16,256]{3,2,1,0:T(8,128)S(1)}, f32[8,2,16,256]{3,2,1,0:T(8,128)S(1)}, u32[]{:S(2)}, u32[]{:S(2)}) collective-permute-start(f32[8,2,16,256]{3,2,1,0:T(8,128)S(1)} %dynamic-slice_bitcast_fusion.1), channel_id=1, source_target_pairs={{0,4},{4,0},{8,12},{12,8},{16,20},{20,16},{24,28},{28,24},{32,36},... | collective-permute-start | bytes 786440 | tf_op jit(solution)/shard_map/ppermute | solution.py:123
  166.6 4.8 %collective-permute-done.9 = f32[8,2,16,256]{3,2,1,0:T(8,128)S(1)} collective-permute-done((f32[8,2,16,256]{3,2,1,0:T(8,128)S(1)}, f32[8,2,16,256]{3,2,1,0:T(8,128)S(1)}, u32[]{:S(2)}, u32[]{:S(2)}) %collective-permute-start.9) | collective-permute-done | bytes 262176 | tf_op jit(solution)/shard_map/ppermute | solution.py:123
  171.4 0.7 bitcast_add_fusion.1
  172.2 7.5 %all-to-all-start.1 = ((f32[8,2,16,256]{3,2,1,0:T(8,128)}), f32[8,2,16,256]{3,2,1,0:T(8,128)S(1)}, u32[]{:S(2)}, u32[]{:S(2)}) async-start(f32[8,2,16,256]{3,2,1,0:T(8,128)} %bitcast_add_fusion.1), calls=%async_computation.1 | async-start | bytes 524288 | tf_op jit(solution)/shard_map/all_to_all | solution.py:125
  179.7 1.1 constant_dynamic-slice_fusion
  180.9 20.2 %all-to-all-done.1 = f32[8,2,16,256]{3,2,1,0:T(8,128)S(1)} async-done(((f32[8,2,16,256]{3,2,1,0:T(8,128)}), f32[8,2,16,256]{3,2,1,0:T(8,128)S(1)}, u32[]{:S(2)}, u32[]{:S(2)}) %all-to-all-start.1) | async-done | bytes 262176 | tf_op jit(solution)/shard_map/all_to_all | solution.py:125
  201.3 20.3 %all_to_all.20 = f32[32,2,16,256]{3,2,1,0:T(8,128)S(1)} all-to-all(f32[32,2,16,256]{3,2,1,0:T(8,128)S(1)} %broadcast_in_dim.64), channel_id=1, replica_groups=mesh['front'=8,'row'=16,'col'=4] {'front','col'}, dimensions={0} | all-to-all | bytes 2097152 | tf_op jit(solution)/shard_map/all_to_all | solution.py:24
  221.6 0.8 copy.22
  222.4 0.8 dot_general.37
  223.3 1.7 fusion.16
  225.0 2.1 collective-permute-start.10
  227.1 6.2 %collective-permute-done.10 = f32[8,32,256]{2,1,0:T(8,128)S(1)} collective-permute-done((f32[8,32,256]{2,1,0:T(8,128)S(1)}, f32[8,32,256]{2,1,0:T(8,128)S(1)}, u32[]{:S(2)}, u32[]{:S(2)}) %collective-permute-start.10) | collective-permute-done | bytes 262176 | tf_op jit(solution)/shard_map/ppermute | solution.py:123
  233.3 24.0 %all_to_all.21 = f32[8,32,256]{2,1,0:T(8,128)S(1)} all-to-all(f32[8,32,256]{2,1,0:T(8,128)S(1)} %bitcast_add_fusion), channel_id=1, replica_groups={{0,8,16,24,32,40,48,56},{4,12,20,28,36,44,52,60},{1,9,17,25,33,41,49,57..., dimensions={0} | all-to-all | bytes 524288 | tf_op jit(solution)/shard_map/all_to_all | solution.py:125
  (31 shorter events, 2.3 us)
Async XLA Ops:
  0.6 15.1 %copy-start = (f32[1,1024,256]{2,1,0:T(8,128)S(1)}, f32[1,1024,256]{2,1,0:T(8,128)}, u32[]{:S(2)}) copy-start(f32[1,1024,256]{2,1,0:T(8,128)} %param.8) | copy-start | bytes 3145732
  16.4 25.9 %collective-permute-start.1 = (f32[128,1024]{1,0:T(8,128)S(1)}, f32[128,1024]{1,0:T(8,128)S(1)}, u32[]{:S(2)}, u32[]{:S(2)}) collective-permute-start(f32[128,1024]{1,0:T(8,128)S(1)} %fusion.9), channel_id=1, source_target_pairs={{0,60},{4,0},{8,4},{12,8},{16,12},{20,16},{24,20},{28,24},{32,28},... | collective-permute-start | bytes 1572872 | tf_op jit(solution)/shard_map/ppermute | solution.py:111
  27.8 0.7 copy-start.3
  31.1 16.6 %collective-permute-start = (f32[128,1024]{1,0:T(8,128)S(1)}, f32[128,1024]{1,0:T(8,128)S(1)}, u32[]{:S(2)}, u32[]{:S(2)}) collective-permute-start(f32[128,1024]{1,0:T(8,128)S(1)} %fusion.13), channel_id=1, source_target_pairs={{0,4},{4,8},{8,12},{12,16},{16,20},{20,24},{24,28},{28,32},{32,36}... | collective-permute-start | bytes 1572872 | tf_op jit(solution)/shard_map/ppermute | solution.py:111
  42.5 11.8 %collective-permute-start.2 = (f32[128,1024]{1,0:T(8,128)S(1)}, f32[128,1024]{1,0:T(8,128)S(1)}, u32[]{:S(2)}, u32[]{:S(2)}) collective-permute-start(f32[128,1024]{1,0:T(8,128)S(1)} %add.155), channel_id=1, source_target_pairs={{0,60},{4,0},{8,4},{12,8},{16,12},{20,16},{24,20},{28,24},{32,28},... | collective-permute-start | bytes 1572872 | tf_op jit(solution)/shard_map/ppermute | solution.py:111
  55.0 66.8 %copy-start.1 = (f32[1,256,1024]{2,1,0:T(8,128)S(1)}, f32[1,256,1024]{2,1,0:T(8,128)}, u32[]{:S(2)}) copy-start(f32[1,256,1024]{2,1,0:T(8,128)} %param.9) | copy-start | bytes 3145732
  55.0 24.2 %collective-permute-start.3 = (f32[32,1024]{1,0:T(8,128)S(1)}, f32[32,1024]{1,0:T(8,128)S(1)}, u32[]{:S(2)}, u32[]{:S(2)}) collective-permute-start(f32[32,1024]{1,0:T(8,128)S(1)} %get-tuple-element.10), channel_id=1, source_target_pairs={{0,16},{4,20},{8,24},{12,28},{16,32},{20,36},{24,40},{28,44},{32,4... | collective-permute-start | bytes 393224 | tf_op jit(solution)/shard_map/ppermute | solution.py:111
  57.1 29.1 %collective-permute-start.4 = (f32[32,1024]{1,0:T(8,128)S(1)}, f32[32,1024]{1,0:T(8,128)S(1)}, u32[]{:S(2)}, u32[]{:S(2)}) collective-permute-start(f32[32,1024]{1,0:T(8,128)S(1)} %get-tuple-element.12), channel_id=1, source_target_pairs={{0,32},{4,36},{8,40},{12,44},{16,48},{20,52},{24,56},{28,60},{32,0... | collective-permute-start | bytes 393224 | tf_op jit(solution)/shard_map/ppermute | solution.py:111
  68.0 19.7 %collective-permute-start.5 = (f32[32,1024]{1,0:T(8,128)S(1)}, f32[32,1024]{1,0:T(8,128)S(1)}, u32[]{:S(2)}, u32[]{:S(2)}) collective-permute-start(f32[32,1024]{1,0:T(8,128)S(1)} %get-tuple-element.11), channel_id=1, source_target_pairs={{0,48},{4,52},{8,56},{12,60},{16,0},{20,4},{24,8},{28,12},{32,16},... | collective-permute-start | bytes 393224 | tf_op jit(solution)/shard_map/ppermute | solution.py:111
  87.8 26.0 %copy-start.2 = (f32[32,1024]{1,0:T(8,128)}, f32[32,1024]{1,0:T(8,128)S(1)}, u32[]{:S(2)}) copy-start(f32[32,1024]{1,0:T(8,128)S(1)} %fusion.20) | copy-start | bytes 393220
  113.8 14.0 %collective-permute-start.6 = (f32[128,1024]{1,0:T(8,128)S(1)}, f32[128,1024]{1,0:T(8,128)S(1)}, u32[]{:S(2)}, u32[]{:S(2)}) collective-permute-start(f32[128,1024]{1,0:T(8,128)S(1)} %all_gather.15), channel_id=1, source_target_pairs={{0,60},{4,0},{8,4},{12,8},{16,12},{20,16},{24,20},{28,24},{32,28},... | collective-permute-start | bytes 1572872 | tf_op jit(solution)/shard_map/ppermute | solution.py:111
  119.0 18.5 %collective-permute-start.7 = (f32[128,1024]{1,0:T(8,128)S(1)}, f32[128,1024]{1,0:T(8,128)S(1)}, u32[]{:S(2)}, u32[]{:S(2)}) collective-permute-start(f32[128,1024]{1,0:T(8,128)S(1)} %all_gather.15), channel_id=1, source_target_pairs={{0,4},{4,8},{8,12},{12,16},{16,20},{20,24},{24,28},{28,32},{32,36}... | collective-permute-start | bytes 1572872 | tf_op jit(solution)/shard_map/ppermute | solution.py:111
  127.7 15.2 %collective-permute-start.8 = (f32[128,1024]{1,0:T(8,128)S(1)}, f32[128,1024]{1,0:T(8,128)S(1)}, u32[]{:S(2)}, u32[]{:S(2)}) collective-permute-start(f32[128,1024]{1,0:T(8,128)S(1)} %collective-permute-done.6), channel_id=1, source_target_pairs={{0,60},{4,0},{8,4},{12,8},{16,12},{20,16},{24,20},{28,24},{32,28},... | collective-permute-start | bytes 1572872 | tf_op jit(solution)/shard_map/ppermute | solution.py:111
  144.2 17.6 %all-to-all-start = ((f32[32,16,256]{2,1,0:T(8,128)}), f32[32,16,256]{2,1,0:T(8,128)S(1)}, u32[]{:S(2)}, u32[]{:S(2)}) async-start(f32[32,16,256]{2,1,0:T(8,128)} %bitcast.26), calls=%async_computation | async-start | bytes 1048576 | tf_op jit(solution)/shard_map/all_to_all | solution.py:24
  163.2 8.3 %collective-permute-start.9 = (f32[8,2,16,256]{3,2,1,0:T(8,128)S(1)}, f32[8,2,16,256]{3,2,1,0:T(8,128)S(1)}, u32[]{:S(2)}, u32[]{:S(2)}) collective-permute-start(f32[8,2,16,256]{3,2,1,0:T(8,128)S(1)} %dynamic-slice_bitcast_fusion.1), channel_id=1, source_target_pairs={{0,4},{4,0},{8,12},{12,8},{16,20},{20,16},{24,28},{28,24},{32,36},... | collective-permute-start | bytes 786440 | tf_op jit(solution)/shard_map/ppermute | solution.py:123
  172.2 28.9 %all-to-all-start.1 = ((f32[8,2,16,256]{3,2,1,0:T(8,128)}), f32[8,2,16,256]{3,2,1,0:T(8,128)S(1)}, u32[]{:S(2)}, u32[]{:S(2)}) async-start(f32[8,2,16,256]{3,2,1,0:T(8,128)} %bitcast_add_fusion.1), calls=%async_computation.1 | async-start | bytes 524288 | tf_op jit(solution)/shard_map/all_to_all | solution.py:125
  225.0 8.3 %collective-permute-start.10 = (f32[8,32,256]{2,1,0:T(8,128)S(1)}, f32[8,32,256]{2,1,0:T(8,128)S(1)}, u32[]{:S(2)}, u32[]{:S(2)}) collective-permute-start(f32[8,32,256]{2,1,0:T(8,128)S(1)} %dynamic-slice_bitcast_fusion), channel_id=1, source_target_pairs={{0,4},{4,0},{8,12},{12,8},{16,20},{20,16},{24,28},{28,24},{32,36},... | collective-permute-start | bytes 786440 | tf_op jit(solution)/shard_map/ppermute | solution.py:123

commit v4 on v3

--- a/solution.py
+++ b/solution.py
@@ -98,8 +98,10 @@
     live = start + jnp.arange(border_rows, dtype=jnp.int32) < front_sizes[0, 1]
     index = jnp.where(live, index, -1)
 
-    near = 4
+    near = 8
     far = rows // near
+    down = near // 2
+    up = near - 1 - down
     block = sources // rows
     step = 1 - 2 * lax.rem(front_id, 2)
 
@@ -128,26 +130,32 @@
     def group_at(offset):
         return lax.rem(row_id + offset + near, near)
 
-    rhs = child_rhs[0].reshape(-1, far, near, block).transpose(2, 0, 1, 3)
-    rhs = rhs.reshape(near, -1, far * block)
-    rhs = jnp.stack(
-        [
-            lax.dynamic_index_in_dim(rhs, group_at(offset), 0, keepdims=False)
-            for offset in (2, step, -step, 0)
-        ]
-    )
-    rhs = lax.all_gather(rhs, "col", axis=1, tiled=True)
-
-    def pivot_product(which):
-        return contract(rhs[which], inverse, (0,), (1,))
-
-    from_two = shift(pivot_product(0), -1)
-    below, index = lax.optimization_barrier((pivot_product(1), index))
-    from_below = shift(below, 1)
-    index = lax.all_gather(index, "front", axis=0)
-    from_two, index = lax.optimization_barrier((from_two, index))
-    from_above = shift(pivot_product(2) + from_two, -1)
-    near_sum = pivot_product(3) + from_below + from_above
+    hops = []
+    for hop in range(down):
+        hops.append(("down", -step * (down - hop)))
+        if hop < up:
+            hops.append(("up", step * (up - hop)))
+    groups = child_rhs[0].reshape(-1, far, near, block)
+    first = lax.dynamic_index_in_dim(groups, group_at(hops[0][1]), 2, keepdims=False)
+    first = lax.all_gather(first.reshape(-1, far * block), "col", axis=0, tiled=True)
+    first = contract(first, inverse, (0,), (1,))
+
+    first, rhs = lax.optimization_barrier((first, child_rhs[0]))
+    running = {"down": shift(first, -1)}
+    rhs = lax.all_gather(rhs, "col", axis=0, tiled=True)
+    rhs = rhs.T.reshape(far, near, block, -1).transpose(1, 0, 2, 3)
+    rhs = rhs.reshape(near, far * block, -1)
+
+    def pivot_product(offset):
+        value = lax.dynamic_index_in_dim(rhs, group_at(offset), 0, keepdims=False)
+        return contract(value, inverse, (1,), (1,))
+
+    for way, offset in hops[1:]:
+        value = pivot_product(offset)
+        if way in running:
+            value = value + running[way]
+        running[way] = shift(value, -1 if way == "down" else 1)
+    near_sum = pivot_product(0) + running["down"] + running["up"]
     near_sum = near_sum.reshape(far, block, pivot_rows)
     far_id = lax.div(row_id, near)
 
@@ -155,23 +163,32 @@
         return lax.dynamic_index_in_dim(near_sum, lax.rem(far_id + offset, far), 0, keepdims=False)
 
     own = far_block(0)
-    for offset in range(1, far):
-        own = own + shift(far_block(offset), offset * near, False)
+    away, index = lax.optimization_barrier((far_block(1), index))
+    away = shift(away, near, False)
+    index = lax.all_gather(index, "front", axis=0)
+    away, index = lax.optimization_barrier((away, index))
     pivot_live = col_id * pivot_rows + jnp.arange(pivot_rows, dtype=jnp.int32) < front_sizes[0, 0]
-    own = jnp.where(pivot_live[None, :], own, 0.0)
-
-    apart = [[g + near * i for i in range(far)] for g in range(near)]
-    solved = lax.all_gather(own, "row", axis_index_groups=apart, axis=0, tiled=True)
-    solved_above = shift(solved, -1)
-    solved_below = shift(solved, 1)
-    solved_two = shift(solved_above, -1)
+    own = jnp.where(pivot_live[None, :], own + away, 0.0)
+
+    away = shift(own, near, False)
+    solved = jnp.where(far_id == 0, jnp.stack([own, away]), jnp.stack([away, own]))
+    solved = solved.reshape(far * block, pivot_rows)
     update = jnp.zeros((near, far * block, border_rows), jnp.float32)
-    for value, offset in (
-        (solved, 0), (solved_above, step), (solved_below, -step), (solved_two, 2)
-    ):
+
+    def place_product(update, value, offset):
         piece = contract(value, border, (1,), (1,))
-        update = lax.dynamic_update_slice_in_dim(update, piece[None], group_at(offset), 0)
-    update = update.reshape(sources, border_rows)
+        return lax.dynamic_update_slice_in_dim(update, piece[None], group_at(offset), 0)
+
+    above, below = solved, solved
+    arrived = [(solved, 0)]
+    for hop in range(1, down + 1):
+        above = shift(above, -1)
+        arrived.append((above, step * hop))
+        if hop <= up:
+            below = shift(below, 1)
+            arrived.append((below, -step * hop))
+    for value, offset in arrived:
+        update = place_product(update, value, offset)
     update = exchange(update.reshape(layer, part, border_rows), ("front", "col"))
 
     low = jnp.where(index < 0, -1, lax.div(index, high_count))

time: 259 us -> 279 us (1.077)
  the two profiles are of different devices: /device:TPU:2 before, /device:TPU:4 now
where the time goes in v4:
time: 279 us; the launch traced here: 277 us
  starting transfers between devices  91.8 us (33%)
  blocking collectives  80 us (29%)
  waiting for transfers between devices  68.6 us (25%)
  matrix products  20.3 us (7%)
  local copies, waits for them, and re-layouts  7.63 us (3%)
  other arithmetic  6.49 us (2%)
    ppermute x16, starting transfers between devices, shift(): return lax.ppermute(value, ('front', 'row'), pairs)  73.8 us
    ppermute x16, waiting for transfers between devices, shift(): return lax.ppermute(value, ('front', 'row'), pairs)  28.3 us
    all_to_all x1, blocking collectives, row_sum(): mine = lax.all_to_all(mine, 'row', 0, 0, axis_index_groups=same, tiled=True)  24.3 us
    all_to_all x1, blocking collectives, exchange(): return lax.all_to_all(blocks, axes, split_axis=0, concat_axis=0, tiled=True)  22 us
    dot_general x17, matrix products, contract(): lax.dot_general(left, right, ((left_dims, right_dims), ((), ())), precisi...  20.3 us
    all_to_all x1, waiting for transfers between devices, row_sum(): mine = lax.all_to_all(mine, 'row', 0, 0, axis_index_groups=same, tiled=True)  18.7 us
    all_gather x1, blocking collectives, local(): rhs = lax.all_gather(rhs, 'col', axis=0, tiled=True)  12.8 us
    all_gather x1, blocking collectives, local(): lax.all_gather(first.reshape(-1, far * block), 'col', axis=0, tiled=True)  12.5 us
  transfers between devices with their start and end apart: 20, of which 14 were waited for; matrix products, arithmetic and copies ran while one was open for 8% of the time, Pallas kernels for 0%

profile of v4, /device:TPU:4, one launch (start us, length us, event | category | flops | bytes accessed | tf_op | source)
XLA Modules:
  0.0 277.3 jit_solution(16055963143461545594)
XLA Ops:
  1.9 12.5 %all_gather.12 = f32[256,64]{1,0:T(8,128)S(1)} all-gather(f32[64,64]{1,0:T(8,128)S(1)} %copy.18), channel_id=1, replica_groups=mesh['front'=8,'row'=16,'col'=4] {'col'}, dimensions={0}, use_global_device_ids=true | all-gather | bytes 81920 | tf_op jit(solution)/shard_map/all_gather | solution.py:140
  14.4 2.6 fusion.28
  17.0 11.4 %collective-permute-start = (f32[64,1024]{1,0:T(8,128)}, f32[64,1024]{1,0:T(8,128)}, u32[]{:S(2)}, u32[]{:S(2)}) collective-permute-start(f32[64,1024]{1,0:T(8,128)} %fusion.28), channel_id=1, source_target_pairs={{0,60},{4,0},{8,4},{12,8},{16,12},{20,16},{24,20},{28,24},{32,28},... | collective-permute-start | bytes 786440 | tf_op jit(solution)/shard_map/ppermute | solution.py:113
  28.4 12.8 %all_gather.13 = f32[256,512]{1,0:T(8,128)S(1)} all-gather(f32[64,512]{1,0:T(8,128)S(1)} %bitcast.167), channel_id=1, replica_groups=mesh['front'=8,'row'=16,'col'=4] {'col'}, dimensions={0}, use_global_device_ids=true | all-gather | bytes 655360 | tf_op jit(solution)/shard_map/all_gather | solution.py:145
  43.1 1.9 collective-permute-start.4
  46.9 1.6 convolution_add_fusion.1
  48.4 5.1 %collective-permute-start.1 = (f32[64,1024]{1,0:T(8,128)S(1)}, f32[64,1024]{1,0:T(8,128)S(1)}, u32[]{:S(2)}, u32[]{:S(2)}) collective-permute-start(f32[64,1024]{1,0:T(8,128)S(1)} %convolution_add_fusion.1), channel_id=1, source_target_pairs={{0,60},{4,0},{8,4},{12,8},{16,12},{20,16},{24,20},{28,24},{32,28},... | collective-permute-start | bytes 786440 | tf_op jit(solution)/shard_map/ppermute | solution.py:113
  54.7 1.6 convolution_add_fusion
  56.3 1.9 collective-permute-start.5
  59.0 5.1 %collective-permute-start.2 = (f32[64,1024]{1,0:T(8,128)}, f32[64,1024]{1,0:T(8,128)}, u32[]{:S(2)}, u32[]{:S(2)}) collective-permute-start(f32[64,1024]{1,0:T(8,128)} %add.205), channel_id=1, source_target_pairs={{0,60},{4,0},{8,4},{12,8},{16,12},{20,16},{24,20},{28,24},{32,28},... | collective-permute-start | bytes 786440 | tf_op jit(solution)/shard_map/ppermute | solution.py:113
  67.5 1.9 collective-permute-start.6
  70.8 5.6 %collective-permute-start.3 = (f32[64,1024]{1,0:T(8,128)S(1)}, f32[64,1024]{1,0:T(8,128)S(1)}, u32[]{:S(2)}, u32[]{:S(2)}) collective-permute-start(f32[64,1024]{1,0:T(8,128)S(1)} %add.206), channel_id=1, source_target_pairs={{0,60},{4,0},{8,4},{12,8},{16,12},{20,16},{24,20},{28,24},{32,28},... | collective-permute-start | bytes 786440 | tf_op jit(solution)/shard_map/ppermute | solution.py:113
  77.7 2.6 collective-permute-done.3
  81.3 13.7 %collective-permute-start.7 = (f32[32,1024]{1,0:T(8,128)S(1)}, f32[32,1024]{1,0:T(8,128)S(1)}, u32[]{:S(2)}, u32[]{:S(2)}) collective-permute-start(f32[32,1024]{1,0:T(8,128)S(1)} %dynamic-slice_bitcast_fusion.2), channel_id=1, source_target_pairs={{0,32},{4,36},{8,40},{12,44},{16,48},{20,52},{24,56},{28,60},{32,0... | collective-permute-start | bytes 393224 | tf_op jit(solution)/shard_map/ppermute | solution.py:113
  95.6 8.4 %all-gather.1 = s32[8,1,256]{2,1,0:T(1,128)S(1)} all-gather(s32[1,1,256]{2,1,0:T(1,128)S(1)} %bitcast.175), channel_id=2, replica_groups=mesh['front'=8,'row'=16,'col'=4] {'front'}, dimensions={0}, use_global_device_ids=true | all-gather | bytes 9216 | tf_op jit(solution)/shard_map/all_gather | solution.py:168
  104.1 6.5 %collective-permute-start.8 = (f32[32,1024]{1,0:T(8,128)S(1)}, f32[32,1024]{1,0:T(8,128)S(1)}, u32[]{:S(2)}, u32[]{:S(2)}) collective-permute-start(f32[32,1024]{1,0:T(8,128)S(1)} %fusion.32), channel_id=1, source_target_pairs={{0,32},{4,36},{8,40},{12,44},{16,48},{20,52},{24,56},{28,60},{32,0... | collective-permute-start | bytes 393224 | tf_op jit(solution)/shard_map/ppermute | solution.py:113
  110.6 13.3 %collective-permute-done.8 = f32[32,1024]{1,0:T(8,128)S(1)} collective-permute-done((f32[32,1024]{1,0:T(8,128)S(1)}, f32[32,1024]{1,0:T(8,128)S(1)}, u32[]{:S(2)}, u32[]{:S(2)}) %collective-permute-start.8) | collective-permute-done | bytes 131104 | tf_op jit(solution)/shard_map/ppermute | solution.py:113
  123.9 3.1 %collective-permute-start.9 = (f32[64,1024]{1,0:T(8,128)S(1)}, f32[64,1024]{1,0:T(8,128)S(1)}, u32[]{:S(2)}, u32[]{:S(2)}) collective-permute-start(f32[64,1024]{1,0:T(8,128)S(1)} %bitcast.161), channel_id=1, source_target_pairs={{0,60},{4,0},{8,4},{12,8},{16,12},{20,16},{24,20},{28,24},{32,28},... | collective-permute-start | bytes 786440 | tf_op jit(solution)/shard_map/ppermute | solution.py:113
  127.1 2.7 collective-permute-start.10
  130.6 1.2 fusion.7
  131.8 2.5 collective-permute-done.9
  134.4 2.5 collective-permute-start.11
  136.9 1.2 fusion.6
  138.1 3.3 %collective-permute-start.12 = (f32[64,1024]{1,0:T(8,128)S(1)}, f32[64,1024]{1,0:T(8,128)S(1)}, u32[]{:S(2)}, u32[]{:S(2)}) collective-permute-start(f32[64,1024]{1,0:T(8,128)S(1)} %collective-permute-done.10), channel_id=1, source_target_pairs={{0,4},{4,8},{8,12},{12,16},{16,20},{20,24},{24,28},{28,32},{32,36}... | collective-permute-start | bytes 786440 | tf_op jit(solution)/shard_map/ppermute | solution.py:113
  141.4 1.2 fusion.5
  142.7 2.7 collective-permute-done.11
  145.4 1.9 collective-permute-start.13
  147.3 1.2 fusion.4
  148.6 3.9 %collective-permute-start.14 = (f32[64,1024]{1,0:T(8,128)S(1)}, f32[64,1024]{1,0:T(8,128)S(1)}, u32[]{:S(2)}, u32[]{:S(2)}) collective-permute-start(f32[64,1024]{1,0:T(8,128)S(1)} %collective-permute-done.12), channel_id=1, source_target_pairs={{0,4},{4,8},{8,12},{12,16},{16,20},{20,24},{24,28},{28,32},{32,36}... | collective-permute-start | bytes 786440 | tf_op jit(solution)/shard_map/ppermute | solution.py:113
  152.5 1.2 fusion.3
  153.7 1.9 collective-permute-done.13
  155.6 3.1 %collective-permute-start.15 = (f32[64,1024]{1,0:T(8,128)S(1)}, f32[64,1024]{1,0:T(8,128)S(1)}, u32[]{:S(2)}, u32[]{:S(2)}) collective-permute-start(f32[64,1024]{1,0:T(8,128)S(1)} %collective-permute-done.13), channel_id=1, source_target_pairs={{0,60},{4,0},{8,4},{12,8},{16,12},{20,16},{24,20},{28,24},{32,28},... | collective-permute-start | bytes 786440 | tf_op jit(solution)/shard_map/ppermute | solution.py:113
  158.8 1.2 fusion.2
  160.2 1.2 fusion.1
  161.4 2.5 collective-permute-done.15
  163.9 1.2 fusion
  165.1 8.8 %all-to-all-start = ((f32[32,16,256]{2,1,0:T(8,128)}), f32[32,16,256]{2,1,0:T(8,128)S(1)}, u32[]{:S(2)}, u32[]{:S(2)}) async-start(f32[32,16,256]{2,1,0:T(8,128)} %bitcast.38), calls=%async_computation | async-start | bytes 1048576 | tf_op jit(solution)/shard_map/all_to_all | solution.py:24
  174.0 9.9 %all-to-all-done.update_ref = f32[32,16,256]{2,1,0:T(8,128)S(1)} async-done(((f32[32,16,256]{2,1,0:T(8,128)}), f32[32,16,256]{2,1,0:T(8,128)S(1)}, u32[]{:S(2)}, u32[]{:S(2)}) %all-to-all-start) | async-done | bytes 524320 | tf_op jit(solution)/shard_map/all_to_all | solution.py:24
  183.9 1.3 shard_map.86
  185.2 1.9 collective-permute-start.16
  187.2 6.3 %collective-permute-done.16 = f32[8,2,16,256]{3,2,1,0:T(8,128)S(1)} collective-permute-done((f32[8,2,16,256]{3,2,1,0:T(8,128)S(1)}, f32[8,2,16,256]{3,2,1,0:T(8,128)S(1)}, u32[]{:S(2)}, u32[]{:S(2)}) %collective-permute-start.16) | collective-permute-done | bytes 262176 | tf_op jit(solution)/shard_map/ppermute | solution.py:125
  194.2 4.4 %all-to-all-start.1 = ((f32[8,2,16,256]{3,2,1,0:T(8,128)}), f32[8,2,16,256]{3,2,1,0:T(8,128)S(1)}, u32[]{:S(2)}, u32[]{:S(2)}) async-start(f32[8,2,16,256]{3,2,1,0:T(8,128)} %bitcast_add_fusion.1), calls=%async_computation.1 | async-start | bytes 524288 | tf_op jit(solution)/shard_map/all_to_all | solution.py:127
  199.8 18.7 %all-to-all-done.1 = f32[8,2,16,256]{3,2,1,0:T(8,128)S(1)} async-done(((f32[8,2,16,256]{3,2,1,0:T(8,128)}), f32[8,2,16,256]{3,2,1,0:T(8,128)S(1)}, u32[]{:S(2)}, u32[]{:S(2)}) %all-to-all-start.1) | async-done | bytes 262176 | tf_op jit(solution)/shard_map/all_to_all | solution.py:127
  218.6 22.0 %all_to_all.20 = f32[32,2,16,256]{3,2,1,0:T(8,128)S(1)} all-to-all(f32[32,2,16,256]{3,2,1,0:T(8,128)S(1)} %broadcast_in_dim.80), channel_id=1, replica_groups=mesh['front'=8,'row'=16,'col'=4] {'front','col'}, dimensions={0} | all-to-all | bytes 2097152 | tf_op jit(solution)/shard_map/all_to_all | solution.py:24
  242.4 1.7 fusion.30
  244.1 2.9 %collective-permute-start.17 = (f32[8,32,256]{2,1,0:T(8,128)S(1)}, f32[8,32,256]{2,1,0:T(8,128)S(1)}, u32[]{:S(2)}, u32[]{:S(2)}) collective-permute-start(f32[8,32,256]{2,1,0:T(8,128)S(1)} %dynamic-slice_bitcast_fusion), channel_id=1, source_target_pairs={{0,4},{4,0},{8,12},{12,8},{16,20},{20,16},{24,28},{28,24},{32,36},... | collective-permute-start | bytes 786440 | tf_op jit(solution)/shard_map/ppermute | solution.py:125
  247.0 5.4 %collective-permute-done.17 = f32[8,32,256]{2,1,0:T(8,128)S(1)} collective-permute-done((f32[8,32,256]{2,1,0:T(8,128)S(1)}, f32[8,32,256]{2,1,0:T(8,128)S(1)}, u32[]{:S(2)}, u32[]{:S(2)}) %collective-permute-start.17) | collective-permute-done | bytes 262176 | tf_op jit(solution)/shard_map/ppermute | solution.py:125
  252.4 24.3 %all_to_all.21 = f32[8,32,256]{2,1,0:T(8,128)S(1)} all-to-all(f32[8,32,256]{2,1,0:T(8,128)S(1)} %bitcast_add_fusion), channel_id=1, replica_groups={{0,8,16,24,32,40,48,56},{4,12,20,28,36,44,52,60},{1,9,17,25,33,41,49,57..., dimensions={0} | all-to-all | bytes 524288 | tf_op jit(solution)/shard_map/all_to_all | solution.py:127
  (58 shorter events, 20.0 us)
Async XLA Ops:
  0.6 130.0 %copy-start = (f32[1,256,1024]{2,1,0:T(8,128)S(1)}, f32[1,256,1024]{2,1,0:T(8,128)}, u32[]{:S(2)}) copy-start(f32[1,256,1024]{2,1,0:T(8,128)} %param.9) | copy-start | bytes 3145732
  14.4 14.0 %copy-start.2 = (f32[1,64,512]{2,1,0:T(8,128)S(1)}, f32[1,64,512]{2,1,0:T(8,128)}, u32[]{:S(2)}) copy-start(f32[1,64,512]{2,1,0:T(8,128)} %param.7) | copy-start | bytes 393220
  17.0 29.8 %collective-permute-start = (f32[64,1024]{1,0:T(8,128)}, f32[64,1024]{1,0:T(8,128)}, u32[]{:S(2)}, u32[]{:S(2)}) collective-permute-start(f32[64,1024]{1,0:T(8,128)} %fusion.28), channel_id=1, source_target_pairs={{0,60},{4,0},{8,4},{12,8},{16,12},{20,16},{24,20},{28,24},{32,28},... | collective-permute-start | bytes 786440 | tf_op jit(solution)/shard_map/ppermute | solution.py:113
  41.2 1.2 copy-start.1
  43.1 11.7 %collective-permute-start.4 = (f32[64,1024]{1,0:T(8,128)S(1)}, f32[64,1024]{1,0:T(8,128)}, u32[]{:S(2)}, u32[]{:S(2)}) collective-permute-start(f32[64,1024]{1,0:T(8,128)S(1)} %fusion.16), channel_id=1, source_target_pairs={{0,4},{4,8},{8,12},{12,16},{16,20},{20,24},{24,28},{28,32},{32,36}... | collective-permute-start | bytes 786440 | tf_op jit(solution)/shard_map/ppermute | solution.py:113
  45.0 0.7 copy-start.4
  48.4 9.8 %collective-permute-start.1 = (f32[64,1024]{1,0:T(8,128)S(1)}, f32[64,1024]{1,0:T(8,128)S(1)}, u32[]{:S(2)}, u32[]{:S(2)}) collective-permute-start(f32[64,1024]{1,0:T(8,128)S(1)} %convolution_add_fusion.1), channel_id=1, source_target_pairs={{0,60},{4,0},{8,4},{12,8},{16,12},{20,16},{24,20},{28,24},{32,28},... | collective-permute-start | bytes 786440 | tf_op jit(solution)/shard_map/ppermute | solution.py:113
  56.3 10.2 %collective-permute-start.5 = (f32[64,1024]{1,0:T(8,128)S(1)}, f32[64,1024]{1,0:T(8,128)}, u32[]{:S(2)}, u32[]{:S(2)}) collective-permute-start(f32[64,1024]{1,0:T(8,128)S(1)} %convolution_add_fusion), channel_id=1, source_target_pairs={{0,4},{4,8},{8,12},{12,16},{16,20},{20,24},{24,28},{28,32},{32,36}... | collective-permute-start | bytes 786440 | tf_op jit(solution)/shard_map/ppermute | solution.py:113
  59.0 10.8 %collective-permute-start.2 = (f32[64,1024]{1,0:T(8,128)}, f32[64,1024]{1,0:T(8,128)}, u32[]{:S(2)}, u32[]{:S(2)}) collective-permute-start(f32[64,1024]{1,0:T(8,128)} %add.205), channel_id=1, source_target_pairs={{0,60},{4,0},{8,4},{12,8},{16,12},{20,16},{24,20},{28,24},{32,28},... | collective-permute-start | bytes 786440 | tf_op jit(solution)/shard_map/ppermute | solution.py:113
  67.5 10.2 %collective-permute-start.6 = (f32[64,1024]{1,0:T(8,128)S(1)}, f32[64,1024]{1,0:T(8,128)}, u32[]{:S(2)}, u32[]{:S(2)}) collective-permute-start(f32[64,1024]{1,0:T(8,128)S(1)} %add.218), channel_id=1, source_target_pairs={{0,4},{4,8},{8,12},{12,16},{16,20},{20,24},{24,28},{28,32},{32,36}... | collective-permute-start | bytes 786440 | tf_op jit(solution)/shard_map/ppermute | solution.py:113
  70.8 9.5 %collective-permute-start.3 = (f32[64,1024]{1,0:T(8,128)S(1)}, f32[64,1024]{1,0:T(8,128)S(1)}, u32[]{:S(2)}, u32[]{:S(2)}) collective-permute-start(f32[64,1024]{1,0:T(8,128)S(1)} %add.206), channel_id=1, source_target_pairs={{0,60},{4,0},{8,4},{12,8},{16,12},{20,16},{24,20},{28,24},{32,28},... | collective-permute-start | bytes 786440 | tf_op jit(solution)/shard_map/ppermute | solution.py:113
  81.3 22.8 %collective-permute-start.7 = (f32[32,1024]{1,0:T(8,128)S(1)}, f32[32,1024]{1,0:T(8,128)S(1)}, u32[]{:S(2)}, u32[]{:S(2)}) collective-permute-start(f32[32,1024]{1,0:T(8,128)S(1)} %dynamic-slice_bitcast_fusion.2), channel_id=1, source_target_pairs={{0,32},{4,36},{8,40},{12,44},{16,48},{20,52},{24,56},{28,60},{32,0... | collective-permute-start | bytes 393224 | tf_op jit(solution)/shard_map/ppermute | solution.py:113
  104.0 19.8 %copy-start.3 = (f32[32,1024]{1,0:T(8,128)}, f32[32,1024]{1,0:T(8,128)S(1)}, u32[]{:S(2)}) copy-start(f32[32,1024]{1,0:T(8,128)S(1)} %fusion.32) | copy-start | bytes 393220
  104.1 19.8 %collective-permute-start.8 = (f32[32,1024]{1,0:T(8,128)S(1)}, f32[32,1024]{1,0:T(8,128)S(1)}, u32[]{:S(2)}, u32[]{:S(2)}) collective-permute-start(f32[32,1024]{1,0:T(8,128)S(1)} %fusion.32), channel_id=1, source_target_pairs={{0,32},{4,36},{8,40},{12,44},{16,48},{20,52},{24,56},{28,60},{32,0... | collective-permute-start | bytes 393224 | tf_op jit(solution)/shard_map/ppermute | solution.py:113
  123.9 10.5 %collective-permute-start.9 = (f32[64,1024]{1,0:T(8,128)S(1)}, f32[64,1024]{1,0:T(8,128)S(1)}, u32[]{:S(2)}, u32[]{:S(2)}) collective-permute-start(f32[64,1024]{1,0:T(8,128)S(1)} %bitcast.161), channel_id=1, source_target_pairs={{0,60},{4,0},{8,4},{12,8},{16,12},{20,16},{24,20},{28,24},{32,28},... | collective-permute-start | bytes 786440 | tf_op jit(solution)/shard_map/ppermute | solution.py:113
  127.1 11.1 %collective-permute-start.10 = (f32[64,1024]{1,0:T(8,128)S(1)}, f32[64,1024]{1,0:T(8,128)S(1)}, u32[]{:S(2)}, u32[]{:S(2)}) collective-permute-start(f32[64,1024]{1,0:T(8,128)S(1)} %bitcast.162), channel_id=1, source_target_pairs={{0,4},{4,8},{8,12},{12,16},{16,20},{20,24},{24,28},{28,32},{32,36}... | collective-permute-start | bytes 786440 | tf_op jit(solution)/shard_map/ppermute | solution.py:113
  134.4 11.1 %collective-permute-start.11 = (f32[64,1024]{1,0:T(8,128)S(1)}, f32[64,1024]{1,0:T(8,128)S(1)}, u32[]{:S(2)}, u32[]{:S(2)}) collective-permute-start(f32[64,1024]{1,0:T(8,128)S(1)} %collective-permute-done.9), channel_id=1, source_target_pairs={{0,60},{4,0},{8,4},{12,8},{16,12},{20,16},{24,20},{28,24},{32,28},... | collective-permute-start | bytes 786440 | tf_op jit(solution)/shard_map/ppermute | solution.py:113
  138.1 10.4 %collective-permute-start.12 = (f32[64,1024]{1,0:T(8,128)S(1)}, f32[64,1024]{1,0:T(8,128)S(1)}, u32[]{:S(2)}, u32[]{:S(2)}) collective-permute-start(f32[64,1024]{1,0:T(8,128)S(1)} %collective-permute-done.10), channel_id=1, source_target_pairs={{0,4},{4,8},{8,12},{12,16},{16,20},{20,24},{24,28},{28,32},{32,36}... | collective-permute-start | bytes 786440 | tf_op jit(solution)/shard_map/ppermute | solution.py:113
  145.4 10.2 %collective-permute-start.13 = (f32[64,1024]{1,0:T(8,128)S(1)}, f32[64,1024]{1,0:T(8,128)S(1)}, u32[]{:S(2)}, u32[]{:S(2)}) collective-permute-start(f32[64,1024]{1,0:T(8,128)S(1)} %collective-permute-done.11), channel_id=1, source_target_pairs={{0,60},{4,0},{8,4},{12,8},{16,12},{20,16},{24,20},{28,24},{32,28},... | collective-permute-start | bytes 786440 | tf_op jit(solution)/shard_map/ppermute | solution.py:113
  148.6 11.6 %collective-permute-start.14 = (f32[64,1024]{1,0:T(8,128)S(1)}, f32[64,1024]{1,0:T(8,128)S(1)}, u32[]{:S(2)}, u32[]{:S(2)}) collective-permute-start(f32[64,1024]{1,0:T(8,128)S(1)} %collective-permute-done.12), channel_id=1, source_target_pairs={{0,4},{4,8},{8,12},{12,16},{16,20},{20,24},{24,28},{28,32},{32,36}... | collective-permute-start | bytes 786440 | tf_op jit(solution)/shard_map/ppermute | solution.py:113
  155.6 8.3 %collective-permute-start.15 = (f32[64,1024]{1,0:T(8,128)S(1)}, f32[64,1024]{1,0:T(8,128)S(1)}, u32[]{:S(2)}, u32[]{:S(2)}) collective-permute-start(f32[64,1024]{1,0:T(8,128)S(1)} %collective-permute-done.13), channel_id=1, source_target_pairs={{0,60},{4,0},{8,4},{12,8},{16,12},{20,16},{24,20},{28,24},{32,28},... | collective-permute-start | bytes 786440 | tf_op jit(solution)/shard_map/ppermute | solution.py:113
  165.1 18.7 %all-to-all-start = ((f32[32,16,256]{2,1,0:T(8,128)}), f32[32,16,256]{2,1,0:T(8,128)S(1)}, u32[]{:S(2)}, u32[]{:S(2)}) async-start(f32[32,16,256]{2,1,0:T(8,128)} %bitcast.38), calls=%async_computation | async-start | bytes 1048576 | tf_op jit(solution)/shard_map/all_to_all | solution.py:24
  185.2 8.3 %collective-permute-start.16 = (f32[8,2,16,256]{3,2,1,0:T(8,128)S(1)}, f32[8,2,16,256]{3,2,1,0:T(8,128)S(1)}, u32[]{:S(2)}, u32[]{:S(2)}) collective-permute-start(f32[8,2,16,256]{3,2,1,0:T(8,128)S(1)} %dynamic-slice_bitcast_fusion.1), channel_id=1, source_target_pairs={{0,4},{4,0},{8,12},{12,8},{16,20},{20,16},{24,28},{28,24},{32,36},... | collective-permute-start | bytes 786440 | tf_op jit(solution)/shard_map/ppermute | solution.py:125
  194.2 24.2 %all-to-all-start.1 = ((f32[8,2,16,256]{3,2,1,0:T(8,128)}), f32[8,2,16,256]{3,2,1,0:T(8,128)S(1)}, u32[]{:S(2)}, u32[]{:S(2)}) async-start(f32[8,2,16,256]{3,2,1,0:T(8,128)} %bitcast_add_fusion.1), calls=%async_computation.1 | async-start | bytes 524288 | tf_op jit(solution)/shard_map/all_to_all | solution.py:127
  244.1 8.3 %collective-permute-start.17 = (f32[8,32,256]{2,1,0:T(8,128)S(1)}, f32[8,32,256]{2,1,0:T(8,128)S(1)}, u32[]{:S(2)}, u32[]{:S(2)}) collective-permute-start(f32[8,32,256]{2,1,0:T(8,128)S(1)} %dynamic-slice_bitcast_fusion), channel_id=1, source_target_pairs={{0,4},{4,0},{8,12},{12,8},{16,20},{20,16},{24,28},{28,24},{32,36},... | collective-permute-start | bytes 786440 | tf_op jit(solution)/shard_map/ppermute | solution.py:125

commit v5 on v3

v5 whole, which is shorter than its diff:
```python
import functools

import jax
import jax.numpy as jnp
from jax import lax
from jax.experimental import pallas as pl
from jax.experimental.pallas import tpu as pltpu
from jax.sharding import PartitionSpec as P

HIGH = lax.Precision.HIGH


def contract(left, right, left_dims, right_dims):
    return lax.dot_general(
        left,
        right,
        ((left_dims, right_dims), ((), ())),
        precision=HIGH,
        preferred_element_type=jnp.float32,
    )


def exchange(blocks, axes):
    return lax.all_to_all(blocks, axes, split_axis=0, concat_axis=0, tiled=True)


def land_kernel(fronts, cols, update_ref, place_ref, high_ref, out_ref):
    part, border_rows = update_ref.shape[1:]
    out_rows, high_count = out_ref.shape
    places = out_rows // part
    repeats = max(1, 8 // part)
    shape = (places // repeats, repeats * part, border_rows)
    place_iota = lax.broadcasted_iota(jnp.int32, shape, 0) * repeats
    place_iota = place_iota + lax.broadcasted_iota(jnp.int32, shape, 1) // part
    high_iota = lax.broadcasted_iota(jnp.int32, (high_count, border_rows), 0)
    total = None
    for front in range(fronts):
        value = update_ref[front * cols]
        for col in range(1, cols):
            value = value + update_ref[front * cols + col]
        value = jnp.concatenate([value] * repeats, 0)
        coarse = value.astype(jnp.bfloat16).astype(jnp.float32)
        at_high = jnp.where(high_iota == high_ref[front], 1.0, 0.0).astype(jnp.bfloat16)
        at_place = place_iota == place_ref[front][None]
        pieces = []
        for piece in (coarse, value - coarse):
            spread = jnp.where(at_place, piece[None], 0.0)
            pieces.append(spread.reshape(out_rows, border_rows).astype(jnp.bfloat16))
        landed = lax.dot_general(
            jnp.concatenate(pieces, 0),
            at_high,
            (((1,), (1,)), ((), ())),
            preferred_element_type=jnp.float32,
        )
        landed = landed[:out_rows] + landed[out_rows:]
        total = landed if total is None else total + landed
    out_ref[...] = total


def land(update, place, high, fronts, cols, places, high_count):
    part, border_rows = update.shape[1:]
    return pl.pallas_call(
        functools.partial(land_kernel, fronts, cols),
        out_shape=jax.ShapeDtypeStruct((places * part, high_count), jnp.float32),
        in_specs=[pl.BlockSpec(memory_space=pltpu.VMEM)] * 3,
        out_specs=pl.BlockSpec(memory_space=pltpu.VMEM),
        compiler_params=pltpu.CompilerParams(vmem_limit_bytes=32 * 1024 * 1024),
        cost_estimate=pl.CostEstimate(
            flops=4 * places * part * high_count * fronts * border_rows,
            bytes_accessed=4 * (update.size + places * part * high_count),
            transcendentals=0,
        ),
    )(update, place[:, None], high[:, None])


def local(
    child_rhs, pivot_inverse, border_factor, front_sizes, border_index, root_rhs, root_inverse
):
    rows = lax.axis_size("row")
    cols = lax.axis_size("col")
    fronts = lax.axis_size("front")
    layer = fronts * cols
    col_id = lax.axis_index("col")
    row_id = lax.axis_index("row")
    front_id = lax.axis_index("front")
    inverse = pivot_inverse[0]
    border = border_factor[0]
    pivot_rows = inverse.shape[0]
    border_rows = border.shape[0]
    root_rows, sources = root_rhs.shape
    near = 4
    part = sources // near // layer
    halves = 2
    low_count = rows * halves
    high_count = root_rows // halves

    far = rows // near
    block = sources // rows
    step = 1 - 2 * lax.rem(front_id, 2)

    def shift(value, distance, mirrored=True):
        pairs = []
        for front in range(fronts):
            by = -distance if mirrored and front % 2 else distance
            pairs += [(front * rows + z, front * rows + (z + by) % rows) for z in range(rows)]
        return lax.ppermute(value, ("front", "row"), pairs)

    def row_sum(blocks):
        parity = lax.rem(row_id, 2)
        pairs = []
        for front in range(fronts):
            by = front % 2
            pairs += [
                (front * rows + z, front * rows + (((z + by) ^ 1) - by) % rows) for z in range(rows)
            ]
        theirs = lax.dynamic_index_in_dim(blocks, 1 - parity, 0, keepdims=False)
        mine = lax.dynamic_index_in_dim(blocks, parity, 0, keepdims=False)
        mine = mine + lax.ppermute(theirs, ("front", "row"), pairs)
        same = [list(range(first, rows, 2)) for first in (0, 1)]
        mine = lax.all_to_all(mine, "row", 0, 0, axis_index_groups=same, tiled=True)
        return mine.sum(0)

    def group_at(offset):
        return lax.rem(row_id + offset + near, near)

    index = []
    for offset in (0, step, -step, 2 * step):
        start = lax.rem(row_id + offset + rows, rows) * border_rows
        live = start + jnp.arange(border_rows, dtype=jnp.int32) < front_sizes[0, 1]
        piece = lax.dynamic_slice_in_dim(border_index[0], start, border_rows)
        index.append(jnp.where(live, piece, -1))
    index = jnp.concatenate(index)

    rhs = child_rhs[0].reshape(-1, far, near, block).transpose(2, 0, 1, 3)
    rhs = rhs.reshape(near, -1, far * block)
    rhs = jnp.stack(
        [
            lax.dynamic_index_in_dim(rhs, group_at(offset), 0, keepdims=False)
            for offset in (2, step, -step, 0)
        ]
    )
    border_above = shift(border, -1)
    rhs = lax.all_gather(rhs, "col", axis=1, tiled=True)
    rhs, border_above = lax.optimization_barrier((rhs, border_above))

    def pivot_product(which):
        return contract(rhs[which], inverse, (0,), (1,))

    from_two = shift(pivot_product(0), -1)
    from_below = shift(pivot_product(1), 1)
    above, border_sent = lax.optimization_barrier((pivot_product(2) + from_two, border))
    from_above = shift(above, -1)
    border_below = shift(border_sent, 1)
    near_sum = pivot_product(3) + from_below + from_above
    near_sum = near_sum.reshape(far, block, pivot_rows)
    far_id = lax.div(row_id, near)

    def far_block(offset):
        return lax.dynamic_index_in_dim(near_sum, lax.rem(far_id + offset, far), 0, keepdims=False)

    own = far_block(0)
    sent = [far_block(offset) for offset in range(1, far)]
    *sent, index, border_sent = lax.optimization_barrier((*sent, index, border_above))
    sent = [shift(value, near * (1 + hop), False) for hop, value in enumerate(sent)]
    border_two = shift(border_sent, -1)
    index = lax.all_gather(index, "front", axis=0)
    *sent, index = lax.optimization_barrier((*sent, index))
    for value in sent:
        own = own + value
    pivot_live = col_id * pivot_rows + jnp.arange(pivot_rows, dtype=jnp.int32) < front_sizes[0, 0]
    own = jnp.where(pivot_live[None, :], own, 0.0)

    apart = [[g + near * i for i in range(far)] for g in range(near)]
    solved = lax.all_gather(own, "row", axis_index_groups=apart, axis=0, tiled=True)
    window = (border, border_above, border_below, border_two)
    update = jnp.concatenate([contract(solved, value, (1,), (1,)) for value in window], 1)
    update = exchange(update.reshape(layer, part, near * border_rows), ("front", "col"))

    place = jnp.where(index < 0, -1, lax.div(index, high_count))
    high = lax.rem(index, high_count)
    landed = land(update, place, high, fronts, cols, low_count, high_count)
    landed = exchange(landed.reshape(rows, halves * part, high_count), "row")
    landed = landed.reshape(far, near, halves, part, high_count).sum(0)

    share = front_id * cols + col_id
    per_block = layer // far
    rhs_share = root_rhs.reshape(root_rows, far, near, per_block, part)
    rhs_share = lax.dynamic_index_in_dim(rhs_share, lax.div(share, per_block), 1, keepdims=False)
    rhs_share = lax.dynamic_index_in_dim(rhs_share, lax.rem(share, per_block), 2, keepdims=False)
    rhs_share = rhs_share.reshape(halves, high_count, near, part).transpose(2, 0, 3, 1)
    residual = rhs_share - landed
    residual = exchange(
        jnp.broadcast_to(residual[None], (layer, near, halves, part, high_count)), ("front", "col")
    )
    residual = residual.reshape(far, per_block, near // 2, 2, halves, part, high_count)
    residual = residual.transpose(3, 0, 2, 1, 5, 4, 6).reshape(sources, root_rows)

    root = contract(residual, root_inverse, (1,), (1,))
    root = row_sum(root.reshape(2, rows // 2, block, root_inverse.shape[0]))
    return own.T[None], root.T


def solution(mesh):
    in_specs = (
        P("front", ("row", "col"), None),
        P("front", "col", "row"),
        P("front", "row", "col"),
        P("front", None),
        P("front", None),
        P("row", None),
        P(("front", "col"), "row"),
    )
    out_specs = (P("front", "col", "row"), P(("front", "col"), "row"))
    return jax.shard_map(local, mesh=mesh, in_specs=in_specs, out_specs=out_specs, check_vma=False)
```

time: 259 us -> 238 us (0.919)
  the two profiles are of different devices: /device:TPU:2 before, /device:TPU:16 now
where the time goes in v5:
time: 238 us; the launch traced here: 237 us
  blocking collectives  88.7 us (37%)
  starting transfers between devices  70.6 us (30%)
  waiting for transfers between devices  55.2 us (23%)
  matrix products  8.29 us (3%)
  local copies, waits for them, and re-layouts  8.21 us (3%)
  other arithmetic  2.8 us (1%)
    ppermute x9, starting transfers between devices, shift(): return lax.ppermute(value, ('front', 'row'), pairs)  46.3 us
    all_gather x1, blocking collectives, local(): lax.all_gather(own, 'row', axis_index_groups=apart, axis=0, tiled=True)  39.1 us
    all_to_all x3, waiting for transfers between devices, exchange(): return lax.all_to_all(blocks, axes, split_axis=0, concat_axis=0, tiled=True)  38.7 us
    all_to_all x1, blocking collectives, row_sum(): mine = lax.all_to_all(mine, 'row', 0, 0, axis_index_groups=same, tiled=True)  24.9 us
    all_to_all x3, starting transfers between devices, exchange(): return lax.all_to_all(blocks, axes, split_axis=0, concat_axis=0, tiled=True)  20.8 us
    all_gather x1, blocking collectives, local(): index = lax.all_gather(index, 'front', axis=0)  13.2 us
    ppermute x9, waiting for transfers between devices, shift(): return lax.ppermute(value, ('front', 'row'), pairs)  11.8 us
    all_gather x1, blocking collectives, local(): rhs = lax.all_gather(rhs, 'col', axis=1, tiled=True)  11.6 us
  transfers between devices with their start and end apart: 13, of which 6 were waited for; matrix products, arithmetic and copies ran while one was open for 4% of the time, Pallas kernels for 0%

profile of v5, /device:TPU:16, one launch (start us, length us, event | category | flops | bytes accessed | tf_op | source)
XLA Modules:
  0.0 237.4 jit_solution(7052732409897729058)
XLA Ops:
  0.6 11.4 %collective-permute-start = (f32[256,1024]{1,0:T(8,128)}, f32[256,1024]{1,0:T(8,128)S(1)}, u32[]{:S(2)}, u32[]{:S(2)}) collective-permute-start(f32[256,1024]{1,0:T(8,128)} %bitcast.82), channel_id=1, source_target_pairs={{0,60},{4,0},{8,4},{12,8},{16,12},{20,16},{24,20},{28,24},{32,28},... | collective-permute-start | bytes 3145736 | tf_op jit(solution)/shard_map/ppermute | solution.py:106
  12.1 1.0 copy.16
  13.4 11.6 %all_gather.12 = f32[4,256,128]{2,0,1:T(4,128)S(1)} all-gather(f32[4,64,128]{2,0,1:T(4,128)S(1)} %copy.18), channel_id=1, replica_groups=mesh['front'=8,'row'=16,'col'=4] {'col'}, dimensions={1}, use_global_device_ids=true | all-gather | bytes 655360 | tf_op jit(solution)/shard_map/all_gather | solution.py:143
  24.9 0.4 fusion.16
  25.3 0.7 fusion.1
  26.1 5.2 %collective-permute-start.2 = (f32[128,1024]{1,0:T(8,128)S(1)}, f32[128,1024]{1,0:T(8,128)S(1)}, u32[]{:S(2)}, u32[]{:S(2)}) collective-permute-start(f32[128,1024]{1,0:T(8,128)S(1)} %fusion.1), channel_id=1, source_target_pairs={{0,60},{4,0},{8,4},{12,8},{16,12},{20,16},{24,20},{28,24},{32,28},... | collective-permute-start | bytes 1572872 | tf_op jit(solution)/shard_map/ppermute | solution.py:106
  31.4 0.7 constant_dynamic-slice_fusion.4
  32.1 0.6 fusion.17
  32.7 0.7 fusion.4
  33.4 1.9 collective-permute-start.1
  35.3 6.4 %collective-permute-done.2 = f32[128,1024]{1,0:T(8,128)S(1)} collective-permute-done((f32[128,1024]{1,0:T(8,128)S(1)}, f32[128,1024]{1,0:T(8,128)S(1)}, u32[]{:S(2)}, u32[]{:S(2)}) %collective-permute-start.2) | collective-permute-done | bytes 524320 | tf_op jit(solution)/shard_map/ppermute | solution.py:106
  41.7 0.7 convolution_add_fusion
  42.4 5.6 %collective-permute-start.3 = (f32[128,1024]{1,0:T(8,128)S(1)}, f32[128,1024]{1,0:T(8,128)S(1)}, u32[]{:S(2)}, u32[]{:S(2)}) collective-permute-start(f32[128,1024]{1,0:T(8,128)S(1)} %convolution_add_fusion), channel_id=1, source_target_pairs={{0,60},{4,0},{8,4},{12,8},{16,12},{20,16},{24,20},{28,24},{32,28},... | collective-permute-start | bytes 1572872 | tf_op jit(solution)/shard_map/ppermute | solution.py:106
  48.1 0.7 compare_select_fusion
  48.7 0.7 compare_select_fusion.2
  49.4 5.3 %collective-permute-done.3 = f32[128,1024]{1,0:T(8,128)S(1)} collective-permute-done((f32[128,1024]{1,0:T(8,128)S(1)}, f32[128,1024]{1,0:T(8,128)S(1)}, u32[]{:S(2)}, u32[]{:S(2)}) %collective-permute-start.3) | collective-permute-done | bytes 524320 | tf_op jit(solution)/shard_map/ppermute | solution.py:106
  54.7 0.7 fusion
  55.5 1.9 collective-permute-start.4
  57.4 10.4 %collective-permute-start.5 = (f32[32,1024]{1,0:T(8,128)S(1)}, f32[32,1024]{1,0:T(8,128)S(1)}, u32[]{:S(2)}, u32[]{:S(2)}) collective-permute-start(f32[32,1024]{1,0:T(8,128)S(1)} %get-tuple-element.19), channel_id=1, source_target_pairs={{0,32},{4,36},{8,40},{12,44},{16,48},{20,52},{24,56},{28,60},{32,0... | collective-permute-start | bytes 393224 | tf_op jit(solution)/shard_map/ppermute | solution.py:106
  67.8 2.7 %collective-permute-start.6 = (f32[32,1024]{1,0:T(8,128)S(1)}, f32[32,1024]{1,0:T(8,128)S(1)}, u32[]{:S(2)}, u32[]{:S(2)}) collective-permute-start(f32[32,1024]{1,0:T(8,128)S(1)} %get-tuple-element.20), channel_id=1, source_target_pairs={{0,48},{4,52},{8,56},{12,60},{16,0},{20,4},{24,8},{28,12},{32,16},... | collective-permute-start | bytes 393224 | tf_op jit(solution)/shard_map/ppermute | solution.py:106
  70.5 3.1 %collective-permute-start.7 = (f32[256,1024]{1,0:T(8,128)S(1)}, f32[256,1024]{1,0:T(8,128)}, u32[]{:S(2)}, u32[]{:S(2)}) collective-permute-start(f32[256,1024]{1,0:T(8,128)S(1)} %bitcast.83), channel_id=1, source_target_pairs={{0,4},{4,8},{8,12},{12,16},{16,20},{20,24},{24,28},{28,32},{32,36}... | collective-permute-start | bytes 3145736 | tf_op jit(solution)/shard_map/ppermute | solution.py:106
  73.6 0.7 add_compare_fusion
  74.3 13.2 %all-gather = s32[8192]{0:T(1024)S(1)} all-gather(s32[1024]{0:T(1024)S(1)} %pad_add_fusion), channel_id=2, replica_groups=mesh['front'=8,'row'=16,'col'=4] {'front'}, dimensions={0}, use_global_device_ids=true | all-gather | bytes 36864 | tf_op jit(solution)/shard_map/all_gather | solution.py:166
  87.5 4.1 %collective-permute-start.8 = (f32[256,1024]{1,0:T(8,128)}, f32[256,1024]{1,0:T(8,128)S(1)}, u32[]{:S(2)}, u32[]{:S(2)}) collective-permute-start(f32[256,1024]{1,0:T(8,128)} %copy-done.3), channel_id=1, source_target_pairs={{0,60},{4,0},{8,4},{12,8},{16,12},{20,16},{24,20},{28,24},{32,28},... | collective-permute-start | bytes 3145736 | tf_op jit(solution)/shard_map/ppermute | solution.py:106
  91.7 39.1 %all_gather.15 = f32[128,1024]{1,0:T(8,128)S(1)} all-gather(f32[32,1024]{1,0:T(8,128)S(1)} %fusion.11), channel_id=1, replica_groups={{0,16,32,48},{4,20,36,52},{8,24,40,56},{12,28,44,60},{1,17,33,49},{5,21..., dimensions={0}, use_global_device_ids=true | all-gather | bytes 655360 | tf_op jit(solution)/shard_map/all_gather | solution.py:174
  130.7 0.7 fusion.18
  131.4 0.7 fusion.14
  132.1 1.9 fusion.19
  134.0 0.7 fusion.20
  134.7 1.0 reshape.49
  135.6 8.0 %all-to-all-start = ((f32[32,4,1024]{2,1,0:T(4,128)}), f32[32,4,1024]{2,1,0:T(4,128)S(1)}, u32[]{:S(2)}, u32[]{:S(2)}) async-start(f32[32,4,1024]{2,1,0:T(4,128)} %reshape.49), calls=%async_computation | async-start | bytes 1048576 | tf_op jit(solution)/shard_map/all_to_all | solution.py:24
  143.8 9.6 %all-to-all-done.update_ref = f32[32,4,1024]{2,1,0:T(4,128)S(1)} async-done(((f32[32,4,1024]{2,1,0:T(4,128)}), f32[32,4,1024]{2,1,0:T(4,128)S(1)}, u32[]{:S(2)}, u32[]{:S(2)}) %all-to-all-start) | async-done | bytes 524320 | tf_op jit(solution)/shard_map/all_to_all | solution.py:24
  153.4 2.3 shard_map.86
  155.6 6.8 %all-to-all-start.1 = ((f32[16,8,256]{2,1,0:T(8,128)}), f32[16,8,256]{2,1,0:T(8,128)S(1)}, u32[]{:S(2)}, u32[]{:S(2)}) async-start(f32[16,8,256]{2,1,0:T(8,128)} %bitcast.25), calls=%async_computation.1 | async-start | bytes 262144 | tf_op jit(solution)/shard_map/all_to_all | solution.py:24
  162.5 0.3 copy.19
  162.8 0.3 reshape.47
  163.1 13.7 %all-to-all-done.1 = f32[16,8,256]{2,1,0:T(8,128)S(1)} async-done(((f32[16,8,256]{2,1,0:T(8,128)}), f32[16,8,256]{2,1,0:T(8,128)S(1)}, u32[]{:S(2)}, u32[]{:S(2)}) %all-to-all-start.1) | async-done | bytes 131104 | tf_op jit(solution)/shard_map/all_to_all | solution.py:24
  177.0 1.2 broadcast_in_dim.46
  178.2 6.0 %all-to-all-start.2 = ((f32[32,4,2,4,256]{4,3,2,1,0:T(4,128)}), f32[32,4,2,4,256]{4,3,2,1,0:T(4,128)S(1)}, u32[]{:S(2)}, u32[]{:S(2)}) async-start(f32[32,4,2,4,256]{4,3,2,1,0:T(4,128)} %broadcast_in_dim.46), calls=%async_computation.2 | async-start | bytes 2097152 | tf_op jit(solution)/shard_map/all_to_all | solution.py:24
  184.2 15.3 %all-to-all-done.2 = f32[32,4,2,4,256]{4,3,2,1,0:T(4,128)S(1)} async-done(((f32[32,4,2,4,256]{4,3,2,1,0:T(4,128)}), f32[32,4,2,4,256]{4,3,2,1,0:T(4,128)S(1)}, u32[]{:S(2)}, u32[]{:S(2)}) %all-to-all-start.2) | async-done | bytes 1048608 | tf_op jit(solution)/shard_map/all_to_all | solution.py:24
  199.6 0.6 copy.22
  200.2 0.8 copy.23
  201.0 0.8 dot_general.37
  201.8 1.7 fusion.7
  203.5 3.5 %collective-permute-start.9 = (f32[8,32,256]{2,1,0:T(8,128)S(1)}, f32[8,32,256]{2,1,0:T(8,128)S(1)}, u32[]{:S(2)}, u32[]{:S(2)}) collective-permute-start(f32[8,32,256]{2,1,0:T(8,128)S(1)} %dynamic-slice_bitcast_fusion), channel_id=1, source_target_pairs={{0,4},{4,0},{8,12},{12,8},{16,20},{20,16},{24,28},{28,24},{32,36},... | collective-permute-start | bytes 786440 | tf_op jit(solution)/shard_map/ppermute | solution.py:118
  207.0 4.8 %collective-permute-done.9 = f32[8,32,256]{2,1,0:T(8,128)S(1)} collective-permute-done((f32[8,32,256]{2,1,0:T(8,128)S(1)}, f32[8,32,256]{2,1,0:T(8,128)S(1)}, u32[]{:S(2)}, u32[]{:S(2)}) %collective-permute-start.9) | collective-permute-done | bytes 262176 | tf_op jit(solution)/shard_map/ppermute | solution.py:118
  211.8 24.9 %all_to_all.20 = f32[8,32,256]{2,1,0:T(8,128)S(1)} all-to-all(f32[8,32,256]{2,1,0:T(8,128)S(1)} %bitcast_add_fusion), channel_id=1, replica_groups={{0,8,16,24,32,40,48,56},{4,12,20,28,36,44,52,60},{1,9,17,25,33,41,49,57..., dimensions={0} | all-to-all | bytes 524288 | tf_op jit(solution)/shard_map/all_to_all | solution.py:120
  236.8 0.6 reduce_sum.19
  (39 shorter events, 0.6 us)
Async XLA Ops:
  0.6 24.7 %copy-start = (f32[1,1024,256]{2,1,0:T(8,128)S(1)}, f32[1,1024,256]{2,1,0:T(8,128)}, u32[]{:S(2)}) copy-start(f32[1,1024,256]{2,1,0:T(8,128)} %param.8) | copy-start | bytes 3145732
  0.6 24.3 %collective-permute-start = (f32[256,1024]{1,0:T(8,128)}, f32[256,1024]{1,0:T(8,128)S(1)}, u32[]{:S(2)}, u32[]{:S(2)}) collective-permute-start(f32[256,1024]{1,0:T(8,128)} %bitcast.82), channel_id=1, source_target_pairs={{0,60},{4,0},{8,4},{12,8},{16,12},{20,16},{24,20},{28,24},{32,28},... | collective-permute-start | bytes 3145736 | tf_op jit(solution)/shard_map/ppermute | solution.py:106
  24.9 1.1 copy-start.3
  26.1 15.7 %collective-permute-start.2 = (f32[128,1024]{1,0:T(8,128)S(1)}, f32[128,1024]{1,0:T(8,128)S(1)}, u32[]{:S(2)}, u32[]{:S(2)}) collective-permute-start(f32[128,1024]{1,0:T(8,128)S(1)} %fusion.1), channel_id=1, source_target_pairs={{0,60},{4,0},{8,4},{12,8},{16,12},{20,16},{24,20},{28,24},{32,28},... | collective-permute-start | bytes 1572872 | tf_op jit(solution)/shard_map/ppermute | solution.py:106
  31.4 0.8 copy-start.6
  33.4 16.0 %collective-permute-start.1 = (f32[128,1024]{1,0:T(8,128)S(1)}, f32[128,1024]{1,0:T(8,128)S(1)}, u32[]{:S(2)}, u32[]{:S(2)}) collective-permute-start(f32[128,1024]{1,0:T(8,128)S(1)} %fusion.4), channel_id=1, source_target_pairs={{0,4},{4,8},{8,12},{12,16},{16,20},{20,24},{24,28},{28,32},{32,36}... | collective-permute-start | bytes 1572872 | tf_op jit(solution)/shard_map/ppermute | solution.py:106
  42.4 12.3 %collective-permute-start.3 = (f32[128,1024]{1,0:T(8,128)S(1)}, f32[128,1024]{1,0:T(8,128)S(1)}, u32[]{:S(2)}, u32[]{:S(2)}) collective-permute-start(f32[128,1024]{1,0:T(8,128)S(1)} %convolution_add_fusion), channel_id=1, source_target_pairs={{0,60},{4,0},{8,4},{12,8},{16,12},{20,16},{24,20},{28,24},{32,28},... | collective-permute-start | bytes 1572872 | tf_op jit(solution)/shard_map/ppermute | solution.py:106
  54.7 15.8 %copy-start.2 = (f32[1,256,1024]{2,1,0:T(8,128)S(1)}, f32[1,256,1024]{2,1,0:T(8,128)}, u32[]{:S(2)}) copy-start(f32[1,256,1024]{2,1,0:T(8,128)} %param.9) | copy-start | bytes 3145732
  55.5 36.1 %collective-permute-start.4 = (f32[32,1024]{1,0:T(8,128)S(1)}, f32[32,1024]{1,0:T(8,128)S(1)}, u32[]{:S(2)}, u32[]{:S(2)}) collective-permute-start(f32[32,1024]{1,0:T(8,128)S(1)} %get-tuple-element.18), channel_id=1, source_target_pairs={{0,16},{4,20},{8,24},{12,28},{16,32},{20,36},{24,40},{28,44},{32,4... | collective-permute-start | bytes 393224 | tf_op jit(solution)/shard_map/ppermute | solution.py:106
  57.4 34.2 %collective-permute-start.5 = (f32[32,1024]{1,0:T(8,128)S(1)}, f32[32,1024]{1,0:T(8,128)S(1)}, u32[]{:S(2)}, u32[]{:S(2)}) collective-permute-start(f32[32,1024]{1,0:T(8,128)S(1)} %get-tuple-element.19), channel_id=1, source_target_pairs={{0,32},{4,36},{8,40},{12,44},{16,48},{20,52},{24,56},{28,60},{32,0... | collective-permute-start | bytes 393224 | tf_op jit(solution)/shard_map/ppermute | solution.py:106
  67.8 23.8 %collective-permute-start.6 = (f32[32,1024]{1,0:T(8,128)S(1)}, f32[32,1024]{1,0:T(8,128)S(1)}, u32[]{:S(2)}, u32[]{:S(2)}) collective-permute-start(f32[32,1024]{1,0:T(8,128)S(1)} %get-tuple-element.20), channel_id=1, source_target_pairs={{0,48},{4,52},{8,56},{12,60},{16,0},{20,4},{24,8},{28,12},{32,16},... | collective-permute-start | bytes 393224 | tf_op jit(solution)/shard_map/ppermute | solution.py:106
  70.5 61.5 %collective-permute-start.7 = (f32[256,1024]{1,0:T(8,128)S(1)}, f32[256,1024]{1,0:T(8,128)}, u32[]{:S(2)}, u32[]{:S(2)}) collective-permute-start(f32[256,1024]{1,0:T(8,128)S(1)} %bitcast.83), channel_id=1, source_target_pairs={{0,4},{4,8},{8,12},{12,16},{16,20},{20,24},{24,28},{28,32},{32,36}... | collective-permute-start | bytes 3145736 | tf_op jit(solution)/shard_map/ppermute | solution.py:106
  87.5 43.2 %copy-start.4 = (f32[256,1024]{1,0:T(8,128)S(1)}, f32[256,1024]{1,0:T(8,128)}, u32[]{:S(2)}) copy-start(f32[256,1024]{1,0:T(8,128)} %copy-done.3) | copy-start | bytes 3145732
  87.5 46.5 %collective-permute-start.8 = (f32[256,1024]{1,0:T(8,128)}, f32[256,1024]{1,0:T(8,128)S(1)}, u32[]{:S(2)}, u32[]{:S(2)}) collective-permute-start(f32[256,1024]{1,0:T(8,128)} %copy-done.3), channel_id=1, source_target_pairs={{0,60},{4,0},{8,4},{12,8},{16,12},{20,16},{24,20},{28,24},{32,28},... | collective-permute-start | bytes 3145736 | tf_op jit(solution)/shard_map/ppermute | solution.py:106
  91.6 39.1 %copy-start.5 = (f32[32,1024]{1,0:T(8,128)}, f32[32,1024]{1,0:T(8,128)S(1)}, u32[]{:S(2)}) copy-start(f32[32,1024]{1,0:T(8,128)S(1)} %fusion.11) | copy-start | bytes 393220
  135.6 17.7 %all-to-all-start = ((f32[32,4,1024]{2,1,0:T(4,128)}), f32[32,4,1024]{2,1,0:T(4,128)S(1)}, u32[]{:S(2)}, u32[]{:S(2)}) async-start(f32[32,4,1024]{2,1,0:T(4,128)} %reshape.49), calls=%async_computation | async-start | bytes 1048576 | tf_op jit(solution)/shard_map/all_to_all | solution.py:24
  143.8 18.7 %copy-start.1 = (f32[512,512]{1,0:T(8,128)S(1)}, f32[512,512]{1,0:T(8,128)}, u32[]{:S(2)}) copy-start(f32[512,512]{1,0:T(8,128)} %param.12) | copy-start | bytes 3145732
  155.6 21.2 %all-to-all-start.1 = ((f32[16,8,256]{2,1,0:T(8,128)}), f32[16,8,256]{2,1,0:T(8,128)S(1)}, u32[]{:S(2)}, u32[]{:S(2)}) async-start(f32[16,8,256]{2,1,0:T(8,128)} %bitcast.25), calls=%async_computation.1 | async-start | bytes 262144 | tf_op jit(solution)/shard_map/all_to_all | solution.py:24
  178.2 21.3 %all-to-all-start.2 = ((f32[32,4,2,4,256]{4,3,2,1,0:T(4,128)}), f32[32,4,2,4,256]{4,3,2,1,0:T(4,128)S(1)}, u32[]{:S(2)}, u32[]{:S(2)}) async-start(f32[32,4,2,4,256]{4,3,2,1,0:T(4,128)} %broadcast_in_dim.46), calls=%async_computation.2 | async-start | bytes 2097152 | tf_op jit(solution)/shard_map/all_to_all | solution.py:24
  203.5 8.3 %collective-permute-start.9 = (f32[8,32,256]{2,1,0:T(8,128)S(1)}, f32[8,32,256]{2,1,0:T(8,128)S(1)}, u32[]{:S(2)}, u32[]{:S(2)}) collective-permute-start(f32[8,32,256]{2,1,0:T(8,128)S(1)} %dynamic-slice_bitcast_fusion), channel_id=1, source_target_pairs={{0,4},{4,0},{8,12},{12,8},{16,20},{20,16},{24,28},{28,24},{32,36},... | collective-permute-start | bytes 786440 | tf_op jit(solution)/shard_map/ppermute | solution.py:118

commit v6 on v5

--- a/solution.py
+++ b/solution.py
@@ -105,21 +105,6 @@
             pairs += [(front * rows + z, front * rows + (z + by) % rows) for z in range(rows)]
         return lax.ppermute(value, ("front", "row"), pairs)
 
-    def row_sum(blocks):
-        parity = lax.rem(row_id, 2)
-        pairs = []
-        for front in range(fronts):
-            by = front % 2
-            pairs += [
-                (front * rows + z, front * rows + (((z + by) ^ 1) - by) % rows) for z in range(rows)
-            ]
-        theirs = lax.dynamic_index_in_dim(blocks, 1 - parity, 0, keepdims=False)
-        mine = lax.dynamic_index_in_dim(blocks, parity, 0, keepdims=False)
-        mine = mine + lax.ppermute(theirs, ("front", "row"), pairs)
-        same = [list(range(first, rows, 2)) for first in (0, 1)]
-        mine = lax.all_to_all(mine, "row", 0, 0, axis_index_groups=same, tiled=True)
-        return mine.sum(0)
-
     def group_at(offset):
         return lax.rem(row_id + offset + near, near)
 
@@ -140,17 +125,18 @@
         ]
     )
     border_above = shift(border, -1)
+    border_below = shift(border, 1)
     rhs = lax.all_gather(rhs, "col", axis=1, tiled=True)
-    rhs, border_above = lax.optimization_barrier((rhs, border_above))
 
     def pivot_product(which):
         return contract(rhs[which], inverse, (0,), (1,))
 
     from_two = shift(pivot_product(0), -1)
     from_below = shift(pivot_product(1), 1)
-    above, border_sent = lax.optimization_barrier((pivot_product(2) + from_two, border))
-    from_above = shift(above, -1)
-    border_below = shift(border_sent, 1)
+    from_two, border_above, border_below = lax.optimization_barrier(
+        (from_two, border_above, border_below)
+    )
+    from_above = shift(pivot_product(2) + from_two, -1)
     near_sum = pivot_product(3) + from_below + from_above
     near_sum = near_sum.reshape(far, block, pivot_rows)
     far_id = lax.div(row_id, near)
@@ -174,29 +160,53 @@
     solved = lax.all_gather(own, "row", axis_index_groups=apart, axis=0, tiled=True)
     window = (border, border_above, border_below, border_two)
     update = jnp.concatenate([contract(solved, value, (1,), (1,)) for value in window], 1)
+
+    share = front_id * cols + col_id
+    per_block = layer // far
+    root_share = root_rhs.reshape(root_rows, far, near, per_block, part)
+    root_share = lax.dynamic_index_in_dim(root_share, lax.div(share, per_block), 1, keepdims=False)
+    root_share = lax.dynamic_index_in_dim(root_share, lax.rem(share, per_block), 2, keepdims=False)
+    root_share = root_share.transpose(1, 2, 0)
+
+    def share_of(offset):
+        return lax.dynamic_index_in_dim(root_share, group_at(offset), 0, keepdims=False)
+
+    share_rows = root_inverse.shape[0]
+    upward = jnp.concatenate([root_inverse, share_of(-1), share_of(-2)])
+    downward = jnp.concatenate([root_inverse, share_of(1), share_of(1)])
+    update, upward, downward = lax.optimization_barrier((update, upward, downward))
     update = exchange(update.reshape(layer, part, near * border_rows), ("front", "col"))
-
-    place = jnp.where(index < 0, -1, lax.div(index, high_count))
+    upward = shift(upward, -1, False)
+    downward = shift(downward, 1, False)
+
+    low = lax.div(jnp.maximum(index, 0), high_count)
+    owner = lax.rem(lax.div(low, halves) - lax.rem(row_id, near) + 1 + rows, rows)
+    place = jnp.where(index < 0, -1, owner * halves + lax.rem(low, halves))
     high = lax.rem(index, high_count)
     landed = land(update, place, high, fronts, cols, low_count, high_count)
-    landed = exchange(landed.reshape(rows, halves * part, high_count), "row")
-    landed = landed.reshape(far, near, halves, part, high_count).sum(0)
-
-    share = front_id * cols + col_id
-    per_block = layer // far
-    rhs_share = root_rhs.reshape(root_rows, far, near, per_block, part)
-    rhs_share = lax.dynamic_index_in_dim(rhs_share, lax.div(share, per_block), 1, keepdims=False)
-    rhs_share = lax.dynamic_index_in_dim(rhs_share, lax.rem(share, per_block), 2, keepdims=False)
-    rhs_share = rhs_share.reshape(halves, high_count, near, part).transpose(2, 0, 3, 1)
-    residual = rhs_share - landed
+    landed = landed.reshape(far, near * halves * part, high_count)
+    landed = lax.all_to_all(landed, "row", 0, 0, axis_index_groups=apart, tiled=True).sum(0)
+    landed = landed.reshape(near, halves, part, high_count)
+
+    twice = shift(upward, -1, False)
+    shares = jnp.stack(
+        [
+            downward[share_rows : share_rows + part],
+            share_of(0),
+            upward[share_rows : share_rows + part],
+            twice[share_rows + part :],
+        ]
+    )
+    residual = shares.reshape(near, part, halves, high_count).transpose(0, 2, 1, 3) - landed
     residual = exchange(
         jnp.broadcast_to(residual[None], (layer, near, halves, part, high_count)), ("front", "col")
     )
-    residual = residual.reshape(far, per_block, near // 2, 2, halves, part, high_count)
-    residual = residual.transpose(3, 0, 2, 1, 5, 4, 6).reshape(sources, root_rows)
-
-    root = contract(residual, root_inverse, (1,), (1,))
-    root = row_sum(root.reshape(2, rows // 2, block, root_inverse.shape[0]))
+    residual = residual.transpose(1, 0, 3, 2, 4).reshape(near, far * block, root_rows)
+
+    window = (downward[:share_rows], root_inverse, upward[:share_rows], twice[:share_rows])
+    root = sum(contract(residual[i], value, (1,), (1,)) for i, value in enumerate(window))
+    root = root.reshape(far, block, share_rows)
+    root = lax.all_to_all(root, "row", 0, 0, axis_index_groups=apart, tiled=True).sum(0)
     return own.T[None], root.T
 
 

time: 238 us -> 231 us (0.971)
  the two profiles are of different devices: /device:TPU:16 before, /device:TPU:32 now
where the time goes in v6:
time: 231 us; the launch traced here: 230 us
  blocking collectives  97.7 us (42%)
  starting transfers between devices  74.7 us (32%)
  waiting for transfers between devices  28.2 us (12%)
  matrix products  13.6 us (6%)
  local copies, waits for them, and re-layouts  7.76 us (3%)
  other arithmetic  4.71 us (2%)
    ppermute x12, starting transfers between devices, shift(): return lax.ppermute(value, ('front', 'row'), pairs)  60.8 us
    all_gather x1, blocking collectives, local(): lax.all_gather(own, 'row', axis_index_groups=apart, axis=0, tiled=True)  33 us
    all_to_all x1, blocking collectives, exchange(): return lax.all_to_all(blocks, axes, split_axis=0, concat_axis=0, tiled=True)  20.7 us
    all_to_all x1, blocking collectives, local(): lax.all_to_all(root, 'row', 0, 0, axis_index_groups=apart, tiled=True)  17.7 us
    dot_general x12, matrix products, contract(): lax.dot_general(left, right, ((left_dims, right_dims), ((), ())), precisi...  13.6 us
    all_gather x1, blocking collectives, local(): index = lax.all_gather(index, 'front', axis=0)  13.2 us
    all_gather x1, blocking collectives, local(): rhs = lax.all_gather(rhs, 'col', axis=1, tiled=True)  13.1 us
    all_to_all x1, waiting for transfers between devices, local(): lax.all_to_all(landed, 'row', 0, 0, axis_index_groups=apart, tiled=True)  12.1 us
  transfers between devices with their start and end apart: 14, of which 4 were waited for; matrix products, arithmetic and copies ran while one was open for 8% of the time, Pallas kernels for 1%

profile of v6, /device:TPU:32, one launch (start us, length us, event | category | flops | bytes accessed | tf_op | source)
XLA Modules:
  0.0 230.3 jit_solution(10092171237822814452)
XLA Ops:
  0.6 4.0 %collective-permute-start.3 = (f32[256,1024]{1,0:T(8,128)}, f32[256,1024]{1,0:T(8,128)}, u32[]{:S(2)}, u32[]{:S(2)}) collective-permute-start(f32[256,1024]{1,0:T(8,128)} %bitcast.121), channel_id=1, source_target_pairs={{0,4},{4,8},{8,12},{12,16},{16,20},{20,24},{24,28},{28,32},{32,36}... | collective-permute-start | bytes 3145736 | tf_op jit(solution)/shard_map/ppermute | solution.py:106
  4.6 5.5 %collective-permute-start.2 = (f32[256,1024]{1,0:T(8,128)}, f32[256,1024]{1,0:T(8,128)}, u32[]{:S(2)}, u32[]{:S(2)}) collective-permute-start(f32[256,1024]{1,0:T(8,128)} %bitcast.122), channel_id=1, source_target_pairs={{0,60},{4,0},{8,4},{12,8},{16,12},{20,16},{24,20},{28,24},{32,28},... | collective-permute-start | bytes 3145736 | tf_op jit(solution)/shard_map/ppermute | solution.py:106
  10.1 1.0 copy.20
  11.4 13.1 %all_gather.12 = f32[4,256,128]{2,0,1:T(4,128)S(1)} all-gather(f32[4,64,128]{2,0,1:T(4,128)S(1)} %copy.22), channel_id=1, replica_groups=mesh['front'=8,'row'=16,'col'=4] {'col'}, dimensions={1}, use_global_device_ids=true | all-gather | bytes 655360 | tf_op jit(solution)/shard_map/all_gather | solution.py:129
  24.9 0.7 fusion.2
  25.6 6.1 %collective-permute-start.1 = (f32[128,1024]{1,0:T(8,128)S(1)}, f32[128,1024]{1,0:T(8,128)S(1)}, u32[]{:S(2)}, u32[]{:S(2)}) collective-permute-start(f32[128,1024]{1,0:T(8,128)S(1)} %fusion.2), channel_id=1, source_target_pairs={{0,60},{4,0},{8,4},{12,8},{16,12},{20,16},{24,20},{28,24},{32,28},... | collective-permute-start | bytes 1572872 | tf_op jit(solution)/shard_map/ppermute | solution.py:106
  31.7 1.5 fusion.6
  33.2 1.9 collective-permute-start
  35.2 0.7 constant_dynamic-slice_fusion.4
  35.9 0.6 fusion.29
  36.5 0.7 fusion.4
  37.2 5.5 %collective-permute-done.1 = f32[128,1024]{1,0:T(8,128)S(1)} collective-permute-done((f32[128,1024]{1,0:T(8,128)S(1)}, f32[128,1024]{1,0:T(8,128)S(1)}, u32[]{:S(2)}, u32[]{:S(2)}) %collective-permute-start.1) | collective-permute-done | bytes 524320 | tf_op jit(solution)/shard_map/ppermute | solution.py:106
  42.7 0.9 add.240
  43.6 4.4 %collective-permute-start.4 = (f32[128,1024]{1,0:T(8,128)}, f32[128,1024]{1,0:T(8,128)}, u32[]{:S(2)}, u32[]{:S(2)}) collective-permute-start(f32[128,1024]{1,0:T(8,128)} %add.240), channel_id=1, source_target_pairs={{0,60},{4,0},{8,4},{12,8},{16,12},{20,16},{24,20},{28,24},{32,28},... | collective-permute-start | bytes 1572872 | tf_op jit(solution)/shard_map/ppermute | solution.py:106
  48.0 0.7 compare_select_fusion.2
  49.4 0.7 compare_select_fusion
  50.1 4.8 %collective-permute-done.4 = f32[128,1024]{1,0:T(8,128)} collective-permute-done((f32[128,1024]{1,0:T(8,128)}, f32[128,1024]{1,0:T(8,128)}, u32[]{:S(2)}, u32[]{:S(2)}) %collective-permute-start.4) | collective-permute-done | bytes 524320 | tf_op jit(solution)/shard_map/ppermute | solution.py:106
  55.0 1.9 fusion
  56.9 0.7 dynamic-slice_bitcast_fusion
  57.6 3.5 %collective-permute-start.5 = (f32[32,1024]{1,0:T(8,128)}, f32[32,1024]{1,0:T(8,128)S(1)}, u32[]{:S(2)}, u32[]{:S(2)}) collective-permute-start(f32[32,1024]{1,0:T(8,128)} %get-tuple-element.19), channel_id=1, source_target_pairs={{0,16},{4,20},{8,24},{12,28},{16,32},{20,36},{24,40},{28,44},{32,4... | collective-permute-start | bytes 393224 | tf_op jit(solution)/shard_map/ppermute | solution.py:106
  61.1 11.4 %collective-permute-start.6 = (f32[32,1024]{1,0:T(8,128)}, f32[32,1024]{1,0:T(8,128)}, u32[]{:S(2)}, u32[]{:S(2)}) collective-permute-start(f32[32,1024]{1,0:T(8,128)} %get-tuple-element.20), channel_id=1, source_target_pairs={{0,32},{4,36},{8,40},{12,44},{16,48},{20,52},{24,56},{28,60},{32,0... | collective-permute-start | bytes 393224 | tf_op jit(solution)/shard_map/ppermute | solution.py:106
  72.6 5.5 %collective-permute-start.7 = (f32[32,1024]{1,0:T(8,128)S(1)}, f32[32,1024]{1,0:T(8,128)}, u32[]{:S(2)}, u32[]{:S(2)}) collective-permute-start(f32[32,1024]{1,0:T(8,128)S(1)} %get-tuple-element.21), channel_id=1, source_target_pairs={{0,48},{4,52},{8,56},{12,60},{16,0},{20,4},{24,8},{28,12},{32,16},... | collective-permute-start | bytes 393224 | tf_op jit(solution)/shard_map/ppermute | solution.py:106
  78.2 0.7 add_compare_fusion
  78.9 13.2 %all-gather = s32[8192]{0:T(1024)S(1)} all-gather(s32[1024]{0:T(1024)S(1)} %pad_add_fusion), channel_id=2, replica_groups=mesh['front'=8,'row'=16,'col'=4] {'front'}, dimensions={0}, use_global_device_ids=true | all-gather | bytes 36864 | tf_op jit(solution)/shard_map/all_gather | solution.py:152
  92.1 4.4 %collective-permute-start.8 = (f32[256,1024]{1,0:T(8,128)}, f32[256,1024]{1,0:T(8,128)S(1)}, u32[]{:S(2)}, u32[]{:S(2)}) collective-permute-start(f32[256,1024]{1,0:T(8,128)} %collective-permute-done.2), channel_id=1, source_target_pairs={{0,60},{4,0},{8,4},{12,8},{16,12},{20,16},{24,20},{28,24},{32,28},... | collective-permute-start | bytes 3145736 | tf_op jit(solution)/shard_map/ppermute | solution.py:106
  96.5 1.0 fusion.15
  97.6 33.0 %all_gather.15 = f32[128,1024]{1,0:T(8,128)S(1)} all-gather(f32[32,1024]{1,0:T(8,128)S(1)} %fusion.15), channel_id=1, replica_groups={{0,16,32,48},{4,20,36,52},{8,24,40,56},{12,28,44,60},{1,17,33,49},{5,21..., dimensions={0}, use_global_device_ids=true | all-gather | bytes 655360 | tf_op jit(solution)/shard_map/all_gather | solution.py:160
  130.6 1.9 fusion.30
  132.5 0.7 fusion.25
  133.2 1.9 fusion.31
  135.1 0.7 fusion.32
  135.8 8.3 %collective-permute-start.10 = (f32[264,512]{1,0:T(8,128)S(1)}, f32[264,512]{1,0:T(8,128)}, u32[]{:S(2)}, u32[]{:S(2)}) collective-permute-start(f32[264,512]{1,0:T(8,128)S(1)} %get-tuple-element.29), channel_id=1, source_target_pairs={{0,60},{4,0},{8,4},{12,8},{16,12},{20,16},{24,20},{28,24},{32,28},... | collective-permute-start | bytes 1622024 | tf_op jit(solution)/shard_map/ppermute | solution.py:106
  144.0 1.0 reshape.73
  145.0 7.3 %all-to-all-start = ((f32[32,4,1024]{2,1,0:T(4,128)}), f32[32,4,1024]{2,1,0:T(4,128)S(1)}, u32[]{:S(2)}, u32[]{:S(2)}) async-start(f32[32,4,1024]{2,1,0:T(4,128)} %reshape.73), calls=%async_computation | async-start | bytes 1048576 | tf_op jit(solution)/shard_map/all_to_all | solution.py:24
  152.2 1.9 collective-permute-start.9
  154.2 3.9 %collective-permute-start.11 = (f32[264,512]{1,0:T(8,128)}, f32[264,512]{1,0:T(8,128)S(1)}, u32[]{:S(2)}, u32[]{:S(2)}) collective-permute-start(f32[264,512]{1,0:T(8,128)} %collective-permute-done.10), channel_id=1, source_target_pairs={{0,60},{4,0},{8,4},{12,8},{16,12},{20,16},{24,20},{28,24},{32,28},... | collective-permute-start | bytes 1622024 | tf_op jit(solution)/shard_map/ppermute | solution.py:106
  158.2 5.8 %all-to-all-done.update_ref = f32[32,4,1024]{2,1,0:T(4,128)S(1)} async-done(((f32[32,4,1024]{2,1,0:T(4,128)}), f32[32,4,1024]{2,1,0:T(4,128)S(1)}, u32[]{:S(2)}, u32[]{:S(2)}) %all-to-all-start) | async-done | bytes 524320 | tf_op jit(solution)/shard_map/all_to_all | solution.py:24
  164.0 2.3 shard_map.86
  166.3 6.7 %all-to-all-start.1 = ((f32[4,32,256]{2,1,0:T(8,128)}), f32[4,32,256]{2,1,0:T(8,128)S(1)}, u32[]{:S(2)}, u32[]{:S(2)}) async-start(f32[4,32,256]{2,1,0:T(8,128)} %bitcast.39), calls=%async_computation.1 | async-start | bytes 262144 | tf_op jit(solution)/shard_map/all_to_all | solution.py:188
  173.0 0.7 slice.76
  173.7 0.7 slice.75
  174.4 12.1 %all-to-all-done.1 = f32[4,32,256]{2,1,0:T(8,128)S(1)} async-done(((f32[4,32,256]{2,1,0:T(8,128)}), f32[4,32,256]{2,1,0:T(8,128)S(1)}, u32[]{:S(2)}, u32[]{:S(2)}) %all-to-all-start.1) | async-done | bytes 131104 | tf_op jit(solution)/shard_map/all_to_all | solution.py:188
  186.6 0.5 broadcast_in_dim.46
  187.1 20.7 %all_to_all.20 = f32[32,4,2,4,256]{4,2,3,1,0:T(2,128)S(1)} all-to-all(f32[32,4,2,4,256]{4,2,3,1,0:T(2,128)S(1)} %broadcast_in_dim.46), channel_id=1, replica_groups=mesh['front'=8,'row'=16,'col'=4] {'front','col'}, dimensions={0} | all-to-all | bytes 2097152 | tf_op jit(solution)/shard_map/all_to_all | solution.py:24
  208.7 1.4 fusion.10
  210.2 1.5 fusion.1
  212.0 17.7 %all_to_all.21 = f32[4,32,256]{2,1,0:T(8,128)S(1)} all-to-all(f32[4,32,256]{2,1,0:T(8,128)S(1)} %bitcast.130), channel_id=1, replica_groups={{0,16,32,48},{4,20,36,52},{8,24,40,56},{12,28,44,60},{1,17,33,49},{5,21..., dimensions={0} | all-to-all | bytes 262144 | tf_op jit(solution)/shard_map/all_to_all | solution.py:209
  229.7 0.6 reduce_sum.19
  (49 shorter events, 2.9 us)
Async XLA Ops:
  0.6 24.3 %copy-start = (f32[1,1024,256]{2,1,0:T(8,128)S(1)}, f32[1,1024,256]{2,1,0:T(8,128)}, u32[]{:S(2)}) copy-start(f32[1,1024,256]{2,1,0:T(8,128)} %param.8) | copy-start | bytes 3145732
  0.6 42.1 %collective-permute-start.3 = (f32[256,1024]{1,0:T(8,128)}, f32[256,1024]{1,0:T(8,128)}, u32[]{:S(2)}, u32[]{:S(2)}) collective-permute-start(f32[256,1024]{1,0:T(8,128)} %bitcast.121), channel_id=1, source_target_pairs={{0,4},{4,8},{8,12},{12,16},{16,20},{20,24},{24,28},{28,32},{32,36}... | collective-permute-start | bytes 3145736 | tf_op jit(solution)/shard_map/ppermute | solution.py:106
  4.6 38.1 %collective-permute-start.2 = (f32[256,1024]{1,0:T(8,128)}, f32[256,1024]{1,0:T(8,128)}, u32[]{:S(2)}, u32[]{:S(2)}) collective-permute-start(f32[256,1024]{1,0:T(8,128)} %bitcast.122), channel_id=1, source_target_pairs={{0,60},{4,0},{8,4},{12,8},{16,12},{20,16},{24,20},{28,24},{32,28},... | collective-permute-start | bytes 3145736 | tf_op jit(solution)/shard_map/ppermute | solution.py:106
  25.6 17.1 %collective-permute-start.1 = (f32[128,1024]{1,0:T(8,128)S(1)}, f32[128,1024]{1,0:T(8,128)S(1)}, u32[]{:S(2)}, u32[]{:S(2)}) collective-permute-start(f32[128,1024]{1,0:T(8,128)S(1)} %fusion.2), channel_id=1, source_target_pairs={{0,60},{4,0},{8,4},{12,8},{16,12},{20,16},{24,20},{28,24},{32,28},... | collective-permute-start | bytes 1572872 | tf_op jit(solution)/shard_map/ppermute | solution.py:106
  33.2 16.9 %collective-permute-start = (f32[128,1024]{1,0:T(8,128)}, f32[128,1024]{1,0:T(8,128)}, u32[]{:S(2)}, u32[]{:S(2)}) collective-permute-start(f32[128,1024]{1,0:T(8,128)} %fusion.6), channel_id=1, source_target_pairs={{0,4},{4,8},{8,12},{12,16},{16,20},{20,24},{24,28},{28,32},{32,36}... | collective-permute-start | bytes 1572872 | tf_op jit(solution)/shard_map/ppermute | solution.py:106
  35.2 0.8 copy-start.5
  37.2 11.5 %copy-start.2 = (f32[512,512]{1,0:T(8,128)S(1)}, f32[512,512]{1,0:T(8,128)}, u32[]{:S(2)}) copy-start(f32[512,512]{1,0:T(8,128)} %param.12) | copy-start | bytes 3145732
  43.6 11.4 %collective-permute-start.4 = (f32[128,1024]{1,0:T(8,128)}, f32[128,1024]{1,0:T(8,128)}, u32[]{:S(2)}, u32[]{:S(2)}) collective-permute-start(f32[128,1024]{1,0:T(8,128)} %add.240), channel_id=1, source_target_pairs={{0,60},{4,0},{8,4},{12,8},{16,12},{20,16},{24,20},{28,24},{32,28},... | collective-permute-start | bytes 1572872 | tf_op jit(solution)/shard_map/ppermute | solution.py:106
  56.9 21.2 %copy-start.1 = (f32[256,512]{1,0:T(8,128)S(1)}, f32[256,512]{1,0:T(8,128)}, u32[]{:S(2)}) copy-start(f32[256,512]{1,0:T(8,128)} %param.13) | copy-start | bytes 1572868
  57.6 38.9 %collective-permute-start.5 = (f32[32,1024]{1,0:T(8,128)}, f32[32,1024]{1,0:T(8,128)S(1)}, u32[]{:S(2)}, u32[]{:S(2)}) collective-permute-start(f32[32,1024]{1,0:T(8,128)} %get-tuple-element.19), channel_id=1, source_target_pairs={{0,16},{4,20},{8,24},{12,28},{16,32},{20,36},{24,40},{28,44},{32,4... | collective-permute-start | bytes 393224 | tf_op jit(solution)/shard_map/ppermute | solution.py:106
  61.1 35.4 %collective-permute-start.6 = (f32[32,1024]{1,0:T(8,128)}, f32[32,1024]{1,0:T(8,128)}, u32[]{:S(2)}, u32[]{:S(2)}) collective-permute-start(f32[32,1024]{1,0:T(8,128)} %get-tuple-element.20), channel_id=1, source_target_pairs={{0,32},{4,36},{8,40},{12,44},{16,48},{20,52},{24,56},{28,60},{32,0... | collective-permute-start | bytes 393224 | tf_op jit(solution)/shard_map/ppermute | solution.py:106
  72.6 23.9 %collective-permute-start.7 = (f32[32,1024]{1,0:T(8,128)S(1)}, f32[32,1024]{1,0:T(8,128)}, u32[]{:S(2)}, u32[]{:S(2)}) collective-permute-start(f32[32,1024]{1,0:T(8,128)S(1)} %get-tuple-element.21), channel_id=1, source_target_pairs={{0,48},{4,52},{8,56},{12,60},{16,0},{20,4},{24,8},{28,12},{32,16},... | collective-permute-start | bytes 393224 | tf_op jit(solution)/shard_map/ppermute | solution.py:106
  92.1 43.0 %collective-permute-start.8 = (f32[256,1024]{1,0:T(8,128)}, f32[256,1024]{1,0:T(8,128)S(1)}, u32[]{:S(2)}, u32[]{:S(2)}) collective-permute-start(f32[256,1024]{1,0:T(8,128)} %collective-permute-done.2), channel_id=1, source_target_pairs={{0,60},{4,0},{8,4},{12,8},{16,12},{20,16},{24,20},{28,24},{32,28},... | collective-permute-start | bytes 3145736 | tf_op jit(solution)/shard_map/ppermute | solution.py:106
  97.5 33.1 %copy-start.4 = (f32[32,1024]{1,0:T(8,128)}, f32[32,1024]{1,0:T(8,128)S(1)}, u32[]{:S(2)}) copy-start(f32[32,1024]{1,0:T(8,128)S(1)} %fusion.15) | copy-start | bytes 393220
  97.5 34.9 %copy-start.3 = (f32[1,256,1024]{2,1,0:T(8,128)S(1)}, f32[1,256,1024]{2,1,0:T(8,128)}, u32[]{:S(2)}) copy-start(f32[1,256,1024]{2,1,0:T(8,128)} %param.9) | copy-start | bytes 3145732
  135.8 18.4 %collective-permute-start.10 = (f32[264,512]{1,0:T(8,128)S(1)}, f32[264,512]{1,0:T(8,128)}, u32[]{:S(2)}, u32[]{:S(2)}) collective-permute-start(f32[264,512]{1,0:T(8,128)S(1)} %get-tuple-element.29), channel_id=1, source_target_pairs={{0,60},{4,0},{8,4},{12,8},{16,12},{20,16},{24,20},{28,24},{32,28},... | collective-permute-start | bytes 1622024 | tf_op jit(solution)/shard_map/ppermute | solution.py:106
  145.0 19.0 %all-to-all-start = ((f32[32,4,1024]{2,1,0:T(4,128)}), f32[32,4,1024]{2,1,0:T(4,128)S(1)}, u32[]{:S(2)}, u32[]{:S(2)}) async-start(f32[32,4,1024]{2,1,0:T(4,128)} %reshape.73), calls=%async_computation | async-start | bytes 1048576 | tf_op jit(solution)/shard_map/all_to_all | solution.py:24
  152.2 21.4 %collective-permute-start.9 = (f32[264,512]{1,0:T(8,128)S(1)}, f32[264,512]{1,0:T(8,128)}, u32[]{:S(2)}, u32[]{:S(2)}) collective-permute-start(f32[264,512]{1,0:T(8,128)S(1)} %get-tuple-element.28), channel_id=1, source_target_pairs={{0,4},{4,8},{8,12},{12,16},{16,20},{20,24},{24,28},{28,32},{32,36}... | collective-permute-start | bytes 1622024 | tf_op jit(solution)/shard_map/ppermute | solution.py:106
  154.2 32.4 %collective-permute-start.11 = (f32[264,512]{1,0:T(8,128)}, f32[264,512]{1,0:T(8,128)S(1)}, u32[]{:S(2)}, u32[]{:S(2)}) collective-permute-start(f32[264,512]{1,0:T(8,128)} %collective-permute-done.10), channel_id=1, source_target_pairs={{0,60},{4,0},{8,4},{12,8},{16,12},{20,16},{24,20},{28,24},{32,28},... | collective-permute-start | bytes 1622024 | tf_op jit(solution)/shard_map/ppermute | solution.py:106
  166.3 20.2 %all-to-all-start.1 = ((f32[4,32,256]{2,1,0:T(8,128)}), f32[4,32,256]{2,1,0:T(8,128)S(1)}, u32[]{:S(2)}, u32[]{:S(2)}) async-start(f32[4,32,256]{2,1,0:T(8,128)} %bitcast.39), calls=%async_computation.1 | async-start | bytes 262144 | tf_op jit(solution)/shard_map/all_to_all | solution.py:188

commit v7 on v6

--- a/solution.py
+++ b/solution.py
@@ -136,7 +136,9 @@
     from_two, border_above, border_below = lax.optimization_barrier(
         (from_two, border_above, border_below)
     )
-    from_above = shift(pivot_product(2) + from_two, -1)
+    above, border_sent = lax.optimization_barrier((pivot_product(2) + from_two, border_above))
+    from_above = shift(above, -1)
+    border_two = shift(border_sent, -1)
     near_sum = pivot_product(3) + from_below + from_above
     near_sum = near_sum.reshape(far, block, pivot_rows)
     far_id = lax.div(row_id, near)
@@ -144,13 +146,13 @@
     def far_block(offset):
         return lax.dynamic_index_in_dim(near_sum, lax.rem(far_id + offset, far), 0, keepdims=False)
 
+    order = sorted(range(1, far), key=lambda offset: -min(offset, far - offset))
     own = far_block(0)
-    sent = [far_block(offset) for offset in range(1, far)]
-    *sent, index, border_sent = lax.optimization_barrier((*sent, index, border_above))
-    sent = [shift(value, near * (1 + hop), False) for hop, value in enumerate(sent)]
-    border_two = shift(border_sent, -1)
+    sent = [far_block(offset) for offset in order]
+    *sent, index = lax.optimization_barrier((*sent, index))
+    sent = [shift(value, near * offset, False) for value, offset in zip(sent, order)]
     index = lax.all_gather(index, "front", axis=0)
-    *sent, index = lax.optimization_barrier((*sent, index))
+    *sent, index, border_two = lax.optimization_barrier((*sent, index, border_two))
     for value in sent:
         own = own + value
     pivot_live = col_id * pivot_rows + jnp.arange(pivot_rows, dtype=jnp.int32) < front_sizes[0, 0]

time: 231 us -> 221 us (0.957)
  the two profiles are of different devices: /device:TPU:32 before, /device:TPU:2 now
where the time goes in v7:
time: 221 us; the launch traced here: 220 us
  blocking collectives  95.1 us (43%)
  starting transfers between devices  69.5 us (31%)
  waiting for transfers between devices  24.3 us (11%)
  matrix products  14.8 us (7%)
  local copies, waits for them, and re-layouts  7.77 us (4%)
  other arithmetic  4.71 us (2%)
  Pallas kernels  2.28 us (1%)
    ppermute x12, starting transfers between devices, shift(): return lax.ppermute(value, ('front', 'row'), pairs)  55.9 us
    all_gather x1, blocking collectives, local(): lax.all_gather(own, 'row', axis_index_groups=apart, axis=0, tiled=True)  28.7 us
    all_to_all x1, blocking collectives, exchange(): return lax.all_to_all(blocks, axes, split_axis=0, concat_axis=0, tiled=True)  21.7 us
    all_to_all x1, blocking collectives, local(): lax.all_to_all(root, 'row', 0, 0, axis_index_groups=apart, tiled=True)  18.6 us
    dot_general x12, matrix products, contract(): lax.dot_general(left, right, ((left_dims, right_dims), ((), ())), precisi...  14.8 us
    all_to_all x1, waiting for transfers between devices, local(): lax.all_to_all(landed, 'row', 0, 0, axis_index_groups=apart, tiled=True)  13.7 us
    all_gather x1, blocking collectives, local(): rhs = lax.all_gather(rhs, 'col', axis=1, tiled=True)  13.3 us
    all_gather x1, blocking collectives, local(): index = lax.all_gather(index, 'front', axis=0)  12.9 us
  transfers between devices with their start and end apart: 14, of which 5 were waited for; matrix products, arithmetic and copies ran while one was open for 7% of the time, Pallas kernels for 1%

profile of v7, /device:TPU:2, one launch (start us, length us, event | category | flops | bytes accessed | tf_op | source)
XLA Modules:
  0.0 219.8 jit_solution(9618438633747611357)
XLA Ops:
  0.6 11.4 %collective-permute-start.2 = (f32[256,1024]{1,0:T(8,128)}, f32[256,1024]{1,0:T(8,128)}, u32[]{:S(2)}, u32[]{:S(2)}) collective-permute-start(f32[256,1024]{1,0:T(8,128)} %bitcast.121), channel_id=1, source_target_pairs={{0,60},{4,0},{8,4},{12,8},{16,12},{20,16},{24,20},{28,24},{32,28},... | collective-permute-start | bytes 3145736 | tf_op jit(solution)/shard_map/ppermute | solution.py:106
  12.1 1.9 collective-permute-start.3
  14.0 1.0 copy.20
  15.3 13.3 %all_gather.12 = f32[4,256,128]{2,0,1:T(4,128)S(1)} all-gather(f32[4,64,128]{2,0,1:T(4,128)S(1)} %copy.22), channel_id=1, replica_groups=mesh['front'=8,'row'=16,'col'=4] {'col'}, dimensions={1}, use_global_device_ids=true | all-gather | bytes 655360 | tf_op jit(solution)/shard_map/all_gather | solution.py:129
  29.0 0.7 fusion.2
  29.7 5.3 %collective-permute-start.1 = (f32[128,1024]{1,0:T(8,128)S(1)}, f32[128,1024]{1,0:T(8,128)S(1)}, u32[]{:S(2)}, u32[]{:S(2)}) collective-permute-start(f32[128,1024]{1,0:T(8,128)S(1)} %fusion.2), channel_id=1, source_target_pairs={{0,60},{4,0},{8,4},{12,8},{16,12},{20,16},{24,20},{28,24},{32,28},... | collective-permute-start | bytes 1572872 | tf_op jit(solution)/shard_map/ppermute | solution.py:106
  35.1 1.5 fusion.6
  36.6 1.9 collective-permute-start
  38.5 0.7 constant_dynamic-slice_fusion.4
  39.3 0.6 fusion.29
  39.9 0.7 fusion.4
  40.6 6.0 %collective-permute-done.1 = f32[128,1024]{1,0:T(8,128)S(1)} collective-permute-done((f32[128,1024]{1,0:T(8,128)S(1)}, f32[128,1024]{1,0:T(8,128)S(1)}, u32[]{:S(2)}, u32[]{:S(2)}) %collective-permute-start.1) | collective-permute-done | bytes 524320 | tf_op jit(solution)/shard_map/ppermute | solution.py:106
  46.6 0.9 add.240
  47.5 5.6 %collective-permute-start.4 = (f32[128,1024]{1,0:T(8,128)}, f32[128,1024]{1,0:T(8,128)}, u32[]{:S(2)}, u32[]{:S(2)}) collective-permute-start(f32[128,1024]{1,0:T(8,128)} %add.240), channel_id=1, source_target_pairs={{0,60},{4,0},{8,4},{12,8},{16,12},{20,16},{24,20},{28,24},{32,28},... | collective-permute-start | bytes 1572872 | tf_op jit(solution)/shard_map/ppermute | solution.py:106
  53.1 0.7 compare_select_fusion
  54.5 1.9 collective-permute-start.8
  56.4 0.7 compare_select_fusion.2
  57.1 2.9 %collective-permute-done.4 = f32[128,1024]{1,0:T(8,128)} collective-permute-done((f32[128,1024]{1,0:T(8,128)}, f32[128,1024]{1,0:T(8,128)}, u32[]{:S(2)}, u32[]{:S(2)}) %collective-permute-start.4) | collective-permute-done | bytes 524320 | tf_op jit(solution)/shard_map/ppermute | solution.py:106
  60.1 1.9 fusion
  62.0 0.7 dynamic-slice_bitcast_fusion
  62.7 7.1 %collective-permute-start.5 = (f32[32,1024]{1,0:T(8,128)}, f32[32,1024]{1,0:T(8,128)S(1)}, u32[]{:S(2)}, u32[]{:S(2)}) collective-permute-start(f32[32,1024]{1,0:T(8,128)} %get-tuple-element.22), channel_id=1, source_target_pairs={{0,32},{4,36},{8,40},{12,44},{16,48},{20,52},{24,56},{28,60},{32,0... | collective-permute-start | bytes 393224 | tf_op jit(solution)/shard_map/ppermute | solution.py:106
  69.8 6.2 %collective-permute-start.6 = (f32[32,1024]{1,0:T(8,128)}, f32[32,1024]{1,0:T(8,128)}, u32[]{:S(2)}, u32[]{:S(2)}) collective-permute-start(f32[32,1024]{1,0:T(8,128)} %get-tuple-element.23), channel_id=1, source_target_pairs={{0,16},{4,20},{8,24},{12,28},{16,32},{20,36},{24,40},{28,44},{32,4... | collective-permute-start | bytes 393224 | tf_op jit(solution)/shard_map/ppermute | solution.py:106
  76.0 3.5 %collective-permute-start.7 = (f32[32,1024]{1,0:T(8,128)S(1)}, f32[32,1024]{1,0:T(8,128)}, u32[]{:S(2)}, u32[]{:S(2)}) collective-permute-start(f32[32,1024]{1,0:T(8,128)S(1)} %get-tuple-element.24), channel_id=1, source_target_pairs={{0,48},{4,52},{8,56},{12,60},{16,0},{20,4},{24,8},{28,12},{32,16},... | collective-permute-start | bytes 393224 | tf_op jit(solution)/shard_map/ppermute | solution.py:106
  79.7 0.7 add_compare_fusion
  80.4 12.9 %all-gather = s32[8192]{0:T(1024)S(1)} all-gather(s32[1024]{0:T(1024)S(1)} %pad_add_fusion), channel_id=2, replica_groups=mesh['front'=8,'row'=16,'col'=4] {'front'}, dimensions={0}, use_global_device_ids=true | all-gather | bytes 36864 | tf_op jit(solution)/shard_map/all_gather | solution.py:154
  93.7 1.0 fusion.15
  94.7 28.7 %all_gather.15 = f32[128,1024]{1,0:T(8,128)S(1)} all-gather(f32[32,1024]{1,0:T(8,128)S(1)} %fusion.15), channel_id=1, replica_groups={{0,16,32,48},{4,20,36,52},{8,24,40,56},{12,28,44,60},{1,17,33,49},{5,21..., dimensions={0}, use_global_device_ids=true | all-gather | bytes 655360 | tf_op jit(solution)/shard_map/all_gather | solution.py:162
  123.4 1.9 fusion.30
  125.3 0.7 fusion.25
  126.0 1.9 fusion.31
  127.9 1.9 fusion.32
  129.8 1.9 collective-permute-start.10
  131.8 1.0 reshape.73
  132.7 7.1 %all-to-all-start = ((f32[32,4,1024]{2,1,0:T(4,128)}), f32[32,4,1024]{2,1,0:T(4,128)S(1)}, u32[]{:S(2)}, u32[]{:S(2)}) async-start(f32[32,4,1024]{2,1,0:T(4,128)} %reshape.73), calls=%async_computation | async-start | bytes 1048576 | tf_op jit(solution)/shard_map/all_to_all | solution.py:24
  139.8 3.9 %collective-permute-start.9 = (f32[264,512]{1,0:T(8,128)S(1)}, f32[264,512]{1,0:T(8,128)}, u32[]{:S(2)}, u32[]{:S(2)}) collective-permute-start(f32[264,512]{1,0:T(8,128)S(1)} %get-tuple-element.32), channel_id=1, source_target_pairs={{0,4},{4,8},{8,12},{12,16},{16,20},{20,24},{24,28},{28,32},{32,36}... | collective-permute-start | bytes 1622024 | tf_op jit(solution)/shard_map/ppermute | solution.py:106
  143.8 5.1 %collective-permute-start.11 = (f32[264,512]{1,0:T(8,128)}, f32[264,512]{1,0:T(8,128)S(1)}, u32[]{:S(2)}, u32[]{:S(2)}) collective-permute-start(f32[264,512]{1,0:T(8,128)} %collective-permute-done.10), channel_id=1, source_target_pairs={{0,60},{4,0},{8,4},{12,8},{16,12},{20,16},{24,20},{28,24},{32,28},... | collective-permute-start | bytes 1622024 | tf_op jit(solution)/shard_map/ppermute | solution.py:106
  149.0 1.2 all-to-all-done.update_ref
  150.2 2.3 %shard_map.86 = f32[128,256]{1,0:T(8,128)} custom-call(f32[32,4,1024]{2,1,0:T(4,128)S(1)} %all-to-all-done.update_ref, s32[8,1,1024]{2,1,0:T(1,128)S(1)} %copy.25.place_ref, s32[8,1,1024]{2,1,0:T(1,128)S(1)} %broadcast_in_dim.45.high_ref), custom_call_target="tpu_custom_call" | custom-call | flops 1073741824 | bytes 655360 | tf_op jit(solution)/shard_map/pallas_call | solution.py:62
  152.5 6.5 %all-to-all-start.1 = ((f32[4,32,256]{2,1,0:T(8,128)}), f32[4,32,256]{2,1,0:T(8,128)S(1)}, u32[]{:S(2)}, u32[]{:S(2)}) async-start(f32[4,32,256]{2,1,0:T(8,128)} %bitcast.39), calls=%async_computation.1 | async-start | bytes 262144 | tf_op jit(solution)/shard_map/all_to_all | solution.py:190
  159.0 0.7 slice.76
  159.7 0.7 slice.75
  160.4 13.7 %all-to-all-done.1 = f32[4,32,256]{2,1,0:T(8,128)S(1)} async-done(((f32[4,32,256]{2,1,0:T(8,128)}), f32[4,32,256]{2,1,0:T(8,128)S(1)}, u32[]{:S(2)}, u32[]{:S(2)}) %all-to-all-start.1) | async-done | bytes 131104 | tf_op jit(solution)/shard_map/all_to_all | solution.py:190
  174.2 0.5 broadcast_in_dim.46
  174.7 21.7 %all_to_all.20 = f32[32,4,2,4,256]{4,2,3,1,0:T(2,128)S(1)} all-to-all(f32[32,4,2,4,256]{4,2,3,1,0:T(2,128)S(1)} %broadcast_in_dim.46), channel_id=1, replica_groups=mesh['front'=8,'row'=16,'col'=4] {'front','col'}, dimensions={0} | all-to-all | bytes 2097152 | tf_op jit(solution)/shard_map/all_to_all | solution.py:24
  197.3 1.4 fusion.10
  198.8 1.5 fusion.1
  200.7 18.6 %all_to_all.21 = f32[4,32,256]{2,1,0:T(8,128)S(1)} all-to-all(f32[4,32,256]{2,1,0:T(8,128)S(1)} %bitcast.130), channel_id=1, replica_groups={{0,16,32,48},{4,20,36,52},{8,24,40,56},{12,28,44,60},{1,17,33,49},{5,21..., dimensions={0} | all-to-all | bytes 262144 | tf_op jit(solution)/shard_map/all_to_all | solution.py:211
  219.2 0.6 reduce_sum.19
  (49 shorter events, 3.4 us)
Async XLA Ops:
  0.6 28.4 %copy-start = (f32[1,1024,256]{2,1,0:T(8,128)S(1)}, f32[1,1024,256]{2,1,0:T(8,128)}, u32[]{:S(2)}) copy-start(f32[1,1024,256]{2,1,0:T(8,128)} %param.8) | copy-start | bytes 3145732
  0.6 46.0 %collective-permute-start.2 = (f32[256,1024]{1,0:T(8,128)}, f32[256,1024]{1,0:T(8,128)}, u32[]{:S(2)}, u32[]{:S(2)}) collective-permute-start(f32[256,1024]{1,0:T(8,128)} %bitcast.121), channel_id=1, source_target_pairs={{0,60},{4,0},{8,4},{12,8},{16,12},{20,16},{24,20},{28,24},{32,28},... | collective-permute-start | bytes 3145736 | tf_op jit(solution)/shard_map/ppermute | solution.py:106
  12.1 34.6 %collective-permute-start.3 = (f32[256,1024]{1,0:T(8,128)}, f32[256,1024]{1,0:T(8,128)}, u32[]{:S(2)}, u32[]{:S(2)}) collective-permute-start(f32[256,1024]{1,0:T(8,128)} %bitcast.122), channel_id=1, source_target_pairs={{0,4},{4,8},{8,12},{12,16},{16,20},{20,24},{24,28},{28,32},{32,36}... | collective-permute-start | bytes 3145736 | tf_op jit(solution)/shard_map/ppermute | solution.py:106
  29.7 16.9 %collective-permute-start.1 = (f32[128,1024]{1,0:T(8,128)S(1)}, f32[128,1024]{1,0:T(8,128)S(1)}, u32[]{:S(2)}, u32[]{:S(2)}) collective-permute-start(f32[128,1024]{1,0:T(8,128)S(1)} %fusion.2), channel_id=1, source_target_pairs={{0,60},{4,0},{8,4},{12,8},{16,12},{20,16},{24,20},{28,24},{32,28},... | collective-permute-start | bytes 1572872 | tf_op jit(solution)/shard_map/ppermute | solution.py:106
  36.6 20.6 %collective-permute-start = (f32[128,1024]{1,0:T(8,128)}, f32[128,1024]{1,0:T(8,128)}, u32[]{:S(2)}, u32[]{:S(2)}) collective-permute-start(f32[128,1024]{1,0:T(8,128)} %fusion.6), channel_id=1, source_target_pairs={{0,4},{4,8},{8,12},{12,16},{16,20},{20,24},{24,28},{28,32},{32,36}... | collective-permute-start | bytes 1572872 | tf_op jit(solution)/shard_map/ppermute | solution.py:106
  38.5 0.8 copy-start.5
  40.6 13.3 %copy-start.2 = (f32[512,512]{1,0:T(8,128)S(1)}, f32[512,512]{1,0:T(8,128)}, u32[]{:S(2)}) copy-start(f32[512,512]{1,0:T(8,128)} %param.12) | copy-start | bytes 3145732
  47.5 12.6 %collective-permute-start.4 = (f32[128,1024]{1,0:T(8,128)}, f32[128,1024]{1,0:T(8,128)}, u32[]{:S(2)}, u32[]{:S(2)}) collective-permute-start(f32[128,1024]{1,0:T(8,128)} %add.240), channel_id=1, source_target_pairs={{0,60},{4,0},{8,4},{12,8},{16,12},{20,16},{24,20},{28,24},{32,28},... | collective-permute-start | bytes 1572872 | tf_op jit(solution)/shard_map/ppermute | solution.py:106
  54.5 39.2 %collective-permute-start.8 = (f32[256,1024]{1,0:T(8,128)}, f32[256,1024]{1,0:T(8,128)}, u32[]{:S(2)}, u32[]{:S(2)}) collective-permute-start(f32[256,1024]{1,0:T(8,128)} %collective-permute-done.2), channel_id=1, source_target_pairs={{0,60},{4,0},{8,4},{12,8},{16,12},{20,16},{24,20},{28,24},{32,28},... | collective-permute-start | bytes 3145736 | tf_op jit(solution)/shard_map/ppermute | solution.py:106
  62.0 17.6 %copy-start.1 = (f32[256,512]{1,0:T(8,128)S(1)}, f32[256,512]{1,0:T(8,128)}, u32[]{:S(2)}) copy-start(f32[256,512]{1,0:T(8,128)} %param.13) | copy-start | bytes 1572868
  62.7 30.5 %collective-permute-start.5 = (f32[32,1024]{1,0:T(8,128)}, f32[32,1024]{1,0:T(8,128)S(1)}, u32[]{:S(2)}, u32[]{:S(2)}) collective-permute-start(f32[32,1024]{1,0:T(8,128)} %get-tuple-element.22), channel_id=1, source_target_pairs={{0,32},{4,36},{8,40},{12,44},{16,48},{20,52},{24,56},{28,60},{32,0... | collective-permute-start | bytes 393224 | tf_op jit(solution)/shard_map/ppermute | solution.py:106
  69.8 23.5 %collective-permute-start.6 = (f32[32,1024]{1,0:T(8,128)}, f32[32,1024]{1,0:T(8,128)}, u32[]{:S(2)}, u32[]{:S(2)}) collective-permute-start(f32[32,1024]{1,0:T(8,128)} %get-tuple-element.23), channel_id=1, source_target_pairs={{0,16},{4,20},{8,24},{12,28},{16,32},{20,36},{24,40},{28,44},{32,4... | collective-permute-start | bytes 393224 | tf_op jit(solution)/shard_map/ppermute | solution.py:106
  76.0 17.7 %collective-permute-start.7 = (f32[32,1024]{1,0:T(8,128)S(1)}, f32[32,1024]{1,0:T(8,128)}, u32[]{:S(2)}, u32[]{:S(2)}) collective-permute-start(f32[32,1024]{1,0:T(8,128)S(1)} %get-tuple-element.24), channel_id=1, source_target_pairs={{0,48},{4,52},{8,56},{12,60},{16,0},{20,4},{24,8},{28,12},{32,16},... | collective-permute-start | bytes 393224 | tf_op jit(solution)/shard_map/ppermute | solution.py:106
  94.7 28.7 %copy-start.4 = (f32[32,1024]{1,0:T(8,128)}, f32[32,1024]{1,0:T(8,128)S(1)}, u32[]{:S(2)}) copy-start(f32[32,1024]{1,0:T(8,128)S(1)} %fusion.15) | copy-start | bytes 393220
  94.7 30.6 %copy-start.3 = (f32[1,256,1024]{2,1,0:T(8,128)S(1)}, f32[1,256,1024]{2,1,0:T(8,128)}, u32[]{:S(2)}) copy-start(f32[1,256,1024]{2,1,0:T(8,128)} %param.9) | copy-start | bytes 3145732
  129.8 14.0 %collective-permute-start.10 = (f32[264,512]{1,0:T(8,128)S(1)}, f32[264,512]{1,0:T(8,128)}, u32[]{:S(2)}, u32[]{:S(2)}) collective-permute-start(f32[264,512]{1,0:T(8,128)S(1)} %get-tuple-element.33), channel_id=1, source_target_pairs={{0,60},{4,0},{8,4},{12,8},{16,12},{20,16},{24,20},{28,24},{32,28},... | collective-permute-start | bytes 1622024 | tf_op jit(solution)/shard_map/ppermute | solution.py:106
  132.7 17.5 %all-to-all-start = ((f32[32,4,1024]{2,1,0:T(4,128)}), f32[32,4,1024]{2,1,0:T(4,128)S(1)}, u32[]{:S(2)}, u32[]{:S(2)}) async-start(f32[32,4,1024]{2,1,0:T(4,128)} %reshape.73), calls=%async_computation | async-start | bytes 1048576 | tf_op jit(solution)/shard_map/all_to_all | solution.py:24
  139.8 19.8 %collective-permute-start.9 = (f32[264,512]{1,0:T(8,128)S(1)}, f32[264,512]{1,0:T(8,128)}, u32[]{:S(2)}, u32[]{:S(2)}) collective-permute-start(f32[264,512]{1,0:T(8,128)S(1)} %get-tuple-element.32), channel_id=1, source_target_pairs={{0,4},{4,8},{8,12},{12,16},{16,20},{20,24},{24,28},{28,32},{32,36}... | collective-permute-start | bytes 1622024 | tf_op jit(solution)/shard_map/ppermute | solution.py:106
  143.8 30.4 %collective-permute-start.11 = (f32[264,512]{1,0:T(8,128)}, f32[264,512]{1,0:T(8,128)S(1)}, u32[]{:S(2)}, u32[]{:S(2)}) collective-permute-start(f32[264,512]{1,0:T(8,128)} %collective-permute-done.10), channel_id=1, source_target_pairs={{0,60},{4,0},{8,4},{12,8},{16,12},{20,16},{24,20},{28,24},{32,28},... | collective-permute-start | bytes 1622024 | tf_op jit(solution)/shard_map/ppermute | solution.py:106
  152.5 21.6 %all-to-all-start.1 = ((f32[4,32,256]{2,1,0:T(8,128)}), f32[4,32,256]{2,1,0:T(8,128)S(1)}, u32[]{:S(2)}, u32[]{:S(2)}) async-start(f32[4,32,256]{2,1,0:T(8,128)} %bitcast.39), calls=%async_computation.1 | async-start | bytes 262144 | tf_op jit(solution)/shard_map/all_to_all | solution.py:190

commit v8 on v7

--- a/solution.py
+++ b/solution.py
@@ -24,8 +24,8 @@
     return lax.all_to_all(blocks, axes, split_axis=0, concat_axis=0, tiled=True)
 
 
-def land_kernel(fronts, cols, update_ref, place_ref, high_ref, out_ref):
-    part, border_rows = update_ref.shape[1:]
+def land_kernel(fronts, cols, border_rows, update_ref, out_ref):
+    part = update_ref.shape[1]
     out_rows, high_count = out_ref.shape
     places = out_rows // part
     repeats = max(1, 8 // part)
@@ -35,13 +35,17 @@
     high_iota = lax.broadcasted_iota(jnp.int32, (high_count, border_rows), 0)
     total = None
     for front in range(fronts):
-        value = update_ref[front * cols]
+        value = update_ref[front * cols][:, :border_rows]
         for col in range(1, cols):
-            value = value + update_ref[front * cols + col]
+            value = value + update_ref[front * cols + col][:, :border_rows]
+        codes = update_ref[front * cols][:, border_rows:]
+        codes = jnp.concatenate([codes[row : row + 1] for row in range(part)], 1).astype(jnp.int32)
+        place = jnp.where(codes < 0, -1, codes // high_count)
+        high = codes % high_count
         value = jnp.concatenate([value] * repeats, 0)
         coarse = value.astype(jnp.bfloat16).astype(jnp.float32)
-        at_high = jnp.where(high_iota == high_ref[front], 1.0, 0.0).astype(jnp.bfloat16)
-        at_place = place_iota == place_ref[front][None]
+        at_high = jnp.where(high_iota == high, 1.0, 0.0).astype(jnp.bfloat16)
+        at_place = place_iota == place[None]
         pieces = []
         for piece in (coarse, value - coarse):
             spread = jnp.where(at_place, piece[None], 0.0)
@@ -57,12 +61,12 @@
     out_ref[...] = total
 
 
-def land(update, place, high, fronts, cols, places, high_count):
-    part, border_rows = update.shape[1:]
+def land(update, border_rows, fronts, cols, places, high_count):
+    part = update.shape[1]
     return pl.pallas_call(
-        functools.partial(land_kernel, fronts, cols),
+        functools.partial(land_kernel, fronts, cols, border_rows),
         out_shape=jax.ShapeDtypeStruct((places * part, high_count), jnp.float32),
-        in_specs=[pl.BlockSpec(memory_space=pltpu.VMEM)] * 3,
+        in_specs=[pl.BlockSpec(memory_space=pltpu.VMEM)],
         out_specs=pl.BlockSpec(memory_space=pltpu.VMEM),
         compiler_params=pltpu.CompilerParams(vmem_limit_bytes=32 * 1024 * 1024),
         cost_estimate=pl.CostEstimate(
@@ -70,7 +74,7 @@
             bytes_accessed=4 * (update.size + places * part * high_count),
             transcendentals=0,
         ),
-    )(update, place[:, None], high[:, None])
+    )(update)
 
 
 def local(
@@ -115,6 +119,11 @@
         piece = lax.dynamic_slice_in_dim(border_index[0], start, border_rows)
         index.append(jnp.where(live, piece, -1))
     index = jnp.concatenate(index)
+    low = lax.div(jnp.maximum(index, 0), high_count)
+    owner = lax.rem(lax.div(low, halves) - lax.rem(row_id, near) + 1 + rows, rows)
+    code = (owner * halves + lax.rem(low, halves)) * high_count + lax.rem(index, high_count)
+    code = jnp.where(index < 0, -1, code).astype(jnp.float32)
+    code = jnp.tile(code.reshape(part, -1), (layer, 1))
 
     rhs = child_rhs[0].reshape(-1, far, near, block).transpose(2, 0, 1, 3)
     rhs = rhs.reshape(near, -1, far * block)
@@ -146,13 +155,11 @@
     def far_block(offset):
         return lax.dynamic_index_in_dim(near_sum, lax.rem(far_id + offset, far), 0, keepdims=False)
 
-    order = sorted(range(1, far), key=lambda offset: -min(offset, far - offset))
     own = far_block(0)
-    sent = [far_block(offset) for offset in order]
-    *sent, index = lax.optimization_barrier((*sent, index))
-    sent = [shift(value, near * offset, False) for value, offset in zip(sent, order)]
-    index = lax.all_gather(index, "front", axis=0)
-    *sent, index, border_two = lax.optimization_barrier((*sent, index, border_two))
+    sent = []
+    for offset in sorted(range(1, far), key=lambda offset: -min(offset, far - offset)):
+        sent.append(shift(far_block(offset), near * offset, False))
+    *sent, border_two = lax.optimization_barrier((*sent, border_two))
     for value in sent:
         own = own + value
     pivot_live = col_id * pivot_rows + jnp.arange(pivot_rows, dtype=jnp.int32) < front_sizes[0, 0]
@@ -161,7 +168,8 @@
     apart = [[g + near * i for i in range(far)] for g in range(near)]
     solved = lax.all_gather(own, "row", axis_index_groups=apart, axis=0, tiled=True)
     window = (border, border_above, border_below, border_two)
-    update = jnp.concatenate([contract(solved, value, (1,), (1,)) for value in window], 1)
+    update = [contract(solved, value, (1,), (1,)) for value in window]
+    update = jnp.concatenate([*update, code], 1)
 
     share = front_id * cols + col_id
     per_block = layer // far
@@ -177,15 +185,11 @@
     upward = jnp.concatenate([root_inverse, share_of(-1), share_of(-2)])
     downward = jnp.concatenate([root_inverse, share_of(1), share_of(1)])
     update, upward, downward = lax.optimization_barrier((update, upward, downward))
-    update = exchange(update.reshape(layer, part, near * border_rows), ("front", "col"))
+    update = exchange(update.reshape(layer, part, -1), ("front", "col"))
     upward = shift(upward, -1, False)
     downward = shift(downward, 1, False)
 
-    low = lax.div(jnp.maximum(index, 0), high_count)
-    owner = lax.rem(lax.div(low, halves) - lax.rem(row_id, near) + 1 + rows, rows)
-    place = jnp.where(index < 0, -1, owner * halves + lax.rem(low, halves))
-    high = lax.rem(index, high_count)
-    landed = land(update, place, high, fronts, cols, low_count, high_count)
+    landed = land(update, near * border_rows, fronts, cols, low_count, high_count)
     landed = landed.reshape(far, near * halves * part, high_count)
     landed = lax.all_to_all(landed, "row", 0, 0, axis_index_groups=apart, tiled=True).sum(0)
     landed = landed.reshape(near, halves, part, high_count)

time: 221 us -> 229 us (1.036)
  the two profiles are of different devices: /device:TPU:2 before, /device:TPU:32 now
where the time goes in v8:
time: 229 us; the launch traced here: 228 us
  blocking collectives  81.1 us (35%)
  starting transfers between devices  74.3 us (32%)
  waiting for transfers between devices  41.7 us (18%)
  matrix products  14.8 us (6%)
  local copies, waits for them, and re-layouts  8.48 us (4%)
  other arithmetic  3.65 us (2%)
  Pallas kernels  2.45 us (1%)
    ppermute x12, starting transfers between devices, shift(): return lax.ppermute(value, ('front', 'row'), pairs)  60 us
    ppermute x12, waiting for transfers between devices, shift(): return lax.ppermute(value, ('front', 'row'), pairs)  28 us
    all_gather x1, blocking collectives, local(): lax.all_gather(own, 'row', axis_index_groups=apart, axis=0, tiled=True)  25.7 us
    all_to_all x1, blocking collectives, exchange(): return lax.all_to_all(blocks, axes, split_axis=0, concat_axis=0, tiled=True)  23.9 us
    all_to_all x1, blocking collectives, local(): lax.all_to_all(root, 'row', 0, 0, axis_index_groups=apart, tiled=True)  18.4 us
    dot_general x12, matrix products, contract(): lax.dot_general(left, right, ((left_dims, right_dims), ((), ())), precisi...  14.8 us
    all_to_all x1, waiting for transfers between devices, local(): lax.all_to_all(landed, 'row', 0, 0, axis_index_groups=apart, tiled=True)  13.6 us
    all_gather x1, blocking collectives, local(): rhs = lax.all_gather(rhs, 'col', axis=1, tiled=True)  13.1 us
  transfers between devices with their start and end apart: 14, of which 5 were waited for; matrix products, arithmetic and copies ran while one was open for 6% of the time, Pallas kernels for 1%

profile of v8, /device:TPU:32, one launch (start us, length us, event | category | flops | bytes accessed | tf_op | source)
XLA Modules:
  0.0 227.9 jit_solution(2711439895892020966)
XLA Ops:
  0.6 7.5 %collective-permute-start.2 = (f32[256,1024]{1,0:T(8,128)}, f32[256,1024]{1,0:T(8,128)}, u32[]{:S(2)}, u32[]{:S(2)}) collective-permute-start(f32[256,1024]{1,0:T(8,128)} %bitcast.119), channel_id=1, source_target_pairs={{0,60},{4,0},{8,4},{12,8},{16,12},{20,16},{24,20},{28,24},{32,28},... | collective-permute-start | bytes 3145736 | tf_op jit(solution)/shard_map/ppermute | solution.py:110
  8.2 1.9 collective-permute-start.3
  10.1 1.0 copy.18
  11.4 13.1 %all_gather.6 = f32[4,256,128]{2,0,1:T(4,128)S(1)} all-gather(f32[4,64,128]{2,0,1:T(4,128)S(1)} %copy.20), channel_id=1, replica_groups=mesh['front'=8,'row'=16,'col'=4] {'col'}, dimensions={1}, use_global_device_ids=true | all-gather | bytes 655360 | tf_op jit(solution)/shard_map/all_gather | solution.py:138
  24.5 1.0 fusion.28
  25.5 0.7 fusion.2
  26.3 6.1 %collective-permute-start.1 = (f32[128,1024]{1,0:T(8,128)S(1)}, f32[128,1024]{1,0:T(8,128)S(1)}, u32[]{:S(2)}, u32[]{:S(2)}) collective-permute-start(f32[128,1024]{1,0:T(8,128)S(1)} %fusion.2), channel_id=1, source_target_pairs={{0,60},{4,0},{8,4},{12,8},{16,12},{20,16},{24,20},{28,24},{32,28},... | collective-permute-start | bytes 1572872 | tf_op jit(solution)/shard_map/ppermute | solution.py:110
  32.4 1.5 fusion.6
  33.9 1.9 collective-permute-start
  35.8 0.7 constant_dynamic-slice_fusion.4
  36.6 0.6 fusion.29
  37.2 0.6 compare_select_fusion
  37.8 0.7 compare_select_fusion.2
  38.5 0.7 fusion.4
  39.2 4.2 %collective-permute-done.1 = f32[128,1024]{1,0:T(8,128)S(1)} collective-permute-done((f32[128,1024]{1,0:T(8,128)S(1)}, f32[128,1024]{1,0:T(8,128)S(1)}, u32[]{:S(2)}, u32[]{:S(2)}) %collective-permute-start.1) | collective-permute-done | bytes 524320 | tf_op jit(solution)/shard_map/ppermute | solution.py:110
  43.4 0.9 add.255
  44.3 5.9 %collective-permute-start.4 = (f32[128,1024]{1,0:T(8,128)}, f32[128,1024]{1,0:T(8,128)}, u32[]{:S(2)}, u32[]{:S(2)}) collective-permute-start(f32[128,1024]{1,0:T(8,128)} %add.255), channel_id=1, source_target_pairs={{0,60},{4,0},{8,4},{12,8},{16,12},{20,16},{24,20},{28,24},{32,28},... | collective-permute-start | bytes 1572872 | tf_op jit(solution)/shard_map/ppermute | solution.py:110
  50.1 5.6 %collective-permute-start.8 = (f32[256,1024]{1,0:T(8,128)}, f32[256,1024]{1,0:T(8,128)}, u32[]{:S(2)}, u32[]{:S(2)}) collective-permute-start(f32[256,1024]{1,0:T(8,128)} %collective-permute-done.2), channel_id=1, source_target_pairs={{0,60},{4,0},{8,4},{12,8},{16,12},{20,16},{24,20},{28,24},{32,28},... | collective-permute-start | bytes 3145736 | tf_op jit(solution)/shard_map/ppermute | solution.py:110
  56.7 0.6 add_compare_fusion
  57.4 1.9 fusion
  59.4 9.1 %collective-permute-start.5 = (f32[32,1024]{1,0:T(8,128)S(1)}, f32[32,1024]{1,0:T(8,128)S(1)}, u32[]{:S(2)}, u32[]{:S(2)}) collective-permute-start(f32[32,1024]{1,0:T(8,128)S(1)} %get-tuple-element.38), channel_id=1, source_target_pairs={{0,32},{4,36},{8,40},{12,44},{16,48},{20,52},{24,56},{28,60},{32,0... | collective-permute-start | bytes 393224 | tf_op jit(solution)/shard_map/ppermute | solution.py:110
  68.5 4.5 %collective-permute-start.6 = (f32[32,1024]{1,0:T(8,128)S(1)}, f32[32,1024]{1,0:T(8,128)S(1)}, u32[]{:S(2)}, u32[]{:S(2)}) collective-permute-start(f32[32,1024]{1,0:T(8,128)S(1)} %get-tuple-element.37), channel_id=1, source_target_pairs={{0,16},{4,20},{8,24},{12,28},{16,32},{20,36},{24,40},{28,44},{32,4... | collective-permute-start | bytes 393224 | tf_op jit(solution)/shard_map/ppermute | solution.py:110
  73.0 5.3 %collective-permute-start.7 = (f32[32,1024]{1,0:T(8,128)S(1)}, f32[32,1024]{1,0:T(8,128)S(1)}, u32[]{:S(2)}, u32[]{:S(2)}) collective-permute-start(f32[32,1024]{1,0:T(8,128)S(1)} %get-tuple-element.36), channel_id=1, source_target_pairs={{0,48},{4,52},{8,56},{12,60},{16,0},{20,4},{24,8},{28,12},{32,16},... | collective-permute-start | bytes 393224 | tf_op jit(solution)/shard_map/ppermute | solution.py:110
  78.4 9.7 %collective-permute-done.5 = f32[32,1024]{1,0:T(8,128)S(1)} collective-permute-done((f32[32,1024]{1,0:T(8,128)S(1)}, f32[32,1024]{1,0:T(8,128)S(1)}, u32[]{:S(2)}, u32[]{:S(2)}) %collective-permute-start.5) | collective-permute-done | bytes 131104 | tf_op jit(solution)/shard_map/ppermute | solution.py:110
  88.1 4.2 %collective-permute-done.7 = f32[32,1024]{1,0:T(8,128)S(1)} collective-permute-done((f32[32,1024]{1,0:T(8,128)S(1)}, f32[32,1024]{1,0:T(8,128)S(1)}, u32[]{:S(2)}, u32[]{:S(2)}) %collective-permute-start.7) | collective-permute-done | bytes 131104 | tf_op jit(solution)/shard_map/ppermute | solution.py:110
  92.3 0.6 copy-done.4
  92.9 25.7 %all_gather.7 = f32[128,1024]{1,0:T(8,128)S(1)} all-gather(f32[32,1024]{1,0:T(8,128)S(1)} %fusion.15), channel_id=1, replica_groups={{0,16,32,48},{4,20,36,52},{8,24,40,56},{12,28,44,60},{1,17,33,49},{5,21..., dimensions={0}, use_global_device_ids=true | all-gather | bytes 655360 | tf_op jit(solution)/shard_map/all_gather | solution.py:169
  118.6 0.7 convolution_dynamic-update-slice_fusion.3
  119.3 1.9 convolution_dynamic-update-slice_fusion.2
  121.2 1.9 convolution_dynamic-update-slice_fusion.1
  123.1 1.9 convolution_dynamic-update-slice_fusion
  125.0 1.0 reshape.120
  126.0 7.7 %all-to-all-start = ((f32[32,4,1280]{2,1,0:T(4,128)}), f32[32,4,1280]{2,1,0:T(4,128)S(1)}, u32[]{:S(2)}, u32[]{:S(2)}) async-start(f32[32,4,1280]{2,1,0:T(4,128)} %reshape.120), calls=%async_computation | async-start | bytes 1310720 | tf_op jit(solution)/shard_map/all_to_all | solution.py:24
  133.7 5.7 %collective-permute-start.10 = (f32[264,512]{1,0:T(8,128)S(1)}, f32[264,512]{1,0:T(8,128)}, u32[]{:S(2)}, u32[]{:S(2)}) collective-permute-start(f32[264,512]{1,0:T(8,128)S(1)} %get-tuple-element.24), channel_id=1, source_target_pairs={{0,60},{4,0},{8,4},{12,8},{16,12},{20,16},{24,20},{28,24},{32,28},... | collective-permute-start | bytes 1622024 | tf_op jit(solution)/shard_map/ppermute | solution.py:110
  139.5 1.9 collective-permute-start.9
  141.4 10.0 %collective-permute-done.10 = f32[264,512]{1,0:T(8,128)} collective-permute-done((f32[264,512]{1,0:T(8,128)S(1)}, f32[264,512]{1,0:T(8,128)}, u32[]{:S(2)}, u32[]{:S(2)}) %collective-permute-start.10) | collective-permute-done | bytes 540704 | tf_op jit(solution)/shard_map/ppermute | solution.py:110
  151.4 4.5 %collective-permute-start.11 = (f32[264,512]{1,0:T(8,128)}, f32[264,512]{1,0:T(8,128)S(1)}, u32[]{:S(2)}, u32[]{:S(2)}) collective-permute-start(f32[264,512]{1,0:T(8,128)} %collective-permute-done.10), channel_id=1, source_target_pairs={{0,60},{4,0},{8,4},{12,8},{16,12},{20,16},{24,20},{28,24},{32,28},... | collective-permute-start | bytes 1622024 | tf_op jit(solution)/shard_map/ppermute | solution.py:110
  155.9 2.4 %shard_map.86 = f32[128,256]{1,0:T(8,128)} custom-call(f32[32,4,1280]{2,1,0:T(4,128)S(1)} %all-to-all-done.update_ref), custom_call_target="tpu_custom_call" | custom-call | flops 1073741824 | bytes 786432 | tf_op jit(solution)/shard_map/pallas_call | solution.py:66
  158.4 6.6 %all-to-all-start.1 = ((f32[4,32,256]{2,1,0:T(8,128)}), f32[4,32,256]{2,1,0:T(8,128)S(1)}, u32[]{:S(2)}, u32[]{:S(2)}) async-start(f32[4,32,256]{2,1,0:T(8,128)} %bitcast.38), calls=%async_computation.1 | async-start | bytes 262144 | tf_op jit(solution)/shard_map/all_to_all | solution.py:194
  165.0 0.7 slice.76
  165.7 0.7 slice.75
  166.5 13.6 %all-to-all-done.1 = f32[4,32,256]{2,1,0:T(8,128)S(1)} async-done(((f32[4,32,256]{2,1,0:T(8,128)}), f32[4,32,256]{2,1,0:T(8,128)S(1)}, u32[]{:S(2)}, u32[]{:S(2)}) %all-to-all-start.1) | async-done | bytes 131104 | tf_op jit(solution)/shard_map/all_to_all | solution.py:194
  180.2 0.5 broadcast_in_dim.38
  180.7 23.9 %all_to_all.20 = f32[32,4,2,4,256]{4,2,3,1,0:T(2,128)S(1)} all-to-all(f32[32,4,2,4,256]{4,2,3,1,0:T(2,128)S(1)} %broadcast_in_dim.38), channel_id=1, replica_groups=mesh['front'=8,'row'=16,'col'=4] {'front','col'}, dimensions={0} | all-to-all | bytes 2097152 | tf_op jit(solution)/shard_map/all_to_all | solution.py:24
  205.5 1.4 fusion.10
  206.9 1.5 fusion.1
  208.8 18.4 %all_to_all.21 = f32[4,32,256]{2,1,0:T(8,128)S(1)} all-to-all(f32[4,32,256]{2,1,0:T(8,128)S(1)} %bitcast.128), channel_id=1, replica_groups={{0,16,32,48},{4,20,36,52},{8,24,40,56},{12,28,44,60},{1,17,33,49},{5,21..., dimensions={0} | all-to-all | bytes 262144 | tf_op jit(solution)/shard_map/all_to_all | solution.py:215
  227.2 0.6 reduce_sum.19
  (50 shorter events, 2.6 us)
Async XLA Ops:
  0.6 24.9 %copy-start = (f32[1,1024,256]{2,1,0:T(8,128)S(1)}, f32[1,1024,256]{2,1,0:T(8,128)}, u32[]{:S(2)}) copy-start(f32[1,1024,256]{2,1,0:T(8,128)} %param.8) | copy-start | bytes 3145732
  0.6 42.7 %collective-permute-start.2 = (f32[256,1024]{1,0:T(8,128)}, f32[256,1024]{1,0:T(8,128)}, u32[]{:S(2)}, u32[]{:S(2)}) collective-permute-start(f32[256,1024]{1,0:T(8,128)} %bitcast.119), channel_id=1, source_target_pairs={{0,60},{4,0},{8,4},{12,8},{16,12},{20,16},{24,20},{28,24},{32,28},... | collective-permute-start | bytes 3145736 | tf_op jit(solution)/shard_map/ppermute | solution.py:110
  8.2 35.2 %collective-permute-start.3 = (f32[256,1024]{1,0:T(8,128)}, f32[256,1024]{1,0:T(8,128)}, u32[]{:S(2)}, u32[]{:S(2)}) collective-permute-start(f32[256,1024]{1,0:T(8,128)} %bitcast.120), channel_id=1, source_target_pairs={{0,4},{4,8},{8,12},{12,16},{16,20},{20,24},{24,28},{28,32},{32,36}... | collective-permute-start | bytes 3145736 | tf_op jit(solution)/shard_map/ppermute | solution.py:110
  26.3 17.1 %collective-permute-start.1 = (f32[128,1024]{1,0:T(8,128)S(1)}, f32[128,1024]{1,0:T(8,128)S(1)}, u32[]{:S(2)}, u32[]{:S(2)}) collective-permute-start(f32[128,1024]{1,0:T(8,128)S(1)} %fusion.2), channel_id=1, source_target_pairs={{0,60},{4,0},{8,4},{12,8},{16,12},{20,16},{24,20},{28,24},{32,28},... | collective-permute-start | bytes 1572872 | tf_op jit(solution)/shard_map/ppermute | solution.py:110
  33.9 23.5 %collective-permute-start = (f32[128,1024]{1,0:T(8,128)}, f32[128,1024]{1,0:T(8,128)}, u32[]{:S(2)}, u32[]{:S(2)}) collective-permute-start(f32[128,1024]{1,0:T(8,128)} %fusion.6), channel_id=1, source_target_pairs={{0,4},{4,8},{8,12},{12,16},{16,20},{20,24},{24,28},{28,32},{32,36}... | collective-permute-start | bytes 1572872 | tf_op jit(solution)/shard_map/ppermute | solution.py:110
  35.8 0.8 copy-start.6
  39.2 16.8 %copy-start.2 = (f32[512,512]{1,0:T(8,128)S(1)}, f32[512,512]{1,0:T(8,128)}, u32[]{:S(2)}) copy-start(f32[512,512]{1,0:T(8,128)} %param.12) | copy-start | bytes 3145732
  44.3 13.1 %collective-permute-start.4 = (f32[128,1024]{1,0:T(8,128)}, f32[128,1024]{1,0:T(8,128)}, u32[]{:S(2)}, u32[]{:S(2)}) collective-permute-start(f32[128,1024]{1,0:T(8,128)} %add.255), channel_id=1, source_target_pairs={{0,60},{4,0},{8,4},{12,8},{16,12},{20,16},{24,20},{28,24},{32,28},... | collective-permute-start | bytes 1572872 | tf_op jit(solution)/shard_map/ppermute | solution.py:110
  50.1 42.1 %collective-permute-start.8 = (f32[256,1024]{1,0:T(8,128)}, f32[256,1024]{1,0:T(8,128)}, u32[]{:S(2)}, u32[]{:S(2)}) collective-permute-start(f32[256,1024]{1,0:T(8,128)} %collective-permute-done.2), channel_id=1, source_target_pairs={{0,60},{4,0},{8,4},{12,8},{16,12},{20,16},{24,20},{28,24},{32,28},... | collective-permute-start | bytes 3145736 | tf_op jit(solution)/shard_map/ppermute | solution.py:110
  56.3 1.1 copy-start.5
  59.3 19.0 %copy-start.1 = (f32[256,512]{1,0:T(8,128)S(1)}, f32[256,512]{1,0:T(8,128)}, u32[]{:S(2)}) copy-start(f32[256,512]{1,0:T(8,128)} %param.13) | copy-start | bytes 1572868
  59.4 28.7 %collective-permute-start.5 = (f32[32,1024]{1,0:T(8,128)S(1)}, f32[32,1024]{1,0:T(8,128)S(1)}, u32[]{:S(2)}, u32[]{:S(2)}) collective-permute-start(f32[32,1024]{1,0:T(8,128)S(1)} %get-tuple-element.38), channel_id=1, source_target_pairs={{0,32},{4,36},{8,40},{12,44},{16,48},{20,52},{24,56},{28,60},{32,0... | collective-permute-start | bytes 393224 | tf_op jit(solution)/shard_map/ppermute | solution.py:110
  68.5 19.6 %collective-permute-start.6 = (f32[32,1024]{1,0:T(8,128)S(1)}, f32[32,1024]{1,0:T(8,128)S(1)}, u32[]{:S(2)}, u32[]{:S(2)}) collective-permute-start(f32[32,1024]{1,0:T(8,128)S(1)} %get-tuple-element.37), channel_id=1, source_target_pairs={{0,16},{4,20},{8,24},{12,28},{16,32},{20,36},{24,40},{28,44},{32,4... | collective-permute-start | bytes 393224 | tf_op jit(solution)/shard_map/ppermute | solution.py:110
  73.0 19.3 %collective-permute-start.7 = (f32[32,1024]{1,0:T(8,128)S(1)}, f32[32,1024]{1,0:T(8,128)S(1)}, u32[]{:S(2)}, u32[]{:S(2)}) collective-permute-start(f32[32,1024]{1,0:T(8,128)S(1)} %get-tuple-element.36), channel_id=1, source_target_pairs={{0,48},{4,52},{8,56},{12,60},{16,0},{20,4},{24,8},{28,12},{32,16},... | collective-permute-start | bytes 393224 | tf_op jit(solution)/shard_map/ppermute | solution.py:110
  78.4 40.2 %copy-start.3 = (f32[1,256,1024]{2,1,0:T(8,128)S(1)}, f32[1,256,1024]{2,1,0:T(8,128)}, u32[]{:S(2)}) copy-start(f32[1,256,1024]{2,1,0:T(8,128)} %param.9) | copy-start | bytes 3145732
  92.3 0.7 copy-start.4
  126.0 29.9 %all-to-all-start = ((f32[32,4,1280]{2,1,0:T(4,128)}), f32[32,4,1280]{2,1,0:T(4,128)S(1)}, u32[]{:S(2)}, u32[]{:S(2)}) async-start(f32[32,4,1280]{2,1,0:T(4,128)} %reshape.120), calls=%async_computation | async-start | bytes 1310720 | tf_op jit(solution)/shard_map/all_to_all | solution.py:24
  133.7 17.7 %collective-permute-start.10 = (f32[264,512]{1,0:T(8,128)S(1)}, f32[264,512]{1,0:T(8,128)}, u32[]{:S(2)}, u32[]{:S(2)}) collective-permute-start(f32[264,512]{1,0:T(8,128)S(1)} %get-tuple-element.24), channel_id=1, source_target_pairs={{0,60},{4,0},{8,4},{12,8},{16,12},{20,16},{24,20},{28,24},{32,28},... | collective-permute-start | bytes 1622024 | tf_op jit(solution)/shard_map/ppermute | solution.py:110
  139.5 26.3 %collective-permute-start.9 = (f32[264,512]{1,0:T(8,128)S(1)}, f32[264,512]{1,0:T(8,128)}, u32[]{:S(2)}, u32[]{:S(2)}) collective-permute-start(f32[264,512]{1,0:T(8,128)S(1)} %get-tuple-element.23), channel_id=1, source_target_pairs={{0,4},{4,8},{8,12},{12,16},{16,20},{20,24},{24,28},{28,32},{32,36}... | collective-permute-start | bytes 1622024 | tf_op jit(solution)/shard_map/ppermute | solution.py:110
  151.4 28.7 %collective-permute-start.11 = (f32[264,512]{1,0:T(8,128)}, f32[264,512]{1,0:T(8,128)S(1)}, u32[]{:S(2)}, u32[]{:S(2)}) collective-permute-start(f32[264,512]{1,0:T(8,128)} %collective-permute-done.10), channel_id=1, source_target_pairs={{0,60},{4,0},{8,4},{12,8},{16,12},{20,16},{24,20},{28,24},{32,28},... | collective-permute-start | bytes 1622024 | tf_op jit(solution)/shard_map/ppermute | solution.py:110
  158.4 21.7 %all-to-all-start.1 = ((f32[4,32,256]{2,1,0:T(8,128)}), f32[4,32,256]{2,1,0:T(8,128)S(1)}, u32[]{:S(2)}, u32[]{:S(2)}) async-start(f32[4,32,256]{2,1,0:T(8,128)} %bitcast.38), calls=%async_computation.1 | async-start | bytes 262144 | tf_op jit(solution)/shard_map/all_to_all | solution.py:194

commit v9 on v8

--- a/solution.py
+++ b/solution.py
@@ -155,22 +155,6 @@
     def far_block(offset):
         return lax.dynamic_index_in_dim(near_sum, lax.rem(far_id + offset, far), 0, keepdims=False)
 
-    own = far_block(0)
-    sent = []
-    for offset in sorted(range(1, far), key=lambda offset: -min(offset, far - offset)):
-        sent.append(shift(far_block(offset), near * offset, False))
-    *sent, border_two = lax.optimization_barrier((*sent, border_two))
-    for value in sent:
-        own = own + value
-    pivot_live = col_id * pivot_rows + jnp.arange(pivot_rows, dtype=jnp.int32) < front_sizes[0, 0]
-    own = jnp.where(pivot_live[None, :], own, 0.0)
-
-    apart = [[g + near * i for i in range(far)] for g in range(near)]
-    solved = lax.all_gather(own, "row", axis_index_groups=apart, axis=0, tiled=True)
-    window = (border, border_above, border_below, border_two)
-    update = [contract(solved, value, (1,), (1,)) for value in window]
-    update = jnp.concatenate([*update, code], 1)
-
     share = front_id * cols + col_id
     per_block = layer // far
     root_share = root_rhs.reshape(root_rows, far, near, per_block, part)
@@ -181,8 +165,25 @@
     def share_of(offset):
         return lax.dynamic_index_in_dim(root_share, group_at(offset), 0, keepdims=False)
 
+    own = far_block(0)
+    sent = []
+    for offset in sorted(range(1, far), key=lambda offset: -min(offset, far - offset)):
+        sent.append(shift(far_block(offset), near * offset, False))
+    share_two = shift(share_of(-2), -2, False)
+    *sent, border_two, share_two = lax.optimization_barrier((*sent, border_two, share_two))
+    for value in sent:
+        own = own + value
+    pivot_live = col_id * pivot_rows + jnp.arange(pivot_rows, dtype=jnp.int32) < front_sizes[0, 0]
+    own = jnp.where(pivot_live[None, :], own, 0.0)
+
+    apart = [[g + near * i for i in range(far)] for g in range(near)]
+    solved = lax.all_gather(own, "row", axis_index_groups=apart, axis=0, tiled=True)
+    window = (border, border_above, border_below, border_two)
+    update = [contract(solved, value, (1,), (1,)) for value in window]
+    update = jnp.concatenate([*update, code], 1)
+
     share_rows = root_inverse.shape[0]
-    upward = jnp.concatenate([root_inverse, share_of(-1), share_of(-2)])
+    upward = jnp.concatenate([root_inverse, share_of(-1), share_of(-1)])
     downward = jnp.concatenate([root_inverse, share_of(1), share_of(1)])
     update, upward, downward = lax.optimization_barrier((update, upward, downward))
     update = exchange(update.reshape(layer, part, -1), ("front", "col"))
@@ -194,22 +195,23 @@
     landed = lax.all_to_all(landed, "row", 0, 0, axis_index_groups=apart, tiled=True).sum(0)
     landed = landed.reshape(near, halves, part, high_count)
 
-    twice = shift(upward, -1, False)
     shares = jnp.stack(
         [
             downward[share_rows : share_rows + part],
             share_of(0),
             upward[share_rows : share_rows + part],
-            twice[share_rows + part :],
+            share_two,
         ]
     )
     residual = shares.reshape(near, part, halves, high_count).transpose(0, 2, 1, 3) - landed
+    residual, upward = lax.optimization_barrier((residual, upward))
+    twice = shift(upward[:share_rows], -1, False)
     residual = exchange(
         jnp.broadcast_to(residual[None], (layer, near, halves, part, high_count)), ("front", "col")
     )
     residual = residual.transpose(1, 0, 3, 2, 4).reshape(near, far * block, root_rows)
 
-    window = (downward[:share_rows], root_inverse, upward[:share_rows], twice[:share_rows])
+    window = (downward[:share_rows], root_inverse, upward[:share_rows], twice)
     root = sum(contract(residual[i], value, (1,), (1,)) for i, value in enumerate(window))
     root = root.reshape(far, block, share_rows)
     root = lax.all_to_all(root, "row", 0, 0, axis_index_groups=apart, tiled=True).sum(0)

time: 229 us -> 230 us (level)
  the two profiles are of different devices: /device:TPU:32 before, /device:TPU:2 now
where the time goes in v9:
time: 230 us; the launch traced here: 229 us
  starting transfers between devices  80.2 us (35%)
  blocking collectives  55.7 us (24%)
  waiting for transfers between devices  52.4 us (23%)
  matrix products  18.1 us (8%)
  local copies, waits for them, and re-layouts  12 us (5%)
  other arithmetic  6.74 us (3%)
  Pallas kernels  2.45 us (1%)
    ppermute x13, starting transfers between devices, shift(): return lax.ppermute(value, ('front', 'row'), pairs)  60.4 us
    all_gather x1, blocking collectives, local(): lax.all_gather(own, 'row', axis_index_groups=apart, axis=0, tiled=True)  23.8 us
    ppermute x13, waiting for transfers between devices, shift(): return lax.ppermute(value, ('front', 'row'), pairs)  21 us
    all_to_all x1, blocking collectives, local(): lax.all_to_all(root, 'row', 0, 0, axis_index_groups=apart, tiled=True)  18.5 us
    dot_general x12, matrix products, contract(): lax.dot_general(left, right, ((left_dims, right_dims), ((), ())), precisi...  18.1 us
    all_to_all x2, waiting for transfers between devices, exchange(): return lax.all_to_all(blocks, axes, split_axis=0, concat_axis=0, tiled=True)  17.5 us
    all_to_all x1, waiting for transfers between devices, local(): lax.all_to_all(landed, 'row', 0, 0, axis_index_groups=apart, tiled=True)  13.9 us
    all_gather x1, blocking collectives, local(): rhs = lax.all_gather(rhs, 'col', axis=1, tiled=True)  13.3 us
  transfers between devices with their start and end apart: 16, of which 6 were waited for; matrix products, arithmetic and copies ran while one was open for 8% of the time, Pallas kernels for 1%

profile of v9, /device:TPU:2, one launch (start us, length us, event | category | flops | bytes accessed | tf_op | source)
XLA Modules:
  0.0 228.8 jit_solution(6259092279060038631)
XLA Ops:
  0.6 4.0 %collective-permute-start.3 = (f32[256,1024]{1,0:T(8,128)}, f32[256,1024]{1,0:T(8,128)}, u32[]{:S(2)}, u32[]{:S(2)}) collective-permute-start(f32[256,1024]{1,0:T(8,128)} %bitcast.120), channel_id=1, source_target_pairs={{0,4},{4,8},{8,12},{12,16},{16,20},{20,24},{24,28},{28,32},{32,36}... | collective-permute-start | bytes 3145736 | tf_op jit(solution)/shard_map/ppermute | solution.py:110
  4.6 9.4 %collective-permute-start.2 = (f32[256,1024]{1,0:T(8,128)}, f32[256,1024]{1,0:T(8,128)}, u32[]{:S(2)}, u32[]{:S(2)}) collective-permute-start(f32[256,1024]{1,0:T(8,128)} %bitcast.121), channel_id=1, source_target_pairs={{0,60},{4,0},{8,4},{12,8},{16,12},{20,16},{24,20},{28,24},{32,28},... | collective-permute-start | bytes 3145736 | tf_op jit(solution)/shard_map/ppermute | solution.py:110
  14.0 1.0 copy.18
  15.3 13.3 %all_gather.6 = f32[4,256,128]{2,0,1:T(4,128)S(1)} all-gather(f32[4,64,128]{2,0,1:T(4,128)S(1)} %copy.20), channel_id=1, replica_groups=mesh['front'=8,'row'=16,'col'=4] {'col'}, dimensions={1}, use_global_device_ids=true | all-gather | bytes 655360 | tf_op jit(solution)/shard_map/all_gather | solution.py:138
  29.0 1.5 fusion.6
  30.5 2.0 collective-permute-start
  32.6 1.5 fusion.2
  34.1 5.1 %collective-permute-start.1 = (f32[128,1024]{1,0:T(8,128)}, f32[128,1024]{1,0:T(8,128)}, u32[]{:S(2)}, u32[]{:S(2)}) collective-permute-start(f32[128,1024]{1,0:T(8,128)} %fusion.2), channel_id=1, source_target_pairs={{0,60},{4,0},{8,4},{12,8},{16,12},{20,16},{24,20},{28,24},{32,28},... | collective-permute-start | bytes 1572872 | tf_op jit(solution)/shard_map/ppermute | solution.py:110
  40.5 3.1 %collective-permute-start.9 = (f32[4,512]{1,0:T(4,128)}, f32[4,512]{1,0:T(4,128)}, u32[]{:S(2)}, u32[]{:S(2)}) collective-permute-start(f32[4,512]{1,0:T(4,128)} %get-tuple-element.39), channel_id=1, source_target_pairs={{0,56},{4,60},{8,0},{12,4},{16,8},{20,12},{24,16},{28,20},{32,24},... | collective-permute-start | bytes 24584 | tf_op jit(solution)/shard_map/ppermute | solution.py:110
  45.0 0.7 constant_dynamic-slice_fusion.4
  46.4 0.7 fusion.4
  47.1 1.1 add.258
  48.2 5.0 %collective-permute-start.4 = (f32[128,1024]{1,0:T(8,128)S(1)}, f32[128,1024]{1,0:T(8,128)S(1)}, u32[]{:S(2)}, u32[]{:S(2)}) collective-permute-start(f32[128,1024]{1,0:T(8,128)S(1)} %add.258), channel_id=1, source_target_pairs={{0,60},{4,0},{8,4},{12,8},{16,12},{20,16},{24,20},{28,24},{32,28},... | collective-permute-start | bytes 1572872 | tf_op jit(solution)/shard_map/ppermute | solution.py:110
  53.2 3.3 %collective-permute-start.8 = (f32[256,1024]{1,0:T(8,128)}, f32[256,1024]{1,0:T(8,128)}, u32[]{:S(2)}, u32[]{:S(2)}) collective-permute-start(f32[256,1024]{1,0:T(8,128)} %collective-permute-done.2), channel_id=1, source_target_pairs={{0,60},{4,0},{8,4},{12,8},{16,12},{20,16},{24,20},{28,24},{32,28},... | collective-permute-start | bytes 3145736 | tf_op jit(solution)/shard_map/ppermute | solution.py:110
  57.3 2.6 %collective-permute-done.4 = f32[128,1024]{1,0:T(8,128)S(1)} collective-permute-done((f32[128,1024]{1,0:T(8,128)S(1)}, f32[128,1024]{1,0:T(8,128)S(1)}, u32[]{:S(2)}, u32[]{:S(2)}) %collective-permute-start.4) | collective-permute-done | bytes 524320 | tf_op jit(solution)/shard_map/ppermute | solution.py:110
  59.9 1.7 fusion
  61.6 0.8 dynamic-slice_bitcast_fusion
  62.4 6.5 %collective-permute-start.7 = (f32[32,1024]{1,0:T(8,128)}, f32[32,1024]{1,0:T(8,128)S(1)}, u32[]{:S(2)}, u32[]{:S(2)}) collective-permute-start(f32[32,1024]{1,0:T(8,128)} %get-tuple-element.42), channel_id=1, source_target_pairs={{0,48},{4,52},{8,56},{12,60},{16,0},{20,4},{24,8},{28,12},{32,16},... | collective-permute-start | bytes 393224 | tf_op jit(solution)/shard_map/ppermute | solution.py:110
  68.8 3.3 %collective-permute-start.6 = (f32[32,1024]{1,0:T(8,128)}, f32[32,1024]{1,0:T(8,128)}, u32[]{:S(2)}, u32[]{:S(2)}) collective-permute-start(f32[32,1024]{1,0:T(8,128)} %get-tuple-element.43), channel_id=1, source_target_pairs={{0,16},{4,20},{8,24},{12,28},{16,32},{20,36},{24,40},{28,44},{32,4... | collective-permute-start | bytes 393224 | tf_op jit(solution)/shard_map/ppermute | solution.py:110
  72.1 9.8 %collective-permute-start.5 = (f32[32,1024]{1,0:T(8,128)}, f32[32,1024]{1,0:T(8,128)}, u32[]{:S(2)}, u32[]{:S(2)}) collective-permute-start(f32[32,1024]{1,0:T(8,128)} %get-tuple-element.44), channel_id=1, source_target_pairs={{0,32},{4,36},{8,40},{12,44},{16,48},{20,52},{24,56},{28,60},{32,0... | collective-permute-start | bytes 393224 | tf_op jit(solution)/shard_map/ppermute | solution.py:110
  82.0 1.2 pad_maximum_fusion.1
  83.1 0.8 add_compare_fusion
  84.0 8.4 %collective-permute-done.7 = f32[32,1024]{1,0:T(8,128)S(1)} collective-permute-done((f32[32,1024]{1,0:T(8,128)}, f32[32,1024]{1,0:T(8,128)S(1)}, u32[]{:S(2)}, u32[]{:S(2)}) %collective-permute-start.7) | collective-permute-done | bytes 131104 | tf_op jit(solution)/shard_map/ppermute | solution.py:110
  92.4 10.0 %collective-permute-done.5 = f32[32,1024]{1,0:T(8,128)} collective-permute-done((f32[32,1024]{1,0:T(8,128)}, f32[32,1024]{1,0:T(8,128)}, u32[]{:S(2)}, u32[]{:S(2)}) %collective-permute-start.5) | collective-permute-done | bytes 131104 | tf_op jit(solution)/shard_map/ppermute | solution.py:110
  102.4 1.0 fusion.12
  103.5 23.8 %all_gather.7 = f32[128,1024]{1,0:T(8,128)S(1)} all-gather(f32[32,1024]{1,0:T(8,128)S(1)} %fusion.12), channel_id=1, replica_groups={{0,16,32,48},{4,20,36,52},{8,24,40,56},{12,28,44,60},{1,17,33,49},{5,21..., dimensions={0}, use_global_device_ids=true | all-gather | bytes 655360 | tf_op jit(solution)/shard_map/all_gather | solution.py:180
  127.3 1.3 convolution_dynamic-update-slice_fusion.3
  128.6 2.6 %convolution_dynamic-update-slice_fusion.2 = f32[128,1280]{1,0:T(8,128)} fusion(f32[128,1280]{1,0:T(8,128)} %convolution_dynamic-update-slice_fusion.3, f32[128,1024]{1,0:T(8,128)S(1)} %all_gather.7, f32[256,1024]{1,0:T(8,128)} %collective-permute-done.2), kind=kOutput, calls=%fused_computation.4 | convolution fusion | flops 201326592 | bytes 1703936 | tf_op jit(solution)/shard_map/dot_general | solution.py:14
  131.2 2.6 %convolution_dynamic-update-slice_fusion.1 = f32[128,1280]{1,0:T(8,128)} fusion(f32[128,1280]{1,0:T(8,128)} %convolution_dynamic-update-slice_fusion.2, f32[128,1024]{1,0:T(8,128)S(1)} %all_gather.7, f32[256,1024]{1,0:T(8,128)} %collective-permute-done.3), kind=kOutput, calls=%fused_computation.3 | convolution fusion | flops 201326592 | bytes 1703936 | tf_op jit(solution)/shard_map/dot_general | solution.py:14
  133.7 2.5 %convolution_dynamic-update-slice_fusion = f32[128,1280]{1,0:T(8,128)} fusion(f32[128,1280]{1,0:T(8,128)} %convolution_dynamic-update-slice_fusion.1, f32[128,1024]{1,0:T(8,128)S(1)} %all_gather.7, f32[256,1024]{1,0:T(8,128)} %collective-permute-done.8), kind=kOutput, calls=%fused_computation.2 | convolution fusion | flops 201326592 | bytes 1703936 | tf_op jit(solution)/shard_map/dot_general | solution.py:14
  136.9 2.1 reshape.120
  139.0 6.6 %all-to-all-start = ((f32[32,4,1280]{2,1,0:T(4,128)}), f32[32,4,1280]{2,1,0:T(4,128)S(1)}, u32[]{:S(2)}, u32[]{:S(2)}) async-start(f32[32,4,1280]{2,1,0:T(4,128)} %reshape.120), calls=%async_computation | async-start | bytes 1310720 | tf_op jit(solution)/shard_map/all_to_all | solution.py:24
  145.7 2.7 %collective-permute-start.10 = (f32[264,512]{1,0:T(8,128)}, f32[264,512]{1,0:T(8,128)}, u32[]{:S(2)}, u32[]{:S(2)}) collective-permute-start(f32[264,512]{1,0:T(8,128)} %get-tuple-element.26), channel_id=1, source_target_pairs={{0,4},{4,8},{8,12},{12,16},{16,20},{20,24},{24,28},{28,32},{32,36}... | collective-permute-start | bytes 1622024 | tf_op jit(solution)/shard_map/ppermute | solution.py:110
  148.4 4.3 %collective-permute-start.11 = (f32[264,512]{1,0:T(8,128)S(1)}, f32[264,512]{1,0:T(8,128)S(1)}, u32[]{:S(2)}, u32[]{:S(2)}) collective-permute-start(f32[264,512]{1,0:T(8,128)S(1)} %copy-done.4), channel_id=1, source_target_pairs={{0,60},{4,0},{8,4},{12,8},{16,12},{20,16},{24,20},{28,24},{32,28},... | collective-permute-start | bytes 1622024 | tf_op jit(solution)/shard_map/ppermute | solution.py:110
  152.7 4.4 %all-to-all-done.update_ref = f32[32,4,1280]{2,1,0:T(4,128)S(1)} async-done(((f32[32,4,1280]{2,1,0:T(4,128)}), f32[32,4,1280]{2,1,0:T(4,128)S(1)}, u32[]{:S(2)}, u32[]{:S(2)}) %all-to-all-start) | async-done | bytes 655392 | tf_op jit(solution)/shard_map/all_to_all | solution.py:24
  157.2 2.4 %shard_map.86 = f32[128,256]{1,0:T(8,128)} custom-call(f32[32,4,1280]{2,1,0:T(4,128)S(1)} %all-to-all-done.update_ref), custom_call_target="tpu_custom_call" | custom-call | flops 1073741824 | bytes 786432 | tf_op jit(solution)/shard_map/pallas_call | solution.py:66
  159.6 6.8 %all-to-all-start.1 = ((f32[4,32,256]{2,1,0:T(8,128)}), f32[4,32,256]{2,1,0:T(8,128)S(1)}, u32[]{:S(2)}, u32[]{:S(2)}) async-start(f32[4,32,256]{2,1,0:T(8,128)} %bitcast.38), calls=%async_computation.1 | async-start | bytes 262144 | tf_op jit(solution)/shard_map/all_to_all | solution.py:195
  166.4 0.7 slice.68
  167.1 13.9 %all-to-all-done.1 = f32[4,32,256]{2,1,0:T(8,128)S(1)} async-done(((f32[4,32,256]{2,1,0:T(8,128)}), f32[4,32,256]{2,1,0:T(8,128)S(1)}, u32[]{:S(2)}, u32[]{:S(2)}) %all-to-all-start.1) | async-done | bytes 131104 | tf_op jit(solution)/shard_map/all_to_all | solution.py:195
  181.0 0.7 fusion.13
  181.7 1.4 broadcast_in_dim.38
  183.2 6.4 %all-to-all-start.2 = ((f32[32,4,2,4,256]{4,2,3,1,0:T(2,128)}), f32[32,4,2,4,256]{4,2,3,1,0:T(2,128)S(1)}, u32[]{:S(2)}, u32[]{:S(2)}) async-start(f32[32,4,2,4,256]{4,2,3,1,0:T(2,128)} %broadcast_in_dim.38), calls=%async_computation.2 | async-start | bytes 2097152 | tf_op jit(solution)/shard_map/all_to_all | solution.py:24
  189.6 0.9 slice.62
  190.4 1.9 collective-permute-start.12
  192.3 13.1 %all-to-all-done.2 = f32[32,4,2,4,256]{4,2,3,1,0:T(2,128)S(1)} async-done(((f32[32,4,2,4,256]{4,2,3,1,0:T(2,128)}), f32[32,4,2,4,256]{4,2,3,1,0:T(2,128)S(1)}, u32[]{:S(2)}, u32[]{:S(2)}) %all-to-all-start.2) | async-done | bytes 1048608 | tf_op jit(solution)/shard_map/all_to_all | solution.py:24
  206.8 1.5 fusion.1
  208.2 1.4 convolution_add_fusion.1
  209.7 18.5 %all_to_all.20 = f32[4,32,256]{2,1,0:T(8,128)S(1)} all-to-all(f32[4,32,256]{2,1,0:T(8,128)S(1)} %bitcast.129), channel_id=1, replica_groups={{0,16,32,48},{4,20,36,52},{8,24,40,56},{12,28,44,60},{1,17,33,49},{5,21..., dimensions={0} | all-to-all | bytes 262144 | tf_op jit(solution)/shard_map/all_to_all | solution.py:217
  (53 shorter events, 7.2 us)
Async XLA Ops:
  0.6 28.4 %copy-start = (f32[1,1024,256]{2,1,0:T(8,128)S(1)}, f32[1,1024,256]{2,1,0:T(8,128)}, u32[]{:S(2)}) copy-start(f32[1,1024,256]{2,1,0:T(8,128)} %param.8) | copy-start | bytes 3145732
  0.6 46.4 %collective-permute-start.3 = (f32[256,1024]{1,0:T(8,128)}, f32[256,1024]{1,0:T(8,128)}, u32[]{:S(2)}, u32[]{:S(2)}) collective-permute-start(f32[256,1024]{1,0:T(8,128)} %bitcast.120), channel_id=1, source_target_pairs={{0,4},{4,8},{8,12},{12,16},{16,20},{20,24},{24,28},{28,32},{32,36}... | collective-permute-start | bytes 3145736 | tf_op jit(solution)/shard_map/ppermute | solution.py:110
  4.6 42.5 %collective-permute-start.2 = (f32[256,1024]{1,0:T(8,128)}, f32[256,1024]{1,0:T(8,128)}, u32[]{:S(2)}, u32[]{:S(2)}) collective-permute-start(f32[256,1024]{1,0:T(8,128)} %bitcast.121), channel_id=1, source_target_pairs={{0,60},{4,0},{8,4},{12,8},{16,12},{20,16},{24,20},{28,24},{32,28},... | collective-permute-start | bytes 3145736 | tf_op jit(solution)/shard_map/ppermute | solution.py:110
  30.5 8.7 %copy-start.2 = (f32[512,512]{1,0:T(8,128)S(1)}, f32[512,512]{1,0:T(8,128)}, u32[]{:S(2)}) copy-start(f32[512,512]{1,0:T(8,128)} %param.12) | copy-start | bytes 3145732
  30.5 26.7 %collective-permute-start = (f32[128,1024]{1,0:T(8,128)}, f32[128,1024]{1,0:T(8,128)}, u32[]{:S(2)}, u32[]{:S(2)}) collective-permute-start(f32[128,1024]{1,0:T(8,128)} %fusion.6), channel_id=1, source_target_pairs={{0,4},{4,8},{8,12},{12,16},{16,20},{20,24},{24,28},{28,32},{32,36}... | collective-permute-start | bytes 1572872 | tf_op jit(solution)/shard_map/ppermute | solution.py:110
  34.1 13.0 %collective-permute-start.1 = (f32[128,1024]{1,0:T(8,128)}, f32[128,1024]{1,0:T(8,128)}, u32[]{:S(2)}, u32[]{:S(2)}) collective-permute-start(f32[128,1024]{1,0:T(8,128)} %fusion.2), channel_id=1, source_target_pairs={{0,60},{4,0},{8,4},{12,8},{16,12},{20,16},{24,20},{28,24},{32,28},... | collective-permute-start | bytes 1572872 | tf_op jit(solution)/shard_map/ppermute | solution.py:110
  40.5 43.5 %collective-permute-start.9 = (f32[4,512]{1,0:T(4,128)}, f32[4,512]{1,0:T(4,128)}, u32[]{:S(2)}, u32[]{:S(2)}) collective-permute-start(f32[4,512]{1,0:T(4,128)} %get-tuple-element.39), channel_id=1, source_target_pairs={{0,56},{4,60},{8,0},{12,4},{16,8},{20,12},{24,16},{28,20},{32,24},... | collective-permute-start | bytes 24584 | tf_op jit(solution)/shard_map/ppermute | solution.py:110
  43.7 0.7 copy-start.6
  48.2 11.6 %collective-permute-start.4 = (f32[128,1024]{1,0:T(8,128)S(1)}, f32[128,1024]{1,0:T(8,128)S(1)}, u32[]{:S(2)}, u32[]{:S(2)}) collective-permute-start(f32[128,1024]{1,0:T(8,128)S(1)} %add.258), channel_id=1, source_target_pairs={{0,60},{4,0},{8,4},{12,8},{16,12},{20,16},{24,20},{28,24},{32,28},... | collective-permute-start | bytes 1572872 | tf_op jit(solution)/shard_map/ppermute | solution.py:110
  53.2 49.3 %collective-permute-start.8 = (f32[256,1024]{1,0:T(8,128)}, f32[256,1024]{1,0:T(8,128)}, u32[]{:S(2)}, u32[]{:S(2)}) collective-permute-start(f32[256,1024]{1,0:T(8,128)} %collective-permute-done.2), channel_id=1, source_target_pairs={{0,60},{4,0},{8,4},{12,8},{16,12},{20,16},{24,20},{28,24},{32,28},... | collective-permute-start | bytes 3145736 | tf_op jit(solution)/shard_map/ppermute | solution.py:110
  61.6 20.4 %copy-start.1 = (f32[256,512]{1,0:T(8,128)S(1)}, f32[256,512]{1,0:T(8,128)}, u32[]{:S(2)}) copy-start(f32[256,512]{1,0:T(8,128)} %param.13) | copy-start | bytes 1572868
  62.4 30.1 %collective-permute-start.7 = (f32[32,1024]{1,0:T(8,128)}, f32[32,1024]{1,0:T(8,128)S(1)}, u32[]{:S(2)}, u32[]{:S(2)}) collective-permute-start(f32[32,1024]{1,0:T(8,128)} %get-tuple-element.42), channel_id=1, source_target_pairs={{0,48},{4,52},{8,56},{12,60},{16,0},{20,4},{24,8},{28,12},{32,16},... | collective-permute-start | bytes 393224 | tf_op jit(solution)/shard_map/ppermute | solution.py:110
  68.8 23.6 %collective-permute-start.6 = (f32[32,1024]{1,0:T(8,128)}, f32[32,1024]{1,0:T(8,128)}, u32[]{:S(2)}, u32[]{:S(2)}) collective-permute-start(f32[32,1024]{1,0:T(8,128)} %get-tuple-element.43), channel_id=1, source_target_pairs={{0,16},{4,20},{8,24},{12,28},{16,32},{20,36},{24,40},{28,44},{32,4... | collective-permute-start | bytes 393224 | tf_op jit(solution)/shard_map/ppermute | solution.py:110
  72.1 30.3 %collective-permute-start.5 = (f32[32,1024]{1,0:T(8,128)}, f32[32,1024]{1,0:T(8,128)}, u32[]{:S(2)}, u32[]{:S(2)}) collective-permute-start(f32[32,1024]{1,0:T(8,128)} %get-tuple-element.44), channel_id=1, source_target_pairs={{0,32},{4,36},{8,40},{12,44},{16,48},{20,52},{24,56},{28,60},{32,0... | collective-permute-start | bytes 393224 | tf_op jit(solution)/shard_map/ppermute | solution.py:110
  83.1 44.1 %copy-start.3 = (f32[1,256,1024]{2,1,0:T(8,128)S(1)}, f32[1,256,1024]{2,1,0:T(8,128)}, u32[]{:S(2)}) copy-start(f32[1,256,1024]{2,1,0:T(8,128)} %param.9) | copy-start | bytes 3145732
  103.4 23.8 %copy-start.5 = (f32[32,1024]{1,0:T(8,128)}, f32[32,1024]{1,0:T(8,128)S(1)}, u32[]{:S(2)}) copy-start(f32[32,1024]{1,0:T(8,128)S(1)} %fusion.12) | copy-start | bytes 393220
  139.0 9.3 %copy-start.4 = (f32[264,512]{1,0:T(8,128)S(1)}, f32[264,512]{1,0:T(8,128)}, u32[]{:S(2)}) copy-start(f32[264,512]{1,0:T(8,128)} %get-tuple-element.27) | copy-start | bytes 1622020
  139.0 18.1 %all-to-all-start = ((f32[32,4,1280]{2,1,0:T(4,128)}), f32[32,4,1280]{2,1,0:T(4,128)S(1)}, u32[]{:S(2)}, u32[]{:S(2)}) async-start(f32[32,4,1280]{2,1,0:T(4,128)} %reshape.120), calls=%async_computation | async-start | bytes 1310720 | tf_op jit(solution)/shard_map/all_to_all | solution.py:24
  145.7 20.7 %collective-permute-start.10 = (f32[264,512]{1,0:T(8,128)}, f32[264,512]{1,0:T(8,128)}, u32[]{:S(2)}, u32[]{:S(2)}) collective-permute-start(f32[264,512]{1,0:T(8,128)} %get-tuple-element.26), channel_id=1, source_target_pairs={{0,4},{4,8},{8,12},{12,16},{16,20},{20,24},{24,28},{28,32},{32,36}... | collective-permute-start | bytes 1622024 | tf_op jit(solution)/shard_map/ppermute | solution.py:110
  148.4 18.7 %collective-permute-start.11 = (f32[264,512]{1,0:T(8,128)S(1)}, f32[264,512]{1,0:T(8,128)S(1)}, u32[]{:S(2)}, u32[]{:S(2)}) collective-permute-start(f32[264,512]{1,0:T(8,128)S(1)} %copy-done.4), channel_id=1, source_target_pairs={{0,60},{4,0},{8,4},{12,8},{16,12},{20,16},{24,20},{28,24},{32,28},... | collective-permute-start | bytes 1622024 | tf_op jit(solution)/shard_map/ppermute | solution.py:110
  159.6 21.4 %all-to-all-start.1 = ((f32[4,32,256]{2,1,0:T(8,128)}), f32[4,32,256]{2,1,0:T(8,128)S(1)}, u32[]{:S(2)}, u32[]{:S(2)}) async-start(f32[4,32,256]{2,1,0:T(8,128)} %bitcast.38), calls=%async_computation.1 | async-start | bytes 262144 | tf_op jit(solution)/shard_map/all_to_all | solution.py:195
  183.2 22.2 %all-to-all-start.2 = ((f32[32,4,2,4,256]{4,2,3,1,0:T(2,128)}), f32[32,4,2,4,256]{4,2,3,1,0:T(2,128)S(1)}, u32[]{:S(2)}, u32[]{:S(2)}) async-start(f32[32,4,2,4,256]{4,2,3,1,0:T(2,128)} %broadcast_in_dim.38), calls=%async_computation.2 | async-start | bytes 2097152 | tf_op jit(solution)/shard_map/all_to_all | solution.py:24
  190.4 17.8 %collective-permute-start.12 = (f32[256,512]{1,0:T(8,128)}, f32[256,512]{1,0:T(8,128)}, u32[]{:S(2)}, u32[]{:S(2)}) collective-permute-start(f32[256,512]{1,0:T(8,128)} %slice.62), channel_id=1, source_target_pairs={{0,60},{4,0},{8,4},{12,8},{16,12},{20,16},{24,20},{28,24},{32,28},... | collective-permute-start | bytes 1572872 | tf_op jit(solution)/shard_map/ppermute | solution.py:110

commit v10 on v8

--- a/solution.py
+++ b/solution.py
@@ -190,11 +190,12 @@
     downward = shift(downward, 1, False)
 
     landed = land(update, near * border_rows, fronts, cols, low_count, high_count)
+    landed, upward = lax.optimization_barrier((landed, upward))
+    twice = shift(upward, -1, False)
     landed = landed.reshape(far, near * halves * part, high_count)
     landed = lax.all_to_all(landed, "row", 0, 0, axis_index_groups=apart, tiled=True).sum(0)
     landed = landed.reshape(near, halves, part, high_count)
 
-    twice = shift(upward, -1, False)
     shares = jnp.stack(
         [
             downward[share_rows : share_rows + part],

time: 229 us -> 230 us (level)
  blocking collectives: 81.1 us -> 84.1 us
  waiting for transfers between devices: 41.7 us -> 39.2 us
    ppermute x12, waiting for transfers between devices: 28 us -> 20.2 us  [shift(): return lax.ppermute(value, ('front', 'row'), pairs)]
    all_to_all x1, waiting for transfers between devices: 0.01 us -> 5.42 us  [exchange(): return lax.all_to_all(blocks, axes, split_axis=0, concat_axis=0, tiled=True)]
    all_to_all x1, blocking collectives: 18.4 us -> 21.2 us  [local(): lax.all_to_all(root, 'row', 0, 0, axis_index_groups=apart, tiled=True)]
  transfers between devices with their start and end apart: 14 -> 14, of which waited for: 5 -> 6; matrix products, arithmetic and copies ran while one was open for 6% -> 6% of each run, Pallas kernels for 1% -> 1%
where the time goes in v10:
time: 230 us; the launch traced here: 228 us
  blocking collectives  84.1 us (37%)
  starting transfers between devices  74.3 us (32%)
  waiting for transfers between devices  39.2 us (17%)
  matrix products  14.8 us (6%)
  local copies, waits for them, and re-layouts  8.48 us (4%)
  other arithmetic  3.65 us (2%)
  Pallas kernels  2.45 us (1%)
    ppermute x12, starting transfers between devices, shift(): return lax.ppermute(value, ('front', 'row'), pairs)  60 us
    all_gather x1, blocking collectives, local(): lax.all_gather(own, 'row', axis_index_groups=apart, axis=0, tiled=True)  25.7 us
    all_to_all x1, blocking collectives, exchange(): return lax.all_to_all(blocks, axes, split_axis=0, concat_axis=0, tiled=True)  24 us
    all_to_all x1, blocking collectives, local(): lax.all_to_all(root, 'row', 0, 0, axis_index_groups=apart, tiled=True)  21.2 us
    ppermute x12, waiting for transfers between devices, shift(): return lax.ppermute(value, ('front', 'row'), pairs)  20.2 us
    dot_general x12, matrix products, contract(): lax.dot_general(left, right, ((left_dims, right_dims), ((), ())), precisi...  14.8 us
    all_to_all x1, waiting for transfers between devices, local(): lax.all_to_all(landed, 'row', 0, 0, axis_index_groups=apart, tiled=True)  13.6 us
    all_gather x1, blocking collectives, local(): rhs = lax.all_gather(rhs, 'col', axis=1, tiled=True)  13.1 us
  transfers between devices with their start and end apart: 14, of which 6 were waited for; matrix products, arithmetic and copies ran while one was open for 6% of the time, Pallas kernels for 1%

profile of v10, /device:TPU:32, one launch (start us, length us, event | category | flops | bytes accessed | tf_op | source)
XLA Modules:
  0.0 228.4 jit_solution(7667682010515771088)
XLA Ops:
  0.6 7.5 %collective-permute-start.2 = (f32[256,1024]{1,0:T(8,128)}, f32[256,1024]{1,0:T(8,128)}, u32[]{:S(2)}, u32[]{:S(2)}) collective-permute-start(f32[256,1024]{1,0:T(8,128)} %bitcast.119), channel_id=1, source_target_pairs={{0,60},{4,0},{8,4},{12,8},{16,12},{20,16},{24,20},{28,24},{32,28},... | collective-permute-start | bytes 3145736 | tf_op jit(solution)/shard_map/ppermute | solution.py:110
  8.2 1.9 collective-permute-start.3
  10.1 1.0 copy.18
  11.4 13.1 %all_gather.6 = f32[4,256,128]{2,0,1:T(4,128)S(1)} all-gather(f32[4,64,128]{2,0,1:T(4,128)S(1)} %copy.20), channel_id=1, replica_groups=mesh['front'=8,'row'=16,'col'=4] {'col'}, dimensions={1}, use_global_device_ids=true | all-gather | bytes 655360 | tf_op jit(solution)/shard_map/all_gather | solution.py:138
  24.5 1.0 fusion.28
  25.5 0.7 fusion.2
  26.3 6.1 %collective-permute-start.1 = (f32[128,1024]{1,0:T(8,128)S(1)}, f32[128,1024]{1,0:T(8,128)S(1)}, u32[]{:S(2)}, u32[]{:S(2)}) collective-permute-start(f32[128,1024]{1,0:T(8,128)S(1)} %fusion.2), channel_id=1, source_target_pairs={{0,60},{4,0},{8,4},{12,8},{16,12},{20,16},{24,20},{28,24},{32,28},... | collective-permute-start | bytes 1572872 | tf_op jit(solution)/shard_map/ppermute | solution.py:110
  32.4 1.5 fusion.6
  33.9 1.9 collective-permute-start
  35.8 0.7 constant_dynamic-slice_fusion.4
  36.6 0.6 fusion.29
  37.2 0.6 compare_select_fusion
  37.8 0.7 compare_select_fusion.2
  38.5 0.7 fusion.4
  39.2 4.2 %collective-permute-done.1 = f32[128,1024]{1,0:T(8,128)S(1)} collective-permute-done((f32[128,1024]{1,0:T(8,128)S(1)}, f32[128,1024]{1,0:T(8,128)S(1)}, u32[]{:S(2)}, u32[]{:S(2)}) %collective-permute-start.1) | collective-permute-done | bytes 524320 | tf_op jit(solution)/shard_map/ppermute | solution.py:110
  43.4 0.9 add.255
  44.3 5.9 %collective-permute-start.4 = (f32[128,1024]{1,0:T(8,128)}, f32[128,1024]{1,0:T(8,128)}, u32[]{:S(2)}, u32[]{:S(2)}) collective-permute-start(f32[128,1024]{1,0:T(8,128)} %add.255), channel_id=1, source_target_pairs={{0,60},{4,0},{8,4},{12,8},{16,12},{20,16},{24,20},{28,24},{32,28},... | collective-permute-start | bytes 1572872 | tf_op jit(solution)/shard_map/ppermute | solution.py:110
  50.1 5.6 %collective-permute-start.8 = (f32[256,1024]{1,0:T(8,128)}, f32[256,1024]{1,0:T(8,128)}, u32[]{:S(2)}, u32[]{:S(2)}) collective-permute-start(f32[256,1024]{1,0:T(8,128)} %collective-permute-done.2), channel_id=1, source_target_pairs={{0,60},{4,0},{8,4},{12,8},{16,12},{20,16},{24,20},{28,24},{32,28},... | collective-permute-start | bytes 3145736 | tf_op jit(solution)/shard_map/ppermute | solution.py:110
  56.7 0.6 add_compare_fusion
  57.4 1.9 fusion
  59.4 9.1 %collective-permute-start.5 = (f32[32,1024]{1,0:T(8,128)S(1)}, f32[32,1024]{1,0:T(8,128)S(1)}, u32[]{:S(2)}, u32[]{:S(2)}) collective-permute-start(f32[32,1024]{1,0:T(8,128)S(1)} %get-tuple-element.42), channel_id=1, source_target_pairs={{0,32},{4,36},{8,40},{12,44},{16,48},{20,52},{24,56},{28,60},{32,0... | collective-permute-start | bytes 393224 | tf_op jit(solution)/shard_map/ppermute | solution.py:110
  68.5 4.5 %collective-permute-start.6 = (f32[32,1024]{1,0:T(8,128)S(1)}, f32[32,1024]{1,0:T(8,128)S(1)}, u32[]{:S(2)}, u32[]{:S(2)}) collective-permute-start(f32[32,1024]{1,0:T(8,128)S(1)} %get-tuple-element.41), channel_id=1, source_target_pairs={{0,16},{4,20},{8,24},{12,28},{16,32},{20,36},{24,40},{28,44},{32,4... | collective-permute-start | bytes 393224 | tf_op jit(solution)/shard_map/ppermute | solution.py:110
  73.0 5.3 %collective-permute-start.7 = (f32[32,1024]{1,0:T(8,128)S(1)}, f32[32,1024]{1,0:T(8,128)S(1)}, u32[]{:S(2)}, u32[]{:S(2)}) collective-permute-start(f32[32,1024]{1,0:T(8,128)S(1)} %get-tuple-element.40), channel_id=1, source_target_pairs={{0,48},{4,52},{8,56},{12,60},{16,0},{20,4},{24,8},{28,12},{32,16},... | collective-permute-start | bytes 393224 | tf_op jit(solution)/shard_map/ppermute | solution.py:110
  78.4 9.7 %collective-permute-done.5 = f32[32,1024]{1,0:T(8,128)S(1)} collective-permute-done((f32[32,1024]{1,0:T(8,128)S(1)}, f32[32,1024]{1,0:T(8,128)S(1)}, u32[]{:S(2)}, u32[]{:S(2)}) %collective-permute-start.5) | collective-permute-done | bytes 131104 | tf_op jit(solution)/shard_map/ppermute | solution.py:110
  88.1 4.2 %collective-permute-done.7 = f32[32,1024]{1,0:T(8,128)S(1)} collective-permute-done((f32[32,1024]{1,0:T(8,128)S(1)}, f32[32,1024]{1,0:T(8,128)S(1)}, u32[]{:S(2)}, u32[]{:S(2)}) %collective-permute-start.7) | collective-permute-done | bytes 131104 | tf_op jit(solution)/shard_map/ppermute | solution.py:110
  92.3 0.6 copy-done.4
  92.9 25.7 %all_gather.7 = f32[128,1024]{1,0:T(8,128)S(1)} all-gather(f32[32,1024]{1,0:T(8,128)S(1)} %fusion.15), channel_id=1, replica_groups={{0,16,32,48},{4,20,36,52},{8,24,40,56},{12,28,44,60},{1,17,33,49},{5,21..., dimensions={0}, use_global_device_ids=true | all-gather | bytes 655360 | tf_op jit(solution)/shard_map/all_gather | solution.py:169
  118.6 0.7 convolution_dynamic-update-slice_fusion.3
  119.3 1.9 convolution_dynamic-update-slice_fusion.2
  121.2 1.9 convolution_dynamic-update-slice_fusion.1
  123.1 1.9 convolution_dynamic-update-slice_fusion
  125.0 1.0 reshape.120
  126.0 7.7 %all-to-all-start = ((f32[32,4,1280]{2,1,0:T(4,128)}), f32[32,4,1280]{2,1,0:T(4,128)S(1)}, u32[]{:S(2)}, u32[]{:S(2)}) async-start(f32[32,4,1280]{2,1,0:T(4,128)} %reshape.120), calls=%async_computation | async-start | bytes 1310720 | tf_op jit(solution)/shard_map/all_to_all | solution.py:24
  133.7 5.7 %collective-permute-start.10 = (f32[264,512]{1,0:T(8,128)S(1)}, f32[264,512]{1,0:T(8,128)}, u32[]{:S(2)}, u32[]{:S(2)}) collective-permute-start(f32[264,512]{1,0:T(8,128)S(1)} %get-tuple-element.27), channel_id=1, source_target_pairs={{0,60},{4,0},{8,4},{12,8},{16,12},{20,16},{24,20},{28,24},{32,28},... | collective-permute-start | bytes 1622024 | tf_op jit(solution)/shard_map/ppermute | solution.py:110
  139.5 1.9 collective-permute-start.9
  141.4 5.4 %all-to-all-done.update_ref = f32[32,4,1280]{2,1,0:T(4,128)S(1)} async-done(((f32[32,4,1280]{2,1,0:T(4,128)}), f32[32,4,1280]{2,1,0:T(4,128)S(1)}, u32[]{:S(2)}, u32[]{:S(2)}) %all-to-all-start) | async-done | bytes 655392 | tf_op jit(solution)/shard_map/all_to_all | solution.py:24
  146.8 2.4 %shard_map.86 = f32[128,256]{1,0:T(8,128)} custom-call(f32[32,4,1280]{2,1,0:T(4,128)S(1)} %all-to-all-done.update_ref), custom_call_target="tpu_custom_call" | custom-call | flops 1073741824 | bytes 786432 | tf_op jit(solution)/shard_map/pallas_call | solution.py:66
  149.3 2.2 collective-permute-done.10
  151.4 4.5 %collective-permute-start.11 = (f32[264,512]{1,0:T(8,128)}, f32[264,512]{1,0:T(8,128)S(1)}, u32[]{:S(2)}, u32[]{:S(2)}) collective-permute-start(f32[264,512]{1,0:T(8,128)} %collective-permute-done.10), channel_id=1, source_target_pairs={{0,60},{4,0},{8,4},{12,8},{16,12},{20,16},{24,20},{28,24},{32,28},... | collective-permute-start | bytes 1622024 | tf_op jit(solution)/shard_map/ppermute | solution.py:110
  155.9 6.7 %all-to-all-start.1 = ((f32[4,32,256]{2,1,0:T(8,128)}), f32[4,32,256]{2,1,0:T(8,128)S(1)}, u32[]{:S(2)}, u32[]{:S(2)}) async-start(f32[4,32,256]{2,1,0:T(8,128)} %bitcast.38), calls=%async_computation.1 | async-start | bytes 262144 | tf_op jit(solution)/shard_map/all_to_all | solution.py:196
  162.6 0.7 slice.75
  163.3 0.7 slice.62
  164.0 13.6 %all-to-all-done.1 = f32[4,32,256]{2,1,0:T(8,128)S(1)} async-done(((f32[4,32,256]{2,1,0:T(8,128)}), f32[4,32,256]{2,1,0:T(8,128)S(1)}, u32[]{:S(2)}, u32[]{:S(2)}) %all-to-all-start.1) | async-done | bytes 131104 | tf_op jit(solution)/shard_map/all_to_all | solution.py:196
  178.2 24.0 %all_to_all.20 = f32[32,4,2,4,256]{4,2,3,1,0:T(2,128)S(1)} all-to-all(f32[32,4,2,4,256]{4,2,3,1,0:T(2,128)S(1)} %broadcast_in_dim.38), channel_id=1, replica_groups=mesh['front'=8,'row'=16,'col'=4] {'front','col'}, dimensions={0} | all-to-all | bytes 2097152 | tf_op jit(solution)/shard_map/all_to_all | solution.py:24
  202.7 1.4 fusion.11
  204.7 1.4 fusion.1
  206.5 21.2 %all_to_all.21 = f32[4,32,256]{2,1,0:T(8,128)S(1)} all-to-all(f32[4,32,256]{2,1,0:T(8,128)S(1)} %bitcast.128), channel_id=1, replica_groups={{0,16,32,48},{4,20,36,52},{8,24,40,56},{12,28,44,60},{1,17,33,49},{5,21..., dimensions={0} | all-to-all | bytes 262144 | tf_op jit(solution)/shard_map/all_to_all | solution.py:216
  227.8 0.6 reduce_sum.19
  (50 shorter events, 3.0 us)
Async XLA Ops:
  0.6 24.9 %copy-start = (f32[1,1024,256]{2,1,0:T(8,128)S(1)}, f32[1,1024,256]{2,1,0:T(8,128)}, u32[]{:S(2)}) copy-start(f32[1,1024,256]{2,1,0:T(8,128)} %param.8) | copy-start | bytes 3145732
  0.6 42.7 %collective-permute-start.2 = (f32[256,1024]{1,0:T(8,128)}, f32[256,1024]{1,0:T(8,128)}, u32[]{:S(2)}, u32[]{:S(2)}) collective-permute-start(f32[256,1024]{1,0:T(8,128)} %bitcast.119), channel_id=1, source_target_pairs={{0,60},{4,0},{8,4},{12,8},{16,12},{20,16},{24,20},{28,24},{32,28},... | collective-permute-start | bytes 3145736 | tf_op jit(solution)/shard_map/ppermute | solution.py:110
  8.2 35.2 %collective-permute-start.3 = (f32[256,1024]{1,0:T(8,128)}, f32[256,1024]{1,0:T(8,128)}, u32[]{:S(2)}, u32[]{:S(2)}) collective-permute-start(f32[256,1024]{1,0:T(8,128)} %bitcast.120), channel_id=1, source_target_pairs={{0,4},{4,8},{8,12},{12,16},{16,20},{20,24},{24,28},{28,32},{32,36}... | collective-permute-start | bytes 3145736 | tf_op jit(solution)/shard_map/ppermute | solution.py:110
  26.3 17.1 %collective-permute-start.1 = (f32[128,1024]{1,0:T(8,128)S(1)}, f32[128,1024]{1,0:T(8,128)S(1)}, u32[]{:S(2)}, u32[]{:S(2)}) collective-permute-start(f32[128,1024]{1,0:T(8,128)S(1)} %fusion.2), channel_id=1, source_target_pairs={{0,60},{4,0},{8,4},{12,8},{16,12},{20,16},{24,20},{28,24},{32,28},... | collective-permute-start | bytes 1572872 | tf_op jit(solution)/shard_map/ppermute | solution.py:110
  33.9 23.5 %collective-permute-start = (f32[128,1024]{1,0:T(8,128)}, f32[128,1024]{1,0:T(8,128)}, u32[]{:S(2)}, u32[]{:S(2)}) collective-permute-start(f32[128,1024]{1,0:T(8,128)} %fusion.6), channel_id=1, source_target_pairs={{0,4},{4,8},{8,12},{12,16},{16,20},{20,24},{24,28},{28,32},{32,36}... | collective-permute-start | bytes 1572872 | tf_op jit(solution)/shard_map/ppermute | solution.py:110
  35.8 0.8 copy-start.6
  39.2 16.8 %copy-start.2 = (f32[512,512]{1,0:T(8,128)S(1)}, f32[512,512]{1,0:T(8,128)}, u32[]{:S(2)}) copy-start(f32[512,512]{1,0:T(8,128)} %param.12) | copy-start | bytes 3145732
  44.3 13.1 %collective-permute-start.4 = (f32[128,1024]{1,0:T(8,128)}, f32[128,1024]{1,0:T(8,128)}, u32[]{:S(2)}, u32[]{:S(2)}) collective-permute-start(f32[128,1024]{1,0:T(8,128)} %add.255), channel_id=1, source_target_pairs={{0,60},{4,0},{8,4},{12,8},{16,12},{20,16},{24,20},{28,24},{32,28},... | collective-permute-start | bytes 1572872 | tf_op jit(solution)/shard_map/ppermute | solution.py:110
  50.1 42.1 %collective-permute-start.8 = (f32[256,1024]{1,0:T(8,128)}, f32[256,1024]{1,0:T(8,128)}, u32[]{:S(2)}, u32[]{:S(2)}) collective-permute-start(f32[256,1024]{1,0:T(8,128)} %collective-permute-done.2), channel_id=1, source_target_pairs={{0,60},{4,0},{8,4},{12,8},{16,12},{20,16},{24,20},{28,24},{32,28},... | collective-permute-start | bytes 3145736 | tf_op jit(solution)/shard_map/ppermute | solution.py:110
  56.3 1.1 copy-start.5
  59.3 19.0 %copy-start.1 = (f32[256,512]{1,0:T(8,128)S(1)}, f32[256,512]{1,0:T(8,128)}, u32[]{:S(2)}) copy-start(f32[256,512]{1,0:T(8,128)} %param.13) | copy-start | bytes 1572868
  59.4 28.7 %collective-permute-start.5 = (f32[32,1024]{1,0:T(8,128)S(1)}, f32[32,1024]{1,0:T(8,128)S(1)}, u32[]{:S(2)}, u32[]{:S(2)}) collective-permute-start(f32[32,1024]{1,0:T(8,128)S(1)} %get-tuple-element.42), channel_id=1, source_target_pairs={{0,32},{4,36},{8,40},{12,44},{16,48},{20,52},{24,56},{28,60},{32,0... | collective-permute-start | bytes 393224 | tf_op jit(solution)/shard_map/ppermute | solution.py:110
  68.5 19.6 %collective-permute-start.6 = (f32[32,1024]{1,0:T(8,128)S(1)}, f32[32,1024]{1,0:T(8,128)S(1)}, u32[]{:S(2)}, u32[]{:S(2)}) collective-permute-start(f32[32,1024]{1,0:T(8,128)S(1)} %get-tuple-element.41), channel_id=1, source_target_pairs={{0,16},{4,20},{8,24},{12,28},{16,32},{20,36},{24,40},{28,44},{32,4... | collective-permute-start | bytes 393224 | tf_op jit(solution)/shard_map/ppermute | solution.py:110
  73.0 19.3 %collective-permute-start.7 = (f32[32,1024]{1,0:T(8,128)S(1)}, f32[32,1024]{1,0:T(8,128)S(1)}, u32[]{:S(2)}, u32[]{:S(2)}) collective-permute-start(f32[32,1024]{1,0:T(8,128)S(1)} %get-tuple-element.40), channel_id=1, source_target_pairs={{0,48},{4,52},{8,56},{12,60},{16,0},{20,4},{24,8},{28,12},{32,16},... | collective-permute-start | bytes 393224 | tf_op jit(solution)/shard_map/ppermute | solution.py:110
  78.4 40.2 %copy-start.3 = (f32[1,256,1024]{2,1,0:T(8,128)S(1)}, f32[1,256,1024]{2,1,0:T(8,128)}, u32[]{:S(2)}) copy-start(f32[1,256,1024]{2,1,0:T(8,128)} %param.9) | copy-start | bytes 3145732
  92.3 0.7 copy-start.4
  126.0 20.8 %all-to-all-start = ((f32[32,4,1280]{2,1,0:T(4,128)}), f32[32,4,1280]{2,1,0:T(4,128)S(1)}, u32[]{:S(2)}, u32[]{:S(2)}) async-start(f32[32,4,1280]{2,1,0:T(4,128)} %reshape.120), calls=%async_computation | async-start | bytes 1310720 | tf_op jit(solution)/shard_map/all_to_all | solution.py:24
  133.7 17.7 %collective-permute-start.10 = (f32[264,512]{1,0:T(8,128)S(1)}, f32[264,512]{1,0:T(8,128)}, u32[]{:S(2)}, u32[]{:S(2)}) collective-permute-start(f32[264,512]{1,0:T(8,128)S(1)} %get-tuple-element.27), channel_id=1, source_target_pairs={{0,60},{4,0},{8,4},{12,8},{16,12},{20,16},{24,20},{28,24},{32,28},... | collective-permute-start | bytes 1622024 | tf_op jit(solution)/shard_map/ppermute | solution.py:110
  139.5 23.1 %collective-permute-start.9 = (f32[264,512]{1,0:T(8,128)S(1)}, f32[264,512]{1,0:T(8,128)}, u32[]{:S(2)}, u32[]{:S(2)}) collective-permute-start(f32[264,512]{1,0:T(8,128)S(1)} %get-tuple-element.25), channel_id=1, source_target_pairs={{0,4},{4,8},{8,12},{12,16},{16,20},{20,24},{24,28},{28,32},{32,36}... | collective-permute-start | bytes 1622024 | tf_op jit(solution)/shard_map/ppermute | solution.py:110
  151.4 26.3 %collective-permute-start.11 = (f32[264,512]{1,0:T(8,128)}, f32[264,512]{1,0:T(8,128)S(1)}, u32[]{:S(2)}, u32[]{:S(2)}) collective-permute-start(f32[264,512]{1,0:T(8,128)} %collective-permute-done.10), channel_id=1, source_target_pairs={{0,60},{4,0},{8,4},{12,8},{16,12},{20,16},{24,20},{28,24},{32,28},... | collective-permute-start | bytes 1622024 | tf_op jit(solution)/shard_map/ppermute | solution.py:110
  155.9 21.7 %all-to-all-start.1 = ((f32[4,32,256]{2,1,0:T(8,128)}), f32[4,32,256]{2,1,0:T(8,128)S(1)}, u32[]{:S(2)}, u32[]{:S(2)}) async-start(f32[4,32,256]{2,1,0:T(8,128)} %bitcast.38), calls=%async_computation.1 | async-start | bytes 262144 | tf_op jit(solution)/shard_map/all_to_all | solution.py:196

commit v11 on v7

--- a/solution.py
+++ b/solution.py
@@ -208,7 +208,13 @@
     window = (downward[:share_rows], root_inverse, upward[:share_rows], twice[:share_rows])
     root = sum(contract(residual[i], value, (1,), (1,)) for i, value in enumerate(window))
     root = root.reshape(far, block, share_rows)
-    root = lax.all_to_all(root, "row", 0, 0, axis_index_groups=apart, tiled=True).sum(0)
+    parts = []
+    for offset in order:
+        value = lax.dynamic_index_in_dim(root, lax.rem(far_id + offset, far), 0, keepdims=False)
+        parts.append(shift(value, near * offset, False))
+    root = lax.dynamic_index_in_dim(root, far_id, 0, keepdims=False)
+    for value in parts:
+        root = root + value
     return own.T[None], root.T
 
 

time: 221 us -> 222 us (level)
  the two profiles are of different devices: /device:TPU:2 before, /device:TPU:96 now
where the time goes in v11:
time: 222 us; the launch traced here: 221 us
  starting transfers between devices  87 us (39%)
  blocking collectives  71.1 us (32%)
  waiting for transfers between devices  31.7 us (14%)
  matrix products  14.8 us (7%)
  local copies, waits for them, and re-layouts  7.8 us (4%)
  other arithmetic  4.68 us (2%)
  Pallas kernels  2.3 us (1%)
    ppermute x15, starting transfers between devices, shift(): return lax.ppermute(value, ('front', 'row'), pairs)  73.5 us
    all_gather x1, blocking collectives, local(): lax.all_gather(own, 'row', axis_index_groups=apart, axis=0, tiled=True)  24.2 us
    all_to_all x1, blocking collectives, exchange(): return lax.all_to_all(blocks, axes, split_axis=0, concat_axis=0, tiled=True)  20.4 us
    ppermute x15, waiting for transfers between devices, shift(): return lax.ppermute(value, ('front', 'row'), pairs)  15.8 us
    dot_general x12, matrix products, contract(): lax.dot_general(left, right, ((left_dims, right_dims), ((), ())), precisi...  14.8 us
    all_to_all x1, waiting for transfers between devices, local(): lax.all_to_all(landed, 'row', 0, 0, axis_index_groups=apart, tiled=True)  13.8 us
    all_gather x1, blocking collectives, local(): rhs = lax.all_gather(rhs, 'col', axis=1, tiled=True)  13.3 us
    all_gather x1, blocking collectives, local(): index = lax.all_gather(index, 'front', axis=0)  13.2 us
  transfers between devices with their start and end apart: 17, of which 7 were waited for; matrix products, arithmetic and copies ran while one was open for 7% of the time, Pallas kernels for 1%

profile of v11, /device:TPU:96, one launch (start us, length us, event | category | flops | bytes accessed | tf_op | source)
XLA Modules:
  0.0 220.8 jit_solution(1197741322395011640)
XLA Ops:
  0.6 2.2 collective-permute-start.2
  2.8 5.0 %collective-permute-start.3 = (f32[256,1024]{1,0:T(8,128)}, f32[256,1024]{1,0:T(8,128)}, u32[]{:S(2)}, u32[]{:S(2)}) collective-permute-start(f32[256,1024]{1,0:T(8,128)} %bitcast.137), channel_id=1, source_target_pairs={{0,4},{4,8},{8,12},{12,16},{16,20},{20,24},{24,28},{28,32},{32,36}... | collective-permute-start | bytes 3145736 | tf_op jit(solution)/shard_map/ppermute | solution.py:106
  7.9 1.0 copy.20
  9.2 13.3 %all_gather.12 = f32[4,256,128]{2,0,1:T(4,128)S(1)} all-gather(f32[4,64,128]{2,0,1:T(4,128)S(1)} %copy.22), channel_id=1, replica_groups=mesh['front'=8,'row'=16,'col'=4] {'col'}, dimensions={1}, use_global_device_ids=true | all-gather | bytes 655360 | tf_op jit(solution)/shard_map/all_gather | solution.py:129
  22.9 0.7 fusion.2
  23.6 1.9 collective-permute-start.1
  25.5 1.5 fusion.6
  27.0 5.1 %collective-permute-start = (f32[128,1024]{1,0:T(8,128)}, f32[128,1024]{1,0:T(8,128)}, u32[]{:S(2)}, u32[]{:S(2)}) collective-permute-start(f32[128,1024]{1,0:T(8,128)} %fusion.6), channel_id=1, source_target_pairs={{0,4},{4,8},{8,12},{12,16},{16,20},{20,24},{24,28},{28,32},{32,36}... | collective-permute-start | bytes 1572872 | tf_op jit(solution)/shard_map/ppermute | solution.py:106
  32.2 0.7 constant_dynamic-slice_fusion.4
  33.5 0.7 fusion.4
  34.2 3.7 %collective-permute-done.1 = f32[128,1024]{1,0:T(8,128)S(1)} collective-permute-done((f32[128,1024]{1,0:T(8,128)S(1)}, f32[128,1024]{1,0:T(8,128)S(1)}, u32[]{:S(2)}, u32[]{:S(2)}) %collective-permute-start.1) | collective-permute-done | bytes 524320 | tf_op jit(solution)/shard_map/ppermute | solution.py:106
  38.0 0.9 add.259
  38.9 3.1 %collective-permute-start.4 = (f32[128,1024]{1,0:T(8,128)}, f32[128,1024]{1,0:T(8,128)}, u32[]{:S(2)}, u32[]{:S(2)}) collective-permute-start(f32[128,1024]{1,0:T(8,128)} %add.259), channel_id=1, source_target_pairs={{0,60},{4,0},{8,4},{12,8},{16,12},{20,16},{24,20},{28,24},{32,28},... | collective-permute-start | bytes 1572872 | tf_op jit(solution)/shard_map/ppermute | solution.py:106
  43.4 5.7 %collective-permute-start.8 = (f32[256,1024]{1,0:T(8,128)}, f32[256,1024]{1,0:T(8,128)}, u32[]{:S(2)}, u32[]{:S(2)}) collective-permute-start(f32[256,1024]{1,0:T(8,128)} %collective-permute-done.2), channel_id=1, source_target_pairs={{0,60},{4,0},{8,4},{12,8},{16,12},{20,16},{24,20},{28,24},{32,28},... | collective-permute-start | bytes 3145736 | tf_op jit(solution)/shard_map/ppermute | solution.py:106
  49.1 0.7 compare_select_fusion.2
  49.8 2.1 collective-permute-done.4
  51.9 1.9 fusion
  53.8 0.8 dynamic-slice_bitcast_fusion
  54.5 16.0 %collective-permute-start.5 = (f32[32,1024]{1,0:T(8,128)}, f32[32,1024]{1,0:T(8,128)S(1)}, u32[]{:S(2)}, u32[]{:S(2)}) collective-permute-start(f32[32,1024]{1,0:T(8,128)} %get-tuple-element.22), channel_id=1, source_target_pairs={{0,32},{4,36},{8,40},{12,44},{16,48},{20,52},{24,56},{28,60},{32,0... | collective-permute-start | bytes 393224 | tf_op jit(solution)/shard_map/ppermute | solution.py:106
  70.5 3.7 %collective-permute-start.6 = (f32[32,1024]{1,0:T(8,128)}, f32[32,1024]{1,0:T(8,128)S(1)}, u32[]{:S(2)}, u32[]{:S(2)}) collective-permute-start(f32[32,1024]{1,0:T(8,128)} %get-tuple-element.23), channel_id=1, source_target_pairs={{0,16},{4,20},{8,24},{12,28},{16,32},{20,36},{24,40},{28,44},{32,4... | collective-permute-start | bytes 393224 | tf_op jit(solution)/shard_map/ppermute | solution.py:106
  74.3 6.0 %collective-permute-start.7 = (f32[32,1024]{1,0:T(8,128)}, f32[32,1024]{1,0:T(8,128)}, u32[]{:S(2)}, u32[]{:S(2)}) collective-permute-start(f32[32,1024]{1,0:T(8,128)} %get-tuple-element.24), channel_id=1, source_target_pairs={{0,48},{4,52},{8,56},{12,60},{16,0},{20,4},{24,8},{28,12},{32,16},... | collective-permute-start | bytes 393224 | tf_op jit(solution)/shard_map/ppermute | solution.py:106
  80.4 0.7 add_compare_fusion
  81.1 13.2 %all-gather = s32[8192]{0:T(1024)S(1)} all-gather(s32[1024]{0:T(1024)S(1)} %pad_add_fusion), channel_id=2, replica_groups=mesh['front'=8,'row'=16,'col'=4] {'front'}, dimensions={0}, use_global_device_ids=true | all-gather | bytes 36864 | tf_op jit(solution)/shard_map/all_gather | solution.py:154
  94.3 0.9 fusion.15
  95.3 24.2 %all_gather.15 = f32[128,1024]{1,0:T(8,128)S(1)} all-gather(f32[32,1024]{1,0:T(8,128)S(1)} %fusion.15), channel_id=1, replica_groups={{0,16,32,48},{4,20,36,52},{8,24,40,56},{12,28,44,60},{1,17,33,49},{5,21..., dimensions={0}, use_global_device_ids=true | all-gather | bytes 655360 | tf_op jit(solution)/shard_map/all_gather | solution.py:162
  119.5 1.9 fusion.33
  121.4 0.7 fusion.28
  122.0 1.9 fusion.34
  123.9 1.9 fusion.35
  125.9 1.9 collective-permute-start.10
  127.8 0.9 reshape.73
  128.7 6.9 %all-to-all-start = ((f32[32,4,1024]{2,1,0:T(4,128)}), f32[32,4,1024]{2,1,0:T(4,128)S(1)}, u32[]{:S(2)}, u32[]{:S(2)}) async-start(f32[32,4,1024]{2,1,0:T(4,128)} %reshape.73), calls=%async_computation | async-start | bytes 1048576 | tf_op jit(solution)/shard_map/all_to_all | solution.py:24
  135.6 5.4 %collective-permute-start.9 = (f32[264,512]{1,0:T(8,128)S(1)}, f32[264,512]{1,0:T(8,128)}, u32[]{:S(2)}, u32[]{:S(2)}) collective-permute-start(f32[264,512]{1,0:T(8,128)S(1)} %get-tuple-element.32), channel_id=1, source_target_pairs={{0,4},{4,8},{8,12},{12,16},{16,20},{20,24},{24,28},{28,32},{32,36}... | collective-permute-start | bytes 1622024 | tf_op jit(solution)/shard_map/ppermute | solution.py:106
  141.1 2.1 collective-permute-done.10
  143.2 1.9 collective-permute-start.11
  145.2 2.2 all-to-all-done.update_ref
  147.4 2.3 %shard_map.86 = f32[128,256]{1,0:T(8,128)} custom-call(f32[32,4,1024]{2,1,0:T(4,128)S(1)} %all-to-all-done.update_ref, s32[8,1,1024]{2,1,0:T(1,128)S(1)} %copy.25.place_ref, s32[8,1,1024]{2,1,0:T(1,128)S(1)} %broadcast_in_dim.45.high_ref), custom_call_target="tpu_custom_call" | custom-call | flops 1073741824 | bytes 655360 | tf_op jit(solution)/shard_map/pallas_call | solution.py:62
  149.7 6.6 %all-to-all-start.1 = ((f32[4,32,256]{2,1,0:T(8,128)}), f32[4,32,256]{2,1,0:T(8,128)S(1)}, u32[]{:S(2)}, u32[]{:S(2)}) async-start(f32[4,32,256]{2,1,0:T(8,128)} %bitcast.39), calls=%async_computation.1 | async-start | bytes 262144 | tf_op jit(solution)/shard_map/all_to_all | solution.py:190
  156.3 0.7 slice.76
  157.0 0.7 slice.75
  157.8 13.8 %all-to-all-done.1 = f32[4,32,256]{2,1,0:T(8,128)S(1)} async-done(((f32[4,32,256]{2,1,0:T(8,128)}), f32[4,32,256]{2,1,0:T(8,128)S(1)}, u32[]{:S(2)}, u32[]{:S(2)}) %all-to-all-start.1) | async-done | bytes 131104 | tf_op jit(solution)/shard_map/all_to_all | solution.py:190
  172.1 20.4 %all_to_all.15 = f32[32,4,2,4,256]{4,2,3,1,0:T(2,128)S(1)} all-to-all(f32[32,4,2,4,256]{4,2,3,1,0:T(2,128)S(1)} %broadcast_in_dim.46), channel_id=1, replica_groups=mesh['front'=8,'row'=16,'col'=4] {'front','col'}, dimensions={0} | all-to-all | bytes 2097152 | tf_op jit(solution)/shard_map/all_to_all | solution.py:24
  193.4 1.4 fusion.10
  194.9 1.5 fusion.1
  196.8 5.8 %collective-permute-start.12 = (f32[32,256]{1,0:T(8,128)S(1)}, f32[32,256]{1,0:T(8,128)S(1)}, u32[]{:S(2)}, u32[]{:S(2)}) collective-permute-start(f32[32,256]{1,0:T(8,128)S(1)} %get-tuple-element.57), channel_id=1, source_target_pairs={{0,32},{4,36},{8,40},{12,44},{16,48},{20,52},{24,56},{28,60},{32,0... | collective-permute-start | bytes 98312 | tf_op jit(solution)/shard_map/ppermute | solution.py:106
  202.6 7.3 %collective-permute-start.13 = (f32[32,256]{1,0:T(8,128)S(1)}, f32[32,256]{1,0:T(8,128)S(1)}, u32[]{:S(2)}, u32[]{:S(2)}) collective-permute-start(f32[32,256]{1,0:T(8,128)S(1)} %get-tuple-element.59), channel_id=1, source_target_pairs={{0,16},{4,20},{8,24},{12,28},{16,32},{20,36},{24,40},{28,44},{32,4... | collective-permute-start | bytes 98312 | tf_op jit(solution)/shard_map/ppermute | solution.py:106
  209.9 2.5 %collective-permute-start.14 = (f32[32,256]{1,0:T(8,128)S(1)}, f32[32,256]{1,0:T(8,128)S(1)}, u32[]{:S(2)}, u32[]{:S(2)}) collective-permute-start(f32[32,256]{1,0:T(8,128)S(1)} %get-tuple-element.58), channel_id=1, source_target_pairs={{0,48},{4,52},{8,56},{12,60},{16,0},{20,4},{24,8},{28,12},{32,16},... | collective-permute-start | bytes 98312 | tf_op jit(solution)/shard_map/ppermute | solution.py:106
  213.0 7.2 %collective-permute-done.14 = f32[32,256]{1,0:T(8,128)S(1)} collective-permute-done((f32[32,256]{1,0:T(8,128)S(1)}, f32[32,256]{1,0:T(8,128)S(1)}, u32[]{:S(2)}, u32[]{:S(2)}) %collective-permute-start.14) | collective-permute-done | bytes 32800 | tf_op jit(solution)/shard_map/ppermute | solution.py:106
  (55 shorter events, 5.9 us)
Async XLA Ops:
  0.6 22.2 %copy-start = (f32[1,1024,256]{2,1,0:T(8,128)S(1)}, f32[1,1024,256]{2,1,0:T(8,128)}, u32[]{:S(2)}) copy-start(f32[1,1024,256]{2,1,0:T(8,128)} %param.8) | copy-start | bytes 3145732
  0.6 37.4 %collective-permute-start.2 = (f32[256,1024]{1,0:T(8,128)}, f32[256,1024]{1,0:T(8,128)}, u32[]{:S(2)}, u32[]{:S(2)}) collective-permute-start(f32[256,1024]{1,0:T(8,128)} %bitcast.136), channel_id=1, source_target_pairs={{0,60},{4,0},{8,4},{12,8},{16,12},{20,16},{24,20},{28,24},{32,28},... | collective-permute-start | bytes 3145736 | tf_op jit(solution)/shard_map/ppermute | solution.py:106
  2.8 35.2 %collective-permute-start.3 = (f32[256,1024]{1,0:T(8,128)}, f32[256,1024]{1,0:T(8,128)}, u32[]{:S(2)}, u32[]{:S(2)}) collective-permute-start(f32[256,1024]{1,0:T(8,128)} %bitcast.137), channel_id=1, source_target_pairs={{0,4},{4,8},{8,12},{12,16},{16,20},{20,24},{24,28},{28,32},{32,36}... | collective-permute-start | bytes 3145736 | tf_op jit(solution)/shard_map/ppermute | solution.py:106
  23.6 14.4 %collective-permute-start.1 = (f32[128,1024]{1,0:T(8,128)S(1)}, f32[128,1024]{1,0:T(8,128)S(1)}, u32[]{:S(2)}, u32[]{:S(2)}) collective-permute-start(f32[128,1024]{1,0:T(8,128)S(1)} %fusion.2), channel_id=1, source_target_pairs={{0,60},{4,0},{8,4},{12,8},{16,12},{20,16},{24,20},{28,24},{32,28},... | collective-permute-start | bytes 1572872 | tf_op jit(solution)/shard_map/ppermute | solution.py:106
  27.0 22.8 %collective-permute-start = (f32[128,1024]{1,0:T(8,128)}, f32[128,1024]{1,0:T(8,128)}, u32[]{:S(2)}, u32[]{:S(2)}) collective-permute-start(f32[128,1024]{1,0:T(8,128)} %fusion.6), channel_id=1, source_target_pairs={{0,4},{4,8},{8,12},{12,16},{16,20},{20,24},{24,28},{28,32},{32,36}... | collective-permute-start | bytes 1572872 | tf_op jit(solution)/shard_map/ppermute | solution.py:106
  32.2 0.8 copy-start.5
  34.2 8.5 %copy-start.2 = (f32[512,512]{1,0:T(8,128)S(1)}, f32[512,512]{1,0:T(8,128)}, u32[]{:S(2)}) copy-start(f32[512,512]{1,0:T(8,128)} %param.12) | copy-start | bytes 3145732
  38.9 13.0 %collective-permute-start.4 = (f32[128,1024]{1,0:T(8,128)}, f32[128,1024]{1,0:T(8,128)}, u32[]{:S(2)}, u32[]{:S(2)}) collective-permute-start(f32[128,1024]{1,0:T(8,128)} %add.259), channel_id=1, source_target_pairs={{0,60},{4,0},{8,4},{12,8},{16,12},{20,16},{24,20},{28,24},{32,28},... | collective-permute-start | bytes 1572872 | tf_op jit(solution)/shard_map/ppermute | solution.py:106
  43.4 50.9 %collective-permute-start.8 = (f32[256,1024]{1,0:T(8,128)}, f32[256,1024]{1,0:T(8,128)}, u32[]{:S(2)}, u32[]{:S(2)}) collective-permute-start(f32[256,1024]{1,0:T(8,128)} %collective-permute-done.2), channel_id=1, source_target_pairs={{0,60},{4,0},{8,4},{12,8},{16,12},{20,16},{24,20},{28,24},{32,28},... | collective-permute-start | bytes 3145736 | tf_op jit(solution)/shard_map/ppermute | solution.py:106
  53.8 26.5 %copy-start.1 = (f32[256,512]{1,0:T(8,128)S(1)}, f32[256,512]{1,0:T(8,128)}, u32[]{:S(2)}) copy-start(f32[256,512]{1,0:T(8,128)} %param.13) | copy-start | bytes 1572868
  54.5 39.7 %collective-permute-start.5 = (f32[32,1024]{1,0:T(8,128)}, f32[32,1024]{1,0:T(8,128)S(1)}, u32[]{:S(2)}, u32[]{:S(2)}) collective-permute-start(f32[32,1024]{1,0:T(8,128)} %get-tuple-element.22), channel_id=1, source_target_pairs={{0,32},{4,36},{8,40},{12,44},{16,48},{20,52},{24,56},{28,60},{32,0... | collective-permute-start | bytes 393224 | tf_op jit(solution)/shard_map/ppermute | solution.py:106
  70.5 23.8 %collective-permute-start.6 = (f32[32,1024]{1,0:T(8,128)}, f32[32,1024]{1,0:T(8,128)S(1)}, u32[]{:S(2)}, u32[]{:S(2)}) collective-permute-start(f32[32,1024]{1,0:T(8,128)} %get-tuple-element.23), channel_id=1, source_target_pairs={{0,16},{4,20},{8,24},{12,28},{16,32},{20,36},{24,40},{28,44},{32,4... | collective-permute-start | bytes 393224 | tf_op jit(solution)/shard_map/ppermute | solution.py:106
  74.3 20.0 %collective-permute-start.7 = (f32[32,1024]{1,0:T(8,128)}, f32[32,1024]{1,0:T(8,128)}, u32[]{:S(2)}, u32[]{:S(2)}) collective-permute-start(f32[32,1024]{1,0:T(8,128)} %get-tuple-element.24), channel_id=1, source_target_pairs={{0,48},{4,52},{8,56},{12,60},{16,0},{20,4},{24,8},{28,12},{32,16},... | collective-permute-start | bytes 393224 | tf_op jit(solution)/shard_map/ppermute | solution.py:106
  95.3 24.2 %copy-start.4 = (f32[32,1024]{1,0:T(8,128)}, f32[32,1024]{1,0:T(8,128)S(1)}, u32[]{:S(2)}) copy-start(f32[32,1024]{1,0:T(8,128)S(1)} %fusion.15) | copy-start | bytes 393220
  95.3 26.1 %copy-start.3 = (f32[1,256,1024]{2,1,0:T(8,128)S(1)}, f32[1,256,1024]{2,1,0:T(8,128)}, u32[]{:S(2)}) copy-start(f32[1,256,1024]{2,1,0:T(8,128)} %param.9) | copy-start | bytes 3145732
  125.9 17.3 %collective-permute-start.10 = (f32[264,512]{1,0:T(8,128)S(1)}, f32[264,512]{1,0:T(8,128)}, u32[]{:S(2)}, u32[]{:S(2)}) collective-permute-start(f32[264,512]{1,0:T(8,128)S(1)} %get-tuple-element.33), channel_id=1, source_target_pairs={{0,60},{4,0},{8,4},{12,8},{16,12},{20,16},{24,20},{28,24},{32,28},... | collective-permute-start | bytes 1622024 | tf_op jit(solution)/shard_map/ppermute | solution.py:106
  128.7 18.7 %all-to-all-start = ((f32[32,4,1024]{2,1,0:T(4,128)}), f32[32,4,1024]{2,1,0:T(4,128)S(1)}, u32[]{:S(2)}, u32[]{:S(2)}) async-start(f32[32,4,1024]{2,1,0:T(4,128)} %reshape.73), calls=%async_computation | async-start | bytes 1048576 | tf_op jit(solution)/shard_map/all_to_all | solution.py:24
  135.6 21.4 %collective-permute-start.9 = (f32[264,512]{1,0:T(8,128)S(1)}, f32[264,512]{1,0:T(8,128)}, u32[]{:S(2)}, u32[]{:S(2)}) collective-permute-start(f32[264,512]{1,0:T(8,128)S(1)} %get-tuple-element.32), channel_id=1, source_target_pairs={{0,4},{4,8},{8,12},{12,16},{16,20},{20,24},{24,28},{28,32},{32,36}... | collective-permute-start | bytes 1622024 | tf_op jit(solution)/shard_map/ppermute | solution.py:106
  143.2 28.4 %collective-permute-start.11 = (f32[264,512]{1,0:T(8,128)}, f32[264,512]{1,0:T(8,128)S(1)}, u32[]{:S(2)}, u32[]{:S(2)}) collective-permute-start(f32[264,512]{1,0:T(8,128)} %collective-permute-done.10), channel_id=1, source_target_pairs={{0,60},{4,0},{8,4},{12,8},{16,12},{20,16},{24,20},{28,24},{32,28},... | collective-permute-start | bytes 1622024 | tf_op jit(solution)/shard_map/ppermute | solution.py:106
  149.7 21.8 %all-to-all-start.1 = ((f32[4,32,256]{2,1,0:T(8,128)}), f32[4,32,256]{2,1,0:T(8,128)S(1)}, u32[]{:S(2)}, u32[]{:S(2)}) async-start(f32[4,32,256]{2,1,0:T(8,128)} %bitcast.39), calls=%async_computation.1 | async-start | bytes 262144 | tf_op jit(solution)/shard_map/all_to_all | solution.py:190
  196.8 15.6 %collective-permute-start.12 = (f32[32,256]{1,0:T(8,128)S(1)}, f32[32,256]{1,0:T(8,128)S(1)}, u32[]{:S(2)}, u32[]{:S(2)}) collective-permute-start(f32[32,256]{1,0:T(8,128)S(1)} %get-tuple-element.57), channel_id=1, source_target_pairs={{0,32},{4,36},{8,40},{12,44},{16,48},{20,52},{24,56},{28,60},{32,0... | collective-permute-start | bytes 98312 | tf_op jit(solution)/shard_map/ppermute | solution.py:106
  202.6 10.4 %collective-permute-start.13 = (f32[32,256]{1,0:T(8,128)S(1)}, f32[32,256]{1,0:T(8,128)S(1)}, u32[]{:S(2)}, u32[]{:S(2)}) collective-permute-start(f32[32,256]{1,0:T(8,128)S(1)} %get-tuple-element.59), channel_id=1, source_target_pairs={{0,16},{4,20},{8,24},{12,28},{16,32},{20,36},{24,40},{28,44},{32,4... | collective-permute-start | bytes 98312 | tf_op jit(solution)/shard_map/ppermute | solution.py:106
  209.9 10.3 %collective-permute-start.14 = (f32[32,256]{1,0:T(8,128)S(1)}, f32[32,256]{1,0:T(8,128)S(1)}, u32[]{:S(2)}, u32[]{:S(2)}) collective-permute-start(f32[32,256]{1,0:T(8,128)S(1)} %get-tuple-element.58), channel_id=1, source_target_pairs={{0,48},{4,52},{8,56},{12,60},{16,0},{20,4},{24,8},{28,12},{32,16},... | collective-permute-start | bytes 98312 | tf_op jit(solution)/shard_map/ppermute | solution.py:106

commit v12 on v8

--- a/solution.py
+++ b/solution.py
@@ -184,9 +184,10 @@
     share_rows = root_inverse.shape[0]
     upward = jnp.concatenate([root_inverse, share_of(-1), share_of(-2)])
     downward = jnp.concatenate([root_inverse, share_of(1), share_of(1)])
-    update, upward, downward = lax.optimization_barrier((update, upward, downward))
+    update, upward, downward = lax.optimization_barrier(
+        (update, shift(upward, -1, False), downward)
+    )
     update = exchange(update.reshape(layer, part, -1), ("front", "col"))
-    upward = shift(upward, -1, False)
     downward = shift(downward, 1, False)
 
     landed = land(update, near * border_rows, fronts, cols, low_count, high_count)

time: 229 us -> 227 us (level)
  the two profiles are of different devices: /device:TPU:32 before, /device:TPU:2 now
where the time goes in v12:
time: 227 us; the launch traced here: 226 us
  blocking collectives  74 us (33%)
  starting transfers between devices  65.3 us (29%)
  waiting for transfers between devices  47.2 us (21%)
  matrix products  18.1 us (8%)
  local copies, waits for them, and re-layouts  12.6 us (6%)
  other arithmetic  4.89 us (2%)
  Pallas kernels  2.44 us (1%)
    ppermute x12, starting transfers between devices, shift(): return lax.ppermute(value, ('front', 'row'), pairs)  53 us
    ppermute x12, waiting for transfers between devices, shift(): return lax.ppermute(value, ('front', 'row'), pairs)  29.5 us
    all_gather x1, blocking collectives, local(): lax.all_gather(own, 'row', axis_index_groups=apart, axis=0, tiled=True)  23.8 us
    all_to_all x1, blocking collectives, exchange(): return lax.all_to_all(blocks, axes, split_axis=0, concat_axis=0, tiled=True)  20.9 us
    dot_general x12, matrix products, contract(): lax.dot_general(left, right, ((left_dims, right_dims), ((), ())), precisi...  18.1 us
    all_to_all x1, blocking collectives, local(): lax.all_to_all(root, 'row', 0, 0, axis_index_groups=apart, tiled=True)  16 us
    all_gather x1, blocking collectives, local(): rhs = lax.all_gather(rhs, 'col', axis=1, tiled=True)  13.3 us
    all_to_all x1, waiting for transfers between devices, local(): lax.all_to_all(landed, 'row', 0, 0, axis_index_groups=apart, tiled=True)  12.1 us
  transfers between devices with their start and end apart: 14, of which 5 were waited for; matrix products, arithmetic and copies ran while one was open for 12% of the time, Pallas kernels for 1%

profile of v12, /device:TPU:2, one launch (start us, length us, event | category | flops | bytes accessed | tf_op | source)
XLA Modules:
  0.0 225.9 jit_solution(11690993954280994553)
XLA Ops:
  0.6 11.4 %collective-permute-start.2 = (f32[256,1024]{1,0:T(8,128)}, f32[256,1024]{1,0:T(8,128)}, u32[]{:S(2)}, u32[]{:S(2)}) collective-permute-start(f32[256,1024]{1,0:T(8,128)} %bitcast.119), channel_id=1, source_target_pairs={{0,60},{4,0},{8,4},{12,8},{16,12},{20,16},{24,20},{28,24},{32,28},... | collective-permute-start | bytes 3145736 | tf_op jit(solution)/shard_map/ppermute | solution.py:110
  12.1 1.9 collective-permute-start.3
  14.0 1.0 copy.18
  15.3 13.3 %all_gather.6 = f32[4,256,128]{2,0,1:T(4,128)S(1)} all-gather(f32[4,64,128]{2,0,1:T(4,128)S(1)} %copy.20), channel_id=1, replica_groups=mesh['front'=8,'row'=16,'col'=4] {'col'}, dimensions={1}, use_global_device_ids=true | all-gather | bytes 655360 | tf_op jit(solution)/shard_map/all_gather | solution.py:138
  29.0 1.5 fusion.2
  30.5 5.3 %collective-permute-start.1 = (f32[128,1024]{1,0:T(8,128)}, f32[128,1024]{1,0:T(8,128)S(1)}, u32[]{:S(2)}, u32[]{:S(2)}) collective-permute-start(f32[128,1024]{1,0:T(8,128)} %fusion.2), channel_id=1, source_target_pairs={{0,60},{4,0},{8,4},{12,8},{16,12},{20,16},{24,20},{28,24},{32,28},... | collective-permute-start | bytes 1572872 | tf_op jit(solution)/shard_map/ppermute | solution.py:110
  35.8 1.5 fusion.6
  37.3 1.9 collective-permute-start
  39.3 1.6 copy.21
  40.9 1.3 reshape.115
  42.2 0.7 constant_dynamic-slice_fusion
  42.9 1.2 pad_maximum_fusion.1
  44.1 5.1 %collective-permute-start.9 = (f32[264,512]{1,0:T(8,128)}, f32[264,512]{1,0:T(8,128)}, u32[]{:S(2)}, u32[]{:S(2)}) collective-permute-start(f32[264,512]{1,0:T(8,128)} %get-tuple-element.35), channel_id=1, source_target_pairs={{0,60},{4,0},{8,4},{12,8},{16,12},{20,16},{24,20},{28,24},{32,28},... | collective-permute-start | bytes 1622024 | tf_op jit(solution)/shard_map/ppermute | solution.py:110
  49.3 0.7 constant_dynamic-slice_fusion.4
  50.7 0.7 fusion.4
  51.5 2.0 collective-permute-start.4
  53.5 0.7 compare_select_fusion
  54.2 1.9 collective-permute-start.8
  56.1 0.7 compare_select_fusion.2
  56.8 8.7 %collective-permute-done.4 = f32[128,1024]{1,0:T(8,128)S(1)} collective-permute-done((f32[128,1024]{1,0:T(8,128)S(1)}, f32[128,1024]{1,0:T(8,128)S(1)}, u32[]{:S(2)}, u32[]{:S(2)}) %collective-permute-start.4) | collective-permute-done | bytes 524320 | tf_op jit(solution)/shard_map/ppermute | solution.py:110
  65.5 1.7 fusion
  67.3 0.8 dynamic-slice_bitcast_fusion
  68.0 7.8 %collective-permute-start.5 = (f32[32,1024]{1,0:T(8,128)}, f32[32,1024]{1,0:T(8,128)S(1)}, u32[]{:S(2)}, u32[]{:S(2)}) collective-permute-start(f32[32,1024]{1,0:T(8,128)} %get-tuple-element.38), channel_id=1, source_target_pairs={{0,32},{4,36},{8,40},{12,44},{16,48},{20,52},{24,56},{28,60},{32,0... | collective-permute-start | bytes 393224 | tf_op jit(solution)/shard_map/ppermute | solution.py:110
  75.8 6.4 %collective-permute-start.6 = (f32[32,1024]{1,0:T(8,128)}, f32[32,1024]{1,0:T(8,128)}, u32[]{:S(2)}, u32[]{:S(2)}) collective-permute-start(f32[32,1024]{1,0:T(8,128)} %get-tuple-element.37), channel_id=1, source_target_pairs={{0,16},{4,20},{8,24},{12,28},{16,32},{20,36},{24,40},{28,44},{32,4... | collective-permute-start | bytes 393224 | tf_op jit(solution)/shard_map/ppermute | solution.py:110
  82.2 3.4 %collective-permute-start.7 = (f32[32,1024]{1,0:T(8,128)}, f32[32,1024]{1,0:T(8,128)}, u32[]{:S(2)}, u32[]{:S(2)}) collective-permute-start(f32[32,1024]{1,0:T(8,128)} %get-tuple-element.36), channel_id=1, source_target_pairs={{0,48},{4,52},{8,56},{12,60},{16,0},{20,4},{24,8},{28,12},{32,16},... | collective-permute-start | bytes 393224 | tf_op jit(solution)/shard_map/ppermute | solution.py:110
  86.4 2.2 collective-permute-done.6
  88.6 18.5 %collective-permute-done.7 = f32[32,1024]{1,0:T(8,128)} collective-permute-done((f32[32,1024]{1,0:T(8,128)}, f32[32,1024]{1,0:T(8,128)}, u32[]{:S(2)}, u32[]{:S(2)}) %collective-permute-start.7) | collective-permute-done | bytes 131104 | tf_op jit(solution)/shard_map/ppermute | solution.py:110
  107.1 1.0 fusion.15
  108.1 23.8 %all_gather.7 = f32[128,1024]{1,0:T(8,128)S(1)} all-gather(f32[32,1024]{1,0:T(8,128)S(1)} %fusion.15), channel_id=1, replica_groups={{0,16,32,48},{4,20,36,52},{8,24,40,56},{12,28,44,60},{1,17,33,49},{5,21..., dimensions={0}, use_global_device_ids=true | all-gather | bytes 655360 | tf_op jit(solution)/shard_map/all_gather | solution.py:169
  131.9 1.4 convolution_dynamic-update-slice_fusion.3
  133.2 2.5 %convolution_dynamic-update-slice_fusion.2 = f32[128,1280]{1,0:T(8,128)} fusion(f32[128,1280]{1,0:T(8,128)} %convolution_dynamic-update-slice_fusion.3, f32[128,1024]{1,0:T(8,128)S(1)} %all_gather.7, f32[256,1024]{1,0:T(8,128)} %collective-permute-done.2), kind=kOutput, calls=%fused_computation.4 | convolution fusion | flops 201326592 | bytes 1703936 | tf_op jit(solution)/shard_map/dot_general | solution.py:14
  135.8 2.5 %convolution_dynamic-update-slice_fusion.1 = f32[128,1280]{1,0:T(8,128)} fusion(f32[128,1280]{1,0:T(8,128)} %convolution_dynamic-update-slice_fusion.2, f32[128,1024]{1,0:T(8,128)S(1)} %all_gather.7, f32[256,1024]{1,0:T(8,128)} %collective-permute-done.3), kind=kOutput, calls=%fused_computation.3 | convolution fusion | flops 201326592 | bytes 1703936 | tf_op jit(solution)/shard_map/dot_general | solution.py:14
  138.3 2.5 %convolution_dynamic-update-slice_fusion = f32[128,1280]{1,0:T(8,128)} fusion(f32[128,1280]{1,0:T(8,128)} %convolution_dynamic-update-slice_fusion.1, f32[128,1024]{1,0:T(8,128)S(1)} %all_gather.7, f32[256,1024]{1,0:T(8,128)} %collective-permute-done.8), kind=kOutput, calls=%fused_computation.2 | convolution fusion | flops 201326592 | bytes 1703936 | tf_op jit(solution)/shard_map/dot_general | solution.py:14
  140.9 0.7 constant_dynamic-update-slice_fusion
  141.6 2.1 reshape.120
  143.7 5.7 %all-to-all-start = ((f32[32,4,1280]{2,1,0:T(4,128)}), f32[32,4,1280]{2,1,0:T(4,128)S(1)}, u32[]{:S(2)}, u32[]{:S(2)}) async-start(f32[32,4,1280]{2,1,0:T(4,128)} %reshape.120), calls=%async_computation | async-start | bytes 1310720 | tf_op jit(solution)/shard_map/all_to_all | solution.py:24
  149.4 1.9 collective-permute-start.11
  151.3 3.9 %collective-permute-start.10 = (f32[264,512]{1,0:T(8,128)S(1)}, f32[264,512]{1,0:T(8,128)}, u32[]{:S(2)}, u32[]{:S(2)}) collective-permute-start(f32[264,512]{1,0:T(8,128)S(1)} %copy-done.3), channel_id=1, source_target_pairs={{0,4},{4,8},{8,12},{12,16},{16,20},{20,24},{24,28},{28,32},{32,36}... | collective-permute-start | bytes 1622024 | tf_op jit(solution)/shard_map/ppermute | solution.py:110
  155.3 5.6 %all-to-all-done.update_ref = f32[32,4,1280]{2,1,0:T(4,128)S(1)} async-done(((f32[32,4,1280]{2,1,0:T(4,128)}), f32[32,4,1280]{2,1,0:T(4,128)S(1)}, u32[]{:S(2)}, u32[]{:S(2)}) %all-to-all-start) | async-done | bytes 655392 | tf_op jit(solution)/shard_map/all_to_all | solution.py:24
  160.9 2.4 %shard_map.86 = f32[128,256]{1,0:T(8,128)} custom-call(f32[32,4,1280]{2,1,0:T(4,128)S(1)} %all-to-all-done.update_ref), custom_call_target="tpu_custom_call" | custom-call | flops 1073741824 | bytes 786432 | tf_op jit(solution)/shard_map/pallas_call | solution.py:66
  163.3 6.6 %all-to-all-start.1 = ((f32[4,32,256]{2,1,0:T(8,128)}), f32[4,32,256]{2,1,0:T(8,128)S(1)}, u32[]{:S(2)}, u32[]{:S(2)}) async-start(f32[4,32,256]{2,1,0:T(8,128)} %bitcast.38), calls=%async_computation.1 | async-start | bytes 262144 | tf_op jit(solution)/shard_map/all_to_all | solution.py:195
  170.0 0.7 slice.62
  170.7 0.7 slice.75
  171.4 12.1 %all-to-all-done.1 = f32[4,32,256]{2,1,0:T(8,128)S(1)} async-done(((f32[4,32,256]{2,1,0:T(8,128)}), f32[4,32,256]{2,1,0:T(8,128)S(1)}, u32[]{:S(2)}, u32[]{:S(2)}) %all-to-all-start.1) | async-done | bytes 131104 | tf_op jit(solution)/shard_map/all_to_all | solution.py:195
  184.1 20.9 %all_to_all.20 = f32[32,4,2,4,256]{4,2,3,1,0:T(2,128)S(1)} all-to-all(f32[32,4,2,4,256]{4,2,3,1,0:T(2,128)S(1)} %broadcast_in_dim.38), channel_id=1, replica_groups=mesh['front'=8,'row'=16,'col'=4] {'front','col'}, dimensions={0} | all-to-all | bytes 2097152 | tf_op jit(solution)/shard_map/all_to_all | solution.py:24
  205.4 1.4 fusion.11
  207.4 1.4 fusion.1
  209.3 16.0 %all_to_all.21 = f32[4,32,256]{2,1,0:T(8,128)S(1)} all-to-all(f32[4,32,256]{2,1,0:T(8,128)S(1)} %bitcast.128), channel_id=1, replica_groups={{0,16,32,48},{4,20,36,52},{8,24,40,56},{12,28,44,60},{1,17,33,49},{5,21..., dimensions={0} | all-to-all | bytes 262144 | tf_op jit(solution)/shard_map/all_to_all | solution.py:216
  (48 shorter events, 4.5 us)
Async XLA Ops:
  0.6 28.4 %copy-start = (f32[1,1024,256]{2,1,0:T(8,128)S(1)}, f32[1,1024,256]{2,1,0:T(8,128)}, u32[]{:S(2)}) copy-start(f32[1,1024,256]{2,1,0:T(8,128)} %param.8) | copy-start | bytes 3145732
  0.6 50.7 %collective-permute-start.2 = (f32[256,1024]{1,0:T(8,128)}, f32[256,1024]{1,0:T(8,128)}, u32[]{:S(2)}, u32[]{:S(2)}) collective-permute-start(f32[256,1024]{1,0:T(8,128)} %bitcast.119), channel_id=1, source_target_pairs={{0,60},{4,0},{8,4},{12,8},{16,12},{20,16},{24,20},{28,24},{32,28},... | collective-permute-start | bytes 3145736 | tf_op jit(solution)/shard_map/ppermute | solution.py:110
  12.1 39.3 %collective-permute-start.3 = (f32[256,1024]{1,0:T(8,128)}, f32[256,1024]{1,0:T(8,128)}, u32[]{:S(2)}, u32[]{:S(2)}) collective-permute-start(f32[256,1024]{1,0:T(8,128)} %bitcast.120), channel_id=1, source_target_pairs={{0,4},{4,8},{8,12},{12,16},{16,20},{20,24},{24,28},{28,32},{32,36}... | collective-permute-start | bytes 3145736 | tf_op jit(solution)/shard_map/ppermute | solution.py:110
  30.5 20.9 %collective-permute-start.1 = (f32[128,1024]{1,0:T(8,128)}, f32[128,1024]{1,0:T(8,128)S(1)}, u32[]{:S(2)}, u32[]{:S(2)}) collective-permute-start(f32[128,1024]{1,0:T(8,128)} %fusion.2), channel_id=1, source_target_pairs={{0,60},{4,0},{8,4},{12,8},{16,12},{20,16},{24,20},{28,24},{32,28},... | collective-permute-start | bytes 1572872 | tf_op jit(solution)/shard_map/ppermute | solution.py:110
  37.3 19.5 %collective-permute-start = (f32[128,1024]{1,0:T(8,128)}, f32[128,1024]{1,0:T(8,128)}, u32[]{:S(2)}, u32[]{:S(2)}) collective-permute-start(f32[128,1024]{1,0:T(8,128)} %fusion.6), channel_id=1, source_target_pairs={{0,4},{4,8},{8,12},{12,16},{16,20},{20,24},{24,28},{28,32},{32,36}... | collective-permute-start | bytes 1572872 | tf_op jit(solution)/shard_map/ppermute | solution.py:110
  40.8 2.1 copy-start.1
  44.1 97.4 %collective-permute-start.9 = (f32[264,512]{1,0:T(8,128)}, f32[264,512]{1,0:T(8,128)}, u32[]{:S(2)}, u32[]{:S(2)}) collective-permute-start(f32[264,512]{1,0:T(8,128)} %get-tuple-element.35), channel_id=1, source_target_pairs={{0,60},{4,0},{8,4},{12,8},{16,12},{20,16},{24,20},{28,24},{32,28},... | collective-permute-start | bytes 1622024 | tf_op jit(solution)/shard_map/ppermute | solution.py:110
  49.3 0.8 copy-start.5
  51.5 14.1 %collective-permute-start.4 = (f32[128,1024]{1,0:T(8,128)S(1)}, f32[128,1024]{1,0:T(8,128)S(1)}, u32[]{:S(2)}, u32[]{:S(2)}) collective-permute-start(f32[128,1024]{1,0:T(8,128)S(1)} %add.255), channel_id=1, source_target_pairs={{0,60},{4,0},{8,4},{12,8},{16,12},{20,16},{24,20},{28,24},{32,28},... | collective-permute-start | bytes 1572872 | tf_op jit(solution)/shard_map/ppermute | solution.py:110
  54.2 52.9 %collective-permute-start.8 = (f32[256,1024]{1,0:T(8,128)}, f32[256,1024]{1,0:T(8,128)}, u32[]{:S(2)}, u32[]{:S(2)}) collective-permute-start(f32[256,1024]{1,0:T(8,128)} %collective-permute-done.2), channel_id=1, source_target_pairs={{0,60},{4,0},{8,4},{12,8},{16,12},{20,16},{24,20},{28,24},{32,28},... | collective-permute-start | bytes 3145736 | tf_op jit(solution)/shard_map/ppermute | solution.py:110
  68.0 63.8 %copy-start.2 = (f32[1,256,1024]{2,1,0:T(8,128)S(1)}, f32[1,256,1024]{2,1,0:T(8,128)}, u32[]{:S(2)}) copy-start(f32[1,256,1024]{2,1,0:T(8,128)} %param.9) | copy-start | bytes 3145732
  68.0 18.4 %collective-permute-start.5 = (f32[32,1024]{1,0:T(8,128)}, f32[32,1024]{1,0:T(8,128)S(1)}, u32[]{:S(2)}, u32[]{:S(2)}) collective-permute-start(f32[32,1024]{1,0:T(8,128)} %get-tuple-element.38), channel_id=1, source_target_pairs={{0,32},{4,36},{8,40},{12,44},{16,48},{20,52},{24,56},{28,60},{32,0... | collective-permute-start | bytes 393224 | tf_op jit(solution)/shard_map/ppermute | solution.py:110
  75.8 12.8 %collective-permute-start.6 = (f32[32,1024]{1,0:T(8,128)}, f32[32,1024]{1,0:T(8,128)}, u32[]{:S(2)}, u32[]{:S(2)}) collective-permute-start(f32[32,1024]{1,0:T(8,128)} %get-tuple-element.37), channel_id=1, source_target_pairs={{0,16},{4,20},{8,24},{12,28},{16,32},{20,36},{24,40},{28,44},{32,4... | collective-permute-start | bytes 393224 | tf_op jit(solution)/shard_map/ppermute | solution.py:110
  82.2 24.9 %collective-permute-start.7 = (f32[32,1024]{1,0:T(8,128)}, f32[32,1024]{1,0:T(8,128)}, u32[]{:S(2)}, u32[]{:S(2)}) collective-permute-start(f32[32,1024]{1,0:T(8,128)} %get-tuple-element.36), channel_id=1, source_target_pairs={{0,48},{4,52},{8,56},{12,60},{16,0},{20,4},{24,8},{28,12},{32,16},... | collective-permute-start | bytes 393224 | tf_op jit(solution)/shard_map/ppermute | solution.py:110
  108.1 23.8 %copy-start.4 = (f32[32,1024]{1,0:T(8,128)}, f32[32,1024]{1,0:T(8,128)S(1)}, u32[]{:S(2)}) copy-start(f32[32,1024]{1,0:T(8,128)S(1)} %fusion.15) | copy-start | bytes 393220
  143.7 7.7 %copy-start.3 = (f32[264,512]{1,0:T(8,128)S(1)}, f32[264,512]{1,0:T(8,128)}, u32[]{:S(2)}) copy-start(f32[264,512]{1,0:T(8,128)} %get-tuple-element.23) | copy-start | bytes 1622020
  143.7 17.2 %all-to-all-start = ((f32[32,4,1280]{2,1,0:T(4,128)}), f32[32,4,1280]{2,1,0:T(4,128)S(1)}, u32[]{:S(2)}, u32[]{:S(2)}) async-start(f32[32,4,1280]{2,1,0:T(4,128)} %reshape.120), calls=%async_computation | async-start | bytes 1310720 | tf_op jit(solution)/shard_map/all_to_all | solution.py:24
  149.4 21.3 %collective-permute-start.11 = (f32[264,512]{1,0:T(8,128)}, f32[264,512]{1,0:T(8,128)S(1)}, u32[]{:S(2)}, u32[]{:S(2)}) collective-permute-start(f32[264,512]{1,0:T(8,128)} %collective-permute-done.9), channel_id=1, source_target_pairs={{0,60},{4,0},{8,4},{12,8},{16,12},{20,16},{24,20},{28,24},{32,28},... | collective-permute-start | bytes 1622024 | tf_op jit(solution)/shard_map/ppermute | solution.py:110
  151.3 19.4 %collective-permute-start.10 = (f32[264,512]{1,0:T(8,128)S(1)}, f32[264,512]{1,0:T(8,128)}, u32[]{:S(2)}, u32[]{:S(2)}) collective-permute-start(f32[264,512]{1,0:T(8,128)S(1)} %copy-done.3), channel_id=1, source_target_pairs={{0,4},{4,8},{8,12},{12,16},{16,20},{20,24},{24,28},{28,32},{32,36}... | collective-permute-start | bytes 1622024 | tf_op jit(solution)/shard_map/ppermute | solution.py:110
  163.3 20.2 %all-to-all-start.1 = ((f32[4,32,256]{2,1,0:T(8,128)}), f32[4,32,256]{2,1,0:T(8,128)S(1)}, u32[]{:S(2)}, u32[]{:S(2)}) async-start(f32[4,32,256]{2,1,0:T(8,128)} %bitcast.38), calls=%async_computation.1 | async-start | bytes 262144 | tf_op jit(solution)/shard_map/all_to_all | solution.py:195
